TPU v7x, 32 devices: a whole 2x2x4 slice. The times are simulated.
32 devices in a mesh: dp: 4 (over z), ctx: 8 (over y, x, core).
Axes of the slice: x: 2, y: 2, z: 4, core: 2. Of those that a mesh axis runs over, the one named last changes fastest.
Arguments:
- query_in: bfloat16 [4, 2048, 1280], P('dp', 'ctx'), may hold values from -150 to 150
- key_in: bfloat16 [4, 2048, 1280], P('dp', 'ctx'), may hold values from -16 to 16
- value_in: bfloat16 [4, 2048, 1280], P('dp', 'ctx'), may hold values from -6 to 6
- grad_out: bfloat16 [4, 2048, 1280], P('dp', 'ctx'), may hold values from -6 to 6
- key_blocks: int32 [10, 8, 6], P(None, 'ctx'), may hold values from 0 to 15, as said below
- sink_logits: float32 [10], replicated, may hold values from 3 to 8
Outputs:
- grad_query: bfloat16 [4, 2048, 1280], P('dp', 'ctx')
- grad_key: bfloat16 [4, 2048, 1280], P('dp', 'ctx')
- grad_value: bfloat16 [4, 2048, 1280], P('dp', 'ctx')
- grad_sink: float32 [10], replicated
Inputs may be any that keep to these rules, and one draw needn't show every extreme that they name: `key_blocks`: block b holds tokens 128 b to 128 b + 127. The 6 entries of one head and segment are distinct, and none falls in the aligned group of 256 tokens that holds the segment. Counting all heads, entries and segments of one aligned group of 256 tokens, at most 9 entries fall in any one other aligned group of 256 tokens, and every group reaches 9 with some other group in every draw.
All inputs are finite; a program needn't handle non-finite values.
Results may differ from a plain program's by a relative error of at most 0.012.
Values may be sent and summed in bfloat16 or wider, within the bound.
No kernel may reach another device: no remote copies, remote signals or barrier semaphores. Data moves between devices by JAX's collectives and lax.ppermute only.
A program may use at most 64 MiB of HBM per device.

v0:
```python
from functools import partial
import math

import jax
import jax.numpy as jnp
from jax import lax
from jax.sharding import PartitionSpec as P

BLOCK = 128


def slot_layout(block_rows, groups, per_group, capacity):
    head_count, segments, listed = block_rows.shape
    ordered = jnp.transpose(block_rows, (2, 0, 1)).reshape(-1)
    head_ids = jnp.broadcast_to(
        jnp.arange(head_count, dtype=jnp.int32)[None, :, None], (listed, head_count, segments)
    ).reshape(-1)
    owners = ordered // per_group
    req_codes = head_ids * per_group + ordered % per_group
    positions = jnp.arange(ordered.shape[0], dtype=jnp.int32)
    earlier = (owners[:, None] == owners[None, :]) & (positions[None, :] < positions[:, None])
    places = owners * capacity + jnp.sum(earlier.astype(jnp.int32), axis=1)
    targets = jnp.arange(groups * capacity, dtype=jnp.int32)
    matched = places[None, :] == targets[:, None]
    filled = jnp.any(matched, axis=1)
    source_ids = jnp.sum(jnp.where(matched, positions[None, :], 0), axis=1)
    sent_codes = jnp.where(filled, jnp.sum(jnp.where(matched, req_codes[None, :], 0), axis=1), -1)
    return (places, filled, source_ids, sent_codes.reshape(groups, capacity))


def log_total(scores, sink_grp):
    sink_side = sink_grp[:, None, None]
    row_top = jnp.maximum(jnp.max(scores, axis=-1), sink_side)
    row_total = jnp.exp(sink_side - row_top) + jnp.sum(
        jnp.exp(scores - row_top[..., None]), axis=-1
    )
    return row_top + jnp.log(row_total)


def forward_group(inputs, scaling):
    query_grp, local_kv, remote_kv, sink_grp = inputs
    head_dim = query_grp.shape[-1]
    kv_all = jnp.concatenate([local_kv, remote_kv], axis=2)
    scores = (
        jnp.einsum(
            "gsqd,gskd->gsqk", query_grp, kv_all[..., :head_dim], preferred_element_type=jnp.float32
        )
        * scaling
    )
    log_norm = log_total(scores, sink_grp)
    prob_bf = jnp.exp(scores - log_norm[..., None]).astype(jnp.bfloat16)
    attended = jnp.einsum(
        "gsqk,gskd->gsqd", prob_bf, kv_all[..., head_dim:], preferred_element_type=jnp.float32
    )
    return (attended.astype(jnp.bfloat16), log_norm)


def backward_group(inputs, scaling, seg_len):
    query_grp, local_kv, remote_kv, sink_grp, grad_grp, attended, log_norm = inputs
    head_dim = query_grp.shape[-1]
    kv_all = jnp.concatenate([local_kv, remote_kv], axis=2)
    scores = (
        jnp.einsum(
            "gsqd,gskd->gsqk", query_grp, kv_all[..., :head_dim], preferred_element_type=jnp.float32
        )
        * scaling
    )
    weights = jnp.exp(scores - log_norm[..., None])
    prob_bf = weights.astype(jnp.bfloat16)
    row_delta = jnp.sum(grad_grp.astype(jnp.float32) * attended.astype(jnp.float32), axis=-1)
    dprobs = jnp.einsum(
        "gsqd,gskd->gsqk", grad_grp, kv_all[..., head_dim:], preferred_element_type=jnp.float32
    )
    dscores = (weights * (dprobs - row_delta[..., None])).astype(jnp.bfloat16)
    grad_q = (
        jnp.einsum(
            "gsqk,gskd->gsqd", dscores, kv_all[..., :head_dim], preferred_element_type=jnp.float32
        )
        * scaling
    )
    key_terms = (
        jnp.einsum("gsqk,gsqd->gskd", dscores, query_grp, preferred_element_type=jnp.float32)
        * scaling
    )
    value_terms = jnp.einsum(
        "gsqk,gsqd->gskd", prob_bf, grad_grp, preferred_element_type=jnp.float32
    )
    all_terms = jnp.concatenate([key_terms, value_terms], axis=-1)
    sink_part = -jnp.sum(jnp.exp(sink_grp[:, None, None] - log_norm) * row_delta, axis=(1, 2))
    return (
        grad_q.astype(jnp.bfloat16),
        all_terms[:, :, :seg_len],
        all_terms[:, :, seg_len:].astype(jnp.bfloat16),
        sink_part,
    )


def body(query_in, key_in, value_in, grad_out, key_blocks, sink_logits):
    groups = lax.axis_size("ctx")
    head_count = sink_logits.shape[0]
    tok_dev = query_in.shape[1]
    head_dim = query_in.shape[2] // head_count
    seg_per_dev = key_blocks.shape[1]
    listed = key_blocks.shape[2]
    seg_len = tok_dev // seg_per_dev
    per_group = tok_dev // BLOCK
    requests = head_count * seg_per_dev * listed
    capacity = (requests + groups - 2) // (groups - 1)
    scaling = 1.0 / math.sqrt(head_dim)
    pair_heads = 2
    pair_count = head_count // pair_heads
    double_dim = 2 * head_dim
    places, filled, source_ids, sent_codes = slot_layout(key_blocks, groups, per_group, capacity)
    recv_codes = lax.all_to_all(sent_codes, "ctx", split_axis=0, concat_axis=0, tiled=True)
    local_kv = jnp.concatenate(
        [
            key_in[0].reshape(per_group, BLOCK, head_count, head_dim),
            value_in[0].reshape(per_group, BLOCK, head_count, head_dim),
        ],
        axis=-1,
    )
    safe_codes = jnp.maximum(recv_codes, 0)
    payload = local_kv[safe_codes % per_group, :, safe_codes // per_group, :]

    def arrange_remote(fetched):
        flat_slots = fetched.reshape(groups * capacity, BLOCK, double_dim)
        remote_rows = flat_slots[places].reshape(listed, head_count, seg_per_dev, BLOCK, double_dim)
        remote_rows = jnp.transpose(remote_rows, (1, 2, 0, 3, 4))
        return remote_rows.reshape(pair_count, pair_heads, seg_per_dev, listed * BLOCK, double_dim)

    def to_pairs(field):
        columns = field.shape[-1]
        split = jnp.transpose(
            field.reshape(seg_per_dev, seg_len, head_count, columns), (2, 0, 1, 3)
        )
        return split.reshape(pair_count, pair_heads, seg_per_dev, seg_len, columns)

    fetched = lax.all_to_all(payload, "ctx", split_axis=0, concat_axis=0, tiled=True)
    remote_pairs = arrange_remote(fetched)
    query_pairs = to_pairs(query_in[0].reshape(tok_dev, head_count, head_dim))
    grad_pairs = to_pairs(grad_out[0].reshape(tok_dev, head_count, head_dim))
    local_pairs = to_pairs(local_kv.reshape(tok_dev, head_count, double_dim))
    sink_pairs = sink_logits.reshape(pair_count, pair_heads)
    attended, log_norm = lax.map(
        partial(forward_group, scaling=scaling),
        (query_pairs, local_pairs, remote_pairs, sink_pairs),
    )
    back_remote = arrange_remote(
        lax.all_to_all(payload, "ctx", split_axis=0, concat_axis=0, tiled=True)
    )
    grad_q, own_terms, list_terms, sink_parts = lax.map(
        partial(backward_group, scaling=scaling, seg_len=seg_len),
        (query_pairs, local_pairs, back_remote, sink_pairs, grad_pairs, attended, log_norm),
    )
    grad_query = jnp.transpose(
        grad_q.reshape(head_count, seg_per_dev, seg_len, head_dim), (1, 2, 0, 3)
    )
    grad_query = grad_query.reshape(1, tok_dev, head_count * head_dim)
    own_flat = jnp.transpose(
        own_terms.reshape(head_count, seg_per_dev, seg_len, double_dim), (1, 2, 0, 3)
    )
    own_flat = own_flat.reshape(tok_dev, head_count, double_dim)
    list_rows = jnp.transpose(
        list_terms.reshape(head_count, seg_per_dev, listed, BLOCK, double_dim), (2, 0, 1, 3, 4)
    )
    list_rows = list_rows.reshape(requests, BLOCK, double_dim)
    send_back = jnp.where(filled[:, None, None], list_rows[source_ids], jnp.zeros((), jnp.bfloat16))
    returned = lax.all_to_all(
        send_back.reshape(groups, capacity, BLOCK, double_dim),
        "ctx",
        split_axis=0,
        concat_axis=0,
        tiled=True,
    )
    selector = (
        recv_codes.reshape(-1)[:, None]
        == jnp.arange(head_count * per_group, dtype=jnp.int32)[None, :]
    ).astype(jnp.bfloat16)
    incoming = jnp.einsum(
        "pj,pbe->jbe",
        selector,
        returned.reshape(groups * capacity, BLOCK, double_dim),
        preferred_element_type=jnp.float32,
    )
    incoming = jnp.transpose(
        incoming.reshape(head_count, per_group, BLOCK, double_dim), (1, 2, 0, 3)
    )
    combined = own_flat + incoming.reshape(tok_dev, head_count, double_dim)
    grad_key = (
        combined[..., :head_dim].astype(jnp.bfloat16).reshape(1, tok_dev, head_count * head_dim)
    )
    grad_value = (
        combined[..., head_dim:].astype(jnp.bfloat16).reshape(1, tok_dev, head_count * head_dim)
    )
    grad_sink = lax.psum(sink_parts.reshape(head_count), ("dp", "ctx"))
    return (grad_query, grad_key, grad_value, grad_sink)


def solution(mesh):
    placed = (
        P("dp", "ctx", None),
        P("dp", "ctx", None),
        P("dp", "ctx", None),
        P("dp", "ctx", None),
        P(None, "ctx", None),
        P(),
    )
    return jax.shard_map(
        body,
        mesh=mesh,
        in_specs=placed,
        out_specs=(P("dp", "ctx", None), P("dp", "ctx", None), P("dp", "ctx", None), P()),
        check_vma=False,
    )
```

profile of v0, /device:TPU:0, one launch (start us, length us, event | category | flops | bytes accessed | tf_op | source)
XLA Modules:
  0.0 309.1 jit_solution(8482472694911084584)
XLA Ops:
  2.5 5.2 %all-to-all-start = ((s32[8,1,9]{2,1,0:T(1,128)}), s32[8,1,9]{2,1,0:T(1,128)S(1)}, u32[]{:S(2)}, u32[]{:S(2)}) async-start(s32[8,1,9]{2,1,0:T(1,128)} %bitcast.31), calls=%async_computation | async-start | bytes 8192 | tf_op jit(solution)/shard_map/all_to_all | solution.py:114
  7.7 1.5 reshape.730
  10.1 2.2 all-to-all-done
  12.4 7.0 %gather_fusion = bf16[72,128,256]{2,1,0:T(8,128)(2,1)} fusion(bf16[2,128,10,256]{3,1,2,0:T(8,128)(2,1)S(1)} %pad_maximum_fusion.4, s32[72]{0:T(128)S(1)} %reshape.705), kind=kCustom, calls=%fused_computation | custom fusion | bytes 9437760 | tf_op jit(solution)/shard_map/gather | solution.py:123
  19.3 4.9 %all-to-all-start.1 = ((bf16[8,9,128,256]{3,2,1,0:T(8,128)(2,1)}), bf16[8,9,128,256]{3,2,1,0:T(8,128)(2,1)}, u32[]{:S(2)}, u32[]{:S(2)}) async-start(bf16[8,9,128,256]{3,2,1,0:T(8,128)(2,1)} %bitcast.225), calls=%async_computation.1 | async-start | bytes 9437184 | tf_op jit(solution)/shard_map/all_to_all | solution.py:149
  26.8 1.5 copy.112
  29.4 49.4 %all-to-all-done.1 = bf16[8,9,128,256]{3,2,1,0:T(8,128)(2,1)} async-done(((bf16[8,9,128,256]{3,2,1,0:T(8,128)(2,1)}), bf16[8,9,128,256]{3,2,1,0:T(8,128)(2,1)}, u32[]{:S(2)}, u32[]{:S(2)}) %all-to-all-start.1) | async-done | bytes 4718624 | tf_op jit(solution)/shard_map/all_to_all | solution.py:149
  78.8 5.0 %gather_fusion.1 = bf16[60,128,256]{2,1,0:T(8,128)(2,1)} fusion(bf16[72,128,256]{2,1,0:T(8,128)(2,1)} %bitcast.37, s32[1024]{0:T(1024)S(1)} %pad_clamp_fusion.1), kind=kCustom, calls=%fused_computation.1 | custom fusion | bytes 7864560 | tf_op jit(solution)/shard_map/gather | solution.py:127
  83.9 4.4 %copy.106 = bf16[10,1,6,128,256]{4,3,2,0,1:T(8,128)(2,1)} copy(bf16[10,1,6,128,256]{4,3,0,2,1:T(8,128)(2,1)} %bitcast.228) | data formatting | bytes 7864320 | tf_op jit(solution)/shard_map/transpose | solution.py:128
  88.3 28.0 %while.28 = (s32[]{:T(128)}, bf16[5,2,1,256,128]{4,3,1,2,0:T(8,128)(2,1)}, f32[5,2,1,256]{3,1,2,0:T(2,128)S(1)}, bf16[5,2,1,256,128]{4,3,1,2,0:T(8,128)(2,1)}, b...) while((s32[]{:T(128)}, ...), condition=%wide.region_6.7_spmd, body=%wide.region_3.6_spmd.sunk | while | flops 274796032 | bytes 10773141 | solution.py:144
  90.5 1.4 multiply_reduce_fusion.6
  96.1 1.4 multiply_reduce_fusion.6
  101.7 1.4 multiply_reduce_fusion.6
  107.3 1.4 multiply_reduce_fusion.6
  112.9 1.4 multiply_reduce_fusion.6
  116.3 66.2 %while.29 = (s32[]{:T(128)}, bf16[5,2,1,256,128]{3,4,1,0,2:T(8,128)(2,1)}, f32[5,2,1,256,256]{3,4,1,2,0:T(8,128)}, bf16[5,2,1,768,256]{4,3,1,0,2:T(8,128)(2,1)},...) while((s32[]{:T(128)}, ...), condition=%wide.region_10.11_spmd, body=%wide.region_7.10_spmd.sunk | while | flops 680788992 | bytes 31602968 | solution.py:151
  118.5 1.3 fusion.112
  125.1 1.6 fusion.115
  138.4 1.6 fusion.115
  145.0 1.3 fusion.112
  151.6 1.6 fusion.115
  164.9 1.6 fusion.115
  171.4 1.3 fusion.112
  178.1 1.6 fusion.115
  182.5 4.5 %copy.117 = bf16[6,10,1,128,256]{4,3,1,0,2:T(8,128)(2,1)} copy(bf16[6,10,1,128,256]{4,3,0,1,2:T(8,128)(2,1)} %bitcast.230) | data formatting | bytes 7864320 | tf_op jit(solution)/shard_map/transpose | solution.py:163
  187.0 7.6 %gather_fusion.2 = bf16[72,128,256]{2,1,0:T(8,128)(2,1)} fusion(bf16[60,128,256]{2,1,0:T(8,128)(2,1)} %bitcast.224, s32[1024]{0:T(1024)S(1)} %pad_clamp_fusion), kind=kCustom, calls=%fused_computation.2 | custom fusion | bytes 9437472 | tf_op jit(solution)/shard_map/gather | solution.py:167
  194.6 4.9 %broadcast_select_fusion = bf16[8,9,128,256]{3,2,1,0:T(8,128)(2,1)} fusion(bf16[8,9,128,256]{3,2,1,0:T(8,128)(2,1)} %bitcast.226, pred[8,9]{1,0:T(8,128)(4,1)S(1)} %broadcast_in_dim.98), kind=kLoop, calls=%fused_computation.88 | loop fusion | flops 2359296 | bytes 9437256 | tf_op jit(solution)/shard_map/jit(_where)/select_n | solution.py:167
  199.5 4.7 %all-to-all-start.2 = ((bf16[8,9,128,256]{3,2,1,0:T(8,128)(2,1)}), bf16[8,9,128,256]{3,2,1,0:T(8,128)(2,1)}, u32[]{:S(2)}, u32[]{:S(2)}) async-start(bf16[8,9,128,256]{3,2,1,0:T(8,128)(2,1)} %broadcast_select_fusion), calls=%async_computation.2 | async-start | bytes 9437184 | tf_op jit(solution)/shard_map/all_to_all | solution.py:168
  205.5 86.7 %psum.7 = f32[10]{0:T(128)} all-reduce(f32[10]{0:T(128)S(1)} %reshape.704), channel_id=1, replica_groups=mesh['dp'=4,'ctx'=8] {'dp','ctx'}, use_global_device_ids=true, to_apply=%region_12.13 | all-reduce | flops 10 | bytes 80 | tf_op jit(solution)/shard_map/psum | solution.py:195
  293.3 7.9 %fusion.53 = f32[10,2,128,256]{3,0,2,1:T(8,128)} fusion(bf16[72,128,256]{2,1,0:T(8,128)(2,1)} %bitcast.65, s32[10,2]{0,1:T(2,128)S(1)} %multiply_add_fusion, s32[72]{0:T(128)S(1)} %eq.67), kind=kOutput, calls=%fused_computation.85 | convolution fusion | flops 94373280 | bytes 7340400 | tf_op jit(solution)/shard_map/pj,pbe->jbe/dot_general | solution.py:179
  301.2 3.4 %copy.119 = f32[256,10,256]{0,2,1:T(8,128)S(1)} copy(f32[256,10,256]{2,1,0:T(8,128)} %bitcast.227) | data formatting | bytes 5242880 | tf_op jit(solution)/shard_map/reshape | solution.py:188
  304.6 2.2 fusion.56
  (204 shorter events, 85.7 us)
Async XLA Ops:
  0.6 0.7 copy-start
  0.6 8.7 %copy-start.4 = (bf16[1,256,1280]{2,1,0:T(8,128)(2,1)S(1)}, bf16[1,256,1280]{2,1,0:T(8,128)(2,1)}, u32[]{:S(2)}) copy-start(bf16[1,256,1280]{2,1,0:T(8,128)(2,1)} %param.11) | copy-start | bytes 1966084
  2.5 9.8 %all-to-all-start = ((s32[8,1,9]{2,1,0:T(1,128)}), s32[8,1,9]{2,1,0:T(1,128)S(1)}, u32[]{:S(2)}, u32[]{:S(2)}) async-start(s32[8,1,9]{2,1,0:T(1,128)} %bitcast.31), calls=%async_computation | async-start | bytes 8192 | tf_op jit(solution)/shard_map/all_to_all | solution.py:114
  19.3 5.0 %copy-start.3 = (bf16[1,256,1280]{2,1,0:T(8,128)(2,1)S(1)}, bf16[1,256,1280]{2,1,0:T(8,128)(2,1)}, u32[]{:S(2)}) copy-start(bf16[1,256,1280]{2,1,0:T(8,128)(2,1)} %param.12) | copy-start | bytes 1966084
  19.3 59.5 %all-to-all-start.1 = ((bf16[8,9,128,256]{3,2,1,0:T(8,128)(2,1)}), bf16[8,9,128,256]{3,2,1,0:T(8,128)(2,1)}, u32[]{:S(2)}, u32[]{:S(2)}) async-start(bf16[8,9,128,256]{3,2,1,0:T(8,128)(2,1)} %bitcast.225), calls=%async_computation.1 | async-start | bytes 9437184 | tf_op jit(solution)/shard_map/all_to_all | solution.py:149
  24.2 1.1 copy-start.5
  26.7 1.6 copy-start.8
  26.7 1.6 copy-start.6
  122.9 1.0 copy-start.2
  136.2 1.0 copy-start.2
  149.4 1.0 copy-start.2
  162.7 1.0 copy-start.2
  175.9 1.0 copy-start.2
  199.5 92.8 %copy-start.7 = (bf16[5,2,1,256,128]{3,4,1,0,2:T(8,128)(2,1)S(1)}, bf16[5,2,1,256,128]{3,4,1,0,2:T(8,128)(2,1)}, u32[]{:S(2)}) copy-start(bf16[5,2,1,256,128]{3,4,1,0,2:T(8,128)(2,1)} %get-tuple-element.109) | copy-start | bytes 1966084
  199.5 93.9 %all-to-all-start.2 = ((bf16[8,9,128,256]{3,2,1,0:T(8,128)(2,1)}), bf16[8,9,128,256]{3,2,1,0:T(8,128)(2,1)}, u32[]{:S(2)}, u32[]{:S(2)}) async-start(bf16[8,9,128,256]{3,2,1,0:T(8,128)(2,1)} %broadcast_select_fusion), calls=%async_computation.2 | async-start | bytes 9437184 | tf_op jit(solution)/shard_map/all_to_all | solution.py:168
  304.6 4.5 %copy-start.1 = (s32[10,1,6]{0,1,2:T(1,128)S(1)}, s32[10,1,6]{0,1,2:T(1,128)}, u32[]{:S(2)}) copy-start(s32[10,1,6]{0,1,2:T(1,128)} %param.14) | copy-start | bytes 724
where the time goes:
time: 311 us; the launch traced here: 309 us
  blocking collectives  86.7 us (28%)
  local copies, waits for them, and re-layouts  86.5 us (28%)
  waiting for transfers between devices  51.6 us (17%)
  matrix products  44.9 us (14%)
  other arithmetic  23.1 us (7%)
  starting transfers between devices  14.8 us (5%)
    psum x1, blocking collectives, body(): grad_sink = lax.psum(sink_parts.reshape(head_count), ('dp', 'ctx'))  86.7 us
    all_to_all x1, waiting for transfers between devices, body(): lax.all_to_all(payload, 'ctx', split_axis=0, concat_axis=0, tiled=True)  49.4 us
    squeeze x20, local copies, waits for them, and re-layouts, body(): lax.map(partial(forward_group, scaling=scaling), (query_pairs, local_pair...  21.6 us
    dot_general x5, matrix products, backward_group(): jnp.einsum('gsqk,gsqd->gskd', dscores, query_grp, preferred_element_type=...  7.88 us
    dot_general x1, matrix products, body(): jnp.einsum('pj,pbe->jbe', selector, returned.reshape(groups * capacity, B...  7.88 us
    gather x1, local copies, waits for them, and re-layouts, body(): list_rows[source_ids]  7.59 us
    dot_general x5, matrix products, forward_group(): jnp.einsum('gsqd,gskd->gsqk', query_grp, kv_all[..., :head_dim], preferre...  7.11 us
    gather x1, local copies, waits for them, and re-layouts, body(): payload = local_kv[safe_codes % per_group, :, safe_codes // per_group, :]  6.97 us
  transfers between devices with their start and end apart: 3, of which 2 were waited for; matrix products, arithmetic and copies ran while one was open for 3% of the time, Pallas kernels for 0%

commit v1 on v0

v1 whole, which is shorter than its diff:
```python
import math

import jax
import jax.numpy as jnp
from jax import lax
from jax.experimental import pallas as pl
from jax.experimental.pallas import tpu as pltpu
from jax.sharding import PartitionSpec as P

BLOCK = 128
CORES = 2
FAR = -1e30
VMEM_BYTES = 60 * 1024 * 1024
NT = (((1,), (1,)), ((), ()))
NN = (((1,), (0,)), ((), ()))
TN = (((0,), (0,)), ((), ()))


def chunk_sizes(heads):
    first = (heads + 1) // 2
    return (first, heads - first) if heads > first else (first,)


def grid_side(groups):
    side = math.isqrt(groups // CORES)
    assert CORES * side * side == groups
    return side


def moved(index, side, along_query, shift, cross):
    core, col, row = index % CORES, index // CORES % side, index // (CORES * side)
    along_col = (core == 0) == along_query
    if along_col:
        col = (col + shift) % side
    else:
        row = (row + shift) % side
    return (row * side + col) * CORES + (core ^ cross)


def gather_perm(groups, side, along_query, shift, cross):
    return [(moved(i, side, along_query, shift, cross), i) for i in range(groups)]


def return_perm(groups, side, along_query, shift, cross):
    return [(i, moved(i, side, along_query, shift, cross)) for i in range(groups)]


def dot(lhs, rhs, dims):
    return lax.dot_general(lhs, rhs, dims, preferred_element_type=jnp.float32)


def whole(count):
    return [pl.BlockSpec(memory_space=pltpu.VMEM)] * count


def pack_kernel(core_ref, *refs):
    ins, outs = refs[:8], refs[8:]
    for which in range(2):
        for pair in range(2):
            for place in range(2):
                outs[2 * which + pair][place] = ins[4 * which + 2 * pair + place][0]


def pack(core, query_in, grad_out, key_in, value_in, first, heads, half_heads):
    tokens = query_in.shape[1]
    block = (1, tokens, BLOCK)
    mine = pl.BlockSpec(block, lambda h, core: (0, 0, core[0] * half_heads + first + h))
    other = pl.BlockSpec(block, lambda h, core: (0, 0, (1 - core[0]) * half_heads + first + h))
    fields = (query_in, grad_out, key_in, value_in)
    return pl.pallas_call(
        pack_kernel,
        grid_spec=pltpu.PrefetchScalarGridSpec(
            num_scalar_prefetch=1,
            grid=(heads,),
            in_specs=[mine] * 4 + [other] * 4,
            out_specs=[head_spec((2, tokens, BLOCK))] * 4,
        ),
        out_shape=[jax.ShapeDtypeStruct((2, tokens, heads * BLOCK), jnp.bfloat16)] * 4,
        compiler_params=pltpu.CompilerParams(vmem_limit_bytes=VMEM_BYTES),
        cost_estimate=pl.CostEstimate(
            flops=0, bytes_accessed=32 * tokens * heads * BLOCK, transcendentals=0
        ),
        name="pack",
    )(core, *fields, *fields)


def head_spec(shape):
    lead = len(shape) - 1
    return pl.BlockSpec(shape, lambda h, *_: (0,) * lead + (h,))


def stat_spec(rows, tokens):
    return pl.BlockSpec((1, rows, tokens), lambda h, *_: (h, 0, 0))


def spread(refs, firsts, seconds, rows):
    per_slot = refs[0].shape[1] // rows
    for slot, ref in enumerate(refs):
        for part in range(per_slot):
            firsts[slot * per_slot + part] = ref[0, pl.ds(part * rows, rows), :]
            seconds[slot * per_slot + part] = ref[1, pl.ds(part * rows, rows), :]


def paired(ref, one, two):
    return jnp.concatenate([ref[one], ref[two]], axis=0)


def tile_products(tile, bound, base, lists, held, scores, dprobs):
    slot_ref, one_ref, two_ref = lists
    queries, grad_outs, keys, values = held
    place = base + jnp.minimum(tile, bound - 1)
    slot, one, two = slot_ref[place], one_ref[place], two_ref[place]
    raw = dot(paired(keys, one, jnp.maximum(two, 0)), queries[slot], NT)
    scores[:BLOCK] = raw[:BLOCK]
    scores[BLOCK:] = raw[BLOCK:] + jnp.where((two >= 0) & (tile < bound), 0.0, FAR)
    dprobs[...] = dot(paired(values, one, jnp.maximum(two, 0)), grad_outs[slot], NT)


def walk(count, products, work, even, odd):
    products(0, *even)

    def step(index, carry):
        tile = 2 * index
        products(tile + 1, *odd)
        work(tile, *even)
        products(tile + 2, *even)

        @pl.when(tile + 1 < count)
        def _():
            work(tile + 1, *odd)

        return carry

    lax.fori_loop(0, (count + 1) // 2, step, 0)


def stats_kernel(first, slots, most, scaling, cnt_ref, slot_ref, one_ref, two_ref, sink_ref, *refs):
    qd_refs, kv_refs = refs[:slots], refs[slots : 2 * slots]
    out_ref, keys, values, queries, grad_outs, rows, *buffers = refs[2 * slots :]
    head = pl.program_id(0) + first
    tokens = qd_refs[0].shape[1]
    spread(kv_refs, keys, values, BLOCK)
    spread(qd_refs, queries, grad_outs, tokens)
    zero = jnp.zeros((1, tokens), jnp.float32)
    for slot in range(slots):
        rows[slot, 0:1, :] = zero + sink_ref[head]
        rows[slot, 1:2, :] = zero
        rows[slot, 2:3, :] = zero
    base = head * most
    count = cnt_ref[head]
    lists = (slot_ref, one_ref, two_ref)
    held = (queries, grad_outs, keys, values)

    def products(tile, scores, dprobs):
        tile_products(tile, count, base, lists, held, scores, dprobs)

    def work(tile, scores, dprobs):
        slot = slot_ref[base + tile]
        old = rows[slot, 0:1, :]
        top = jnp.maximum(old, jnp.max(scores[...], axis=0, keepdims=True) * scaling)
        parts = jnp.exp(scores[...] * scaling - top)
        shrink = jnp.exp(old - top)
        rows[slot, 0:1, :] = top
        rows[slot, 1:2, :] = rows[slot, 1:2, :] * shrink + jnp.sum(parts, axis=0, keepdims=True)
        rows[slot, 2:3, :] = rows[slot, 2:3, :] * shrink + jnp.sum(
            parts * dprobs[...], axis=0, keepdims=True
        )

    walk(count, products, work, buffers[:2], buffers[2:])
    for slot in range(slots):
        for kind in range(3):
            out_ref[0, pl.ds(kind * slots + slot, 1), :] = rows[slot, kind : kind + 1, :]


def tile_scratch(slots, tokens):
    blocks = slots * (tokens // BLOCK)
    return [pltpu.VMEM((blocks, BLOCK, BLOCK), jnp.bfloat16)] * 2 + [
        pltpu.VMEM((slots, tokens, BLOCK), jnp.bfloat16)
    ] * 2


def tile_buffers(tokens):
    return [pltpu.VMEM((2 * BLOCK, tokens), jnp.float32)] * 4


def stats(lists, sink, qd, kv, first, heads, most, scaling):
    slots, tokens = len(qd), qd[0].shape[1]
    rows = -(-3 * slots // 8) * 8
    tiles = heads * slots * 4
    return pl.pallas_call(
        lambda *refs: stats_kernel(first, slots, most, scaling, *refs),
        grid_spec=pltpu.PrefetchScalarGridSpec(
            num_scalar_prefetch=5,
            grid=(heads,),
            in_specs=[head_spec((2, tokens, BLOCK))] * (2 * slots),
            out_specs=stat_spec(rows, tokens),
            scratch_shapes=tile_scratch(slots, tokens)
            + [pltpu.VMEM((slots, 8, tokens), jnp.float32)]
            + tile_buffers(tokens),
        ),
        out_shape=jax.ShapeDtypeStruct((heads, rows, tokens), jnp.float32),
        compiler_params=pltpu.CompilerParams(vmem_limit_bytes=VMEM_BYTES),
        cost_estimate=pl.CostEstimate(
            flops=tiles * 4 * tokens * BLOCK * BLOCK,
            bytes_accessed=heads * slots * 8 * tokens * BLOCK,
            transcendentals=tiles * tokens * BLOCK,
        ),
        name="row_stats",
    )(*lists, sink, *qd, *kv)


def settle(stat_refs, slot, slots, sink):
    side = len(stat_refs)
    parts = []
    for shift, ref in enumerate(stat_refs):
        place = (slot // CORES - shift) % side * CORES + slot % CORES
        parts.append([ref[0, pl.ds(kind * slots + place, 1), :] for kind in range(3)])
    top = parts[0][0]
    for part in parts[1:]:
        top = jnp.maximum(top, part[0])
    total, mixed = jnp.exp(sink - top), jnp.zeros_like(top)
    for part in parts:
        grow = jnp.exp(part[0] - top)
        total = total + part[1] * grow
        mixed = mixed + part[2] * grow
    return top + jnp.log(total), mixed / total


def grads_kernel(
    first, slots, side, most, scaling, cnt_ref, slot_ref, one_ref, two_ref, sink_ref, *refs
):
    qd_refs, kv_refs = refs[:slots], refs[slots : 2 * slots]
    stat_refs = refs[2 * slots : 2 * slots + side]
    rest = refs[2 * slots + side :]
    remote = slots - CORES
    dq_home, dkv_home, core_out = rest[:3]
    dq_out, dkv_out = rest[3 : 3 + remote], rest[3 + remote : 3 + 2 * remote]
    sink_out = rest[3 + 2 * remote]
    keys, values, queries, grad_outs, rows, dkeys, dvalues, dquery, *buffers = rest[4 + 2 * remote :]
    head = pl.program_id(0) + first
    tokens = qd_refs[0].shape[1]
    spread(kv_refs, keys, values, BLOCK)
    spread(qd_refs, queries, grad_outs, tokens)
    sink = sink_ref[head]
    dkeys[...] = jnp.zeros_like(dkeys)
    dvalues[...] = jnp.zeros_like(dvalues)
    dquery[...] = jnp.zeros_like(dquery)
    sink_row = jnp.zeros((1, tokens), jnp.float32)
    for slot in range(slots):
        log_norm, row_delta = settle(stat_refs, slot, slots, sink)
        rows[slot, 0:1, :] = log_norm
        rows[slot, 1:2, :] = row_delta
        if slot < CORES:
            sink_row = sink_row - jnp.exp(sink - log_norm) * row_delta
    sink_out[0] = jnp.broadcast_to(sink_row, sink_out.shape[1:])
    base = head * most
    count = cnt_ref[head]
    lists = (slot_ref, one_ref, two_ref)
    held = (queries, grad_outs, keys, values)

    def products(tile, scores, dprobs):
        tile_products(tile, count, base, lists, held, scores, dprobs)

    def work(tile, scores, dprobs):
        slot, one = slot_ref[base + tile], one_ref[base + tile]
        two = jnp.maximum(two_ref[base + tile], 0)
        weights = jnp.exp(scores[...] * scaling - rows[slot, 0:1, :])
        probs = weights.astype(jnp.bfloat16)
        dscores = (weights * (dprobs[...] - rows[slot, 1:2, :])).astype(jnp.bfloat16)
        dquery[slot] += dot(paired(keys, one, two), dscores, TN)
        dkey = dot(dscores, queries[slot], NN)
        dvalue = dot(probs, grad_outs[slot], NN)
        dkeys[one] += dkey[:BLOCK]
        dkeys[two] += dkey[BLOCK:]
        dvalues[one] += dvalue[:BLOCK]
        dvalues[two] += dvalue[BLOCK:]

    walk(count, products, work, buffers[:2], buffers[2:])
    for slot in range(slots):
        total = dquery[slot].T * scaling
        if slot == 0:
            dq_home[...] = total
        elif slot < CORES:
            core_out[0] = total.astype(jnp.bfloat16)
        else:
            dq_out[slot - CORES][...] = total.astype(jnp.bfloat16)
    per_slot = tokens // BLOCK
    for slot in range(slots):
        for part in range(per_slot):
            span = pl.ds(part * BLOCK, BLOCK)
            dkey = dkeys[slot * per_slot + part] * scaling
            dvalue = dvalues[slot * per_slot + part]
            if slot == 0:
                dkv_home[0, span, :] = dkey
                dkv_home[1, span, :] = dvalue
            else:
                ref = core_out if slot < CORES else dkv_out[slot - CORES]
                lead = 1 if slot < CORES else 0
                ref[lead, span, :] = dkey.astype(jnp.bfloat16)
                ref[lead + 1, span, :] = dvalue.astype(jnp.bfloat16)


def grads(lists, sink, qd, kv, partials, first, heads, most, scaling):
    slots, tokens = len(qd), qd[0].shape[1]
    side, rows = len(partials), partials[0].shape[1]
    remote = slots - CORES
    blocks = slots * (tokens // BLOCK)
    tiles = heads * slots * 4
    width = heads * BLOCK
    low, high = jnp.bfloat16, jnp.float32
    one, two, three = (tokens, BLOCK), (2, tokens, BLOCK), (3, tokens, BLOCK)
    shapes = [(one, high), (two, high), (three, low)] + [(one, low)] * remote + [(two, low)] * remote
    return pl.pallas_call(
        lambda *refs: grads_kernel(first, slots, side, most, scaling, *refs),
        grid_spec=pltpu.PrefetchScalarGridSpec(
            num_scalar_prefetch=5,
            grid=(heads,),
            in_specs=[head_spec(two)] * (2 * slots) + [stat_spec(rows, tokens)] * side,
            out_specs=[head_spec(shape) for shape, _ in shapes] + [stat_spec(8, tokens)],
            scratch_shapes=tile_scratch(slots, tokens)
            + [pltpu.VMEM((slots, 8, tokens), high)]
            + [pltpu.VMEM((blocks, BLOCK, BLOCK), high)] * 2
            + [pltpu.VMEM((slots, BLOCK, tokens), high)]
            + tile_buffers(tokens),
        ),
        out_shape=[jax.ShapeDtypeStruct(shape[:-1] + (width,), kind) for shape, kind in shapes]
        + [jax.ShapeDtypeStruct((heads, 8, tokens), high)],
        compiler_params=pltpu.CompilerParams(vmem_limit_bytes=VMEM_BYTES),
        cost_estimate=pl.CostEstimate(
            flops=tiles * 10 * tokens * BLOCK * BLOCK,
            bytes_accessed=heads * slots * 16 * tokens * BLOCK,
            transcendentals=tiles * tokens * BLOCK,
        ),
        name="gradients",
    )(*lists, sink, *qd, *kv, *partials)


def close_kernel(sizes, side, half, core_ref, *refs):
    per = 3 + 4 * (side - 1)
    outs = refs[per * len(sizes) :]
    core = core_ref[0]
    first = 0
    for chunk, heads in enumerate(sizes):
        width = heads * BLOCK
        dq_home, dkv_home, from_core, *far = refs[per * chunk : per * (chunk + 1)]
        dq_far, dkv_far = far[: 2 * (side - 1)], far[2 * (side - 1) :]
        mine = pl.ds(pl.multiple_of(core * half + first, BLOCK), width)
        other = pl.ds(pl.multiple_of((1 - core) * half + first, BLOCK), width)
        for place, out in enumerate(outs):
            if place == 0:
                parts = [dq_home[...], from_core[0]] + [ref[...] for ref in dq_far]
            else:
                parts = [dkv_home[place - 1], from_core[place]] + [ref[place - 1] for ref in dkv_far]
            parts = [part.astype(jnp.float32) for part in parts]
            out[0, :, mine] = sum(parts[2::2], parts[0]).astype(jnp.bfloat16)
            out[0, :, other] = sum(parts[3::2], parts[1]).astype(jnp.bfloat16)
        first += width


def close(core, pieces, sizes, side, half, tokens):
    flat = [piece for chunk in pieces for piece in chunk]
    return pl.pallas_call(
        lambda *refs: close_kernel(sizes, side, half, *refs),
        in_specs=[pl.BlockSpec(memory_space=pltpu.SMEM)] + whole(len(flat)),
        out_specs=whole(3),
        out_shape=[jax.ShapeDtypeStruct((1, tokens, 2 * half), jnp.bfloat16)] * 3,
        compiler_params=pltpu.CompilerParams(vmem_limit_bytes=VMEM_BYTES),
        cost_estimate=pl.CostEstimate(
            flops=tokens * half * 12, bytes_accessed=tokens * half * 42, transcendentals=0
        ),
        name="closing_sums",
    )(core, *flat)


def tile_lists(rows, key_devs, per_group):
    heads, slots, listed = rows.shape
    hit = (rows // per_group)[..., None] == key_devs
    slot_ids = jnp.arange(slots, dtype=jnp.int32)
    places = jnp.sum(jnp.where(hit, slot_ids * per_group, 0), axis=-1) + rows % per_group
    found = jnp.any(hit, axis=-1)
    ahead = jnp.arange(listed)[None, :] < jnp.arange(listed)[:, None]
    before = jnp.sum((ahead & found[..., None, :]).astype(jnp.int32), axis=-1)
    own = jnp.where(slot_ids < CORES, per_group // 2, 0)
    needs = own + (jnp.sum(found.astype(jnp.int32), axis=-1) + 1) // 2
    upto = jnp.sum(jnp.where(slot_ids[None, :] <= slot_ids[:, None], needs[:, None, :], 0), axis=-1)
    start = upto - needs
    most = slots * ((listed + 1) // 2) + CORES * (per_group // 2)
    target = jnp.arange(most, dtype=jnp.int32)
    tiles = (start + own)[..., None] + before // 2
    meet = (found[..., None] & (tiles[..., None] == target)).astype(jnp.int32)
    even = (before % 2 == 0).astype(jnp.int32)
    ones = jnp.sum(meet * (places * even)[..., None], axis=(1, 2))
    twos = jnp.sum(meet * ((places + 1) * (1 - even))[..., None], axis=(1, 2)) - 1
    for slot in range(CORES):
        step = target[None, :] - start[:, slot : slot + 1]
        home = (step >= 0) & (step < per_group // 2)
        ones = ones + jnp.where(home, slot * per_group + 2 * step, 0)
        twos = twos + jnp.where(home, slot * per_group + 2 * step + 2, 0)
    where_to = jnp.sum((upto[:, None, :] <= target[None, :, None]).astype(jnp.int32), axis=-1)
    where_to = jnp.minimum(where_to, slots - 1)
    flat = (where_to.reshape(-1), ones.reshape(-1), twos.reshape(-1))
    return (upto[:, -1],) + flat, most


def key_devices(me, side):
    core, col, row = me % CORES, me // CORES % side, me // (CORES * side)
    shifts = jnp.arange(side, dtype=jnp.int32)[:, None]
    cores = core ^ jnp.arange(CORES, dtype=jnp.int32)[None, :]
    by_col = (row * side + (col + shifts) % side) * CORES + cores
    by_row = ((row + shifts) % side * side + col) * CORES + cores
    return jnp.where(core == 0, by_row, by_col).reshape(-1)


def spot_sum(part, groups, me):
    copies = lax.axis_size("dp")
    side = grid_side(groups)
    spot = lax.axis_index("dp") * groups + me
    held = jnp.where(jnp.arange(copies * groups)[:, None] == spot, part[None, :], 0.0)
    for axis, perms in (
        ("dp", [[(i, (i + s) % copies) for i in range(copies)] for s in range(1, copies)]),
        ("ctx", [gather_perm(groups, side, True, s, 0) for s in range(1, side)]),
        ("ctx", [gather_perm(groups, side, False, s, 0) for s in range(1, side)]),
        ("ctx", [gather_perm(groups, side, True, 0, 1)]),
    ):
        came = [lax.ppermute(held, axis, perm) for perm in perms]
        held = sum(came, held)
    return jnp.sum(held, axis=0)


def body(query_in, key_in, value_in, grad_out, key_blocks, sink_logits):
    groups = lax.axis_size("ctx")
    side = grid_side(groups)
    head_count = sink_logits.shape[0]
    tokens = query_in.shape[1]
    per_group = tokens // BLOCK
    assert key_blocks.shape[1] == 1 and query_in.shape[2] == head_count * BLOCK
    assert per_group % 2 == 0 and head_count % CORES == 0
    half_heads = head_count // 2
    half = half_heads * BLOCK
    scaling = 1.0 / math.sqrt(BLOCK)
    sizes = chunk_sizes(half_heads)
    me = lax.axis_index("ctx").astype(jnp.int32)
    core = me % CORES
    core_arg = core.reshape(1)
    swap = gather_perm(groups, side, True, 0, 1)
    places = [(shift, cross) for shift in range(1, side) for cross in range(CORES)]

    asked = key_blocks[:, 0, :]
    asked_own = jnp.where(core == 0, asked[:half_heads], asked[half_heads:])
    asked_oth = jnp.where(core == 0, asked[half_heads:], asked[:half_heads])
    rows = [asked_own, lax.ppermute(asked_oth, "ctx", swap)] + [
        lax.ppermute(
            asked_oth if cross else asked_own, "ctx", gather_perm(groups, side, True, shift, cross)
        )
        for shift, cross in places
    ]
    lists, most = tile_lists(jnp.stack(rows, axis=1), key_devices(me, side), per_group)
    sink = jnp.where(core == 0, sink_logits[:half_heads], sink_logits[half_heads:])

    starts = [sum(sizes[:i]) for i in range(len(sizes))]
    qds, kvs = [], []
    for first, heads in zip(starts, sizes):
        qd_own, kv_own, qd_oth, kv_oth = pack(
            core_arg, query_in, grad_out, key_in, value_in, first, heads, half_heads
        )
        qd = [qd_own, lax.ppermute(qd_oth, "ctx", swap)]
        kv = [kv_own, lax.ppermute(kv_oth, "ctx", swap)]
        for shift, cross in places:
            perm = gather_perm(groups, side, True, shift, cross)
            qd.append(lax.ppermute(qd_oth if cross else qd_own, "ctx", perm))
            perm = gather_perm(groups, side, False, shift, cross)
            kv.append(lax.ppermute(kv_oth if cross else kv_own, "ctx", perm))
        qds.append(qd)
        kvs.append(kv)

    pieces, sink_rows = [], []
    for chunk, (first, heads) in enumerate(zip(starts, sizes)):
        qd, kv = qds[chunk], kvs[chunk]
        partial = stats(lists, sink, qd, kv, first, heads, most, scaling)
        partials = [partial] + [
            lax.ppermute(partial, "ctx", gather_perm(groups, side, True, shift, 0))
            for shift in range(1, side)
        ]
        results = grads(lists, sink, qd, kv, partials, first, heads, most, scaling)
        remote = len(places)
        dq_home, dkv_home, core_out = results[:3]
        dq_out, dkv_out = results[3 : 3 + remote], results[3 + remote : 3 + 2 * remote]
        sink_rows.append(jnp.sum(results[-1][:, 0, :], axis=-1))
        back = [
            lax.ppermute(value, "ctx", return_perm(groups, side, along_query, shift, cross))
            for along_query, values in ((True, dq_out), (False, dkv_out))
            for value, (shift, cross) in zip(values, places)
        ]
        pieces.append([dq_home, dkv_home, lax.ppermute(core_out, "ctx", swap)] + back)

    sink_half = jnp.concatenate(sink_rows)
    zeros = jnp.zeros_like(sink_half)
    sink_part = jnp.where(
        core == 0, jnp.concatenate([sink_half, zeros]), jnp.concatenate([zeros, sink_half])
    )
    grad_sink = spot_sum(sink_part, groups, me)
    grad_query, grad_key, grad_value = close(core_arg, pieces, sizes, side, half, tokens)
    return (grad_query, grad_key, grad_value, grad_sink)


def solution(mesh):
    tokens = P("dp", "ctx", None)
    return jax.shard_map(
        body,
        mesh=mesh,
        in_specs=(tokens, tokens, tokens, tokens, P(None, "ctx", None), P()),
        out_specs=(tokens, tokens, tokens, P()),
        check_vma=False,
    )
```

time: 311 us -> 133 us (0.43)
  blocking collectives: 86.7 us -> 0 us
  local copies, waits for them, and re-layouts: 86.5 us -> 7.69 us
  Pallas kernels: 0 us -> 51.5 us
  matrix products: 44.9 us -> 0 us
  other arithmetic: 23.1 us -> 5.79 us
  starting transfers between devices: 14.8 us -> 21.4 us
  waiting for transfers between devices: 51.6 us -> 45.2 us
    psum x1 -> x0, blocking collectives: 86.7 us -> none  [body(): grad_sink = lax.psum(sink_parts.reshape(head_count), ('dp', 'ctx'))]
    all_to_all x3 -> x0, waiting for transfers between devices: 51.6 us -> none  [the longest x1 49.4 us: body(): lax.all_to_all(payload, 'ctx', split_axis=0, concat_axis=0, tiled=True)]
    pallas_call x0 -> x7, Pallas kernels: none -> 51.5 us  [the longest x2 25.1 us: grads(): pl.pallas_call(lambda *refs: grads_kernel(first, slots, side, most, scali...]
    ppermute x0 -> x33, waiting for transfers between devices: none -> 45.2 us  [the longest x8 18.3 us: body(): lax.ppermute(value, 'ctx', return_perm(groups, side, along_query, shift,...]
    dot_general x36 -> x0, matrix products: 44.9 us -> none  [the longest x5 7.88 us: backward_group(): jnp.einsum('gsqk,gsqd->gskd', dscores, query_grp, preferred_element_type=...]
    ppermute x0 -> x33, starting transfers between devices: none -> 21.4 us  [the longest x6 5.63 us: spot_sum(): came = [lax.ppermute(held, axis, perm) for perm in perms]]
    squeeze x20 -> x1, local copies, waits for them, and re-layouts: 21.6 us -> 0.51 us  [tile_lists(): return ((upto[:, -1],) + flat, most)]
    gather x3 -> x0, local copies, waits for them, and re-layouts: 19.6 us -> none  [the longest x1 7.59 us: body(): list_rows[source_ids]]
  transfers between devices with their start and end apart: 3 -> 33, of which waited for: 2 -> 15; matrix products, arithmetic and copies ran while one was open for 3% -> 6% of each run, Pallas kernels for 0% -> 17%
where the time goes in v1:
time: 133 us
  Pallas kernels  51.5 us (39%)
  waiting for transfers between devices  45.2 us (34%)
  starting transfers between devices  21.4 us (16%)
  local copies, waits for them, and re-layouts  7.69 us (6%)
  other arithmetic  5.79 us (4%)
    pallas_call x2, Pallas kernels, grads(): pl.pallas_call(lambda *refs: grads_kernel(first, slots, side, most, scali...  25.1 us
    ppermute x8, waiting for transfers between devices, body(): lax.ppermute(value, 'ctx', return_perm(groups, side, along_query, shift,...  18.3 us
    pallas_call x2, Pallas kernels, stats(): pl.pallas_call(lambda *refs: stats_kernel(first, slots, most, scaling, *r...  16.8 us
    ppermute x6, waiting for transfers between devices, spot_sum(): came = [lax.ppermute(held, axis, perm) for perm in perms]  9.62 us
    ppermute x4, waiting for transfers between devices, body(): kv.append(lax.ppermute(kv_oth if cross else kv_own, 'ctx', perm))  8.97 us
    pallas_call x2, Pallas kernels, pack(): pl.pallas_call(pack_kernel, grid_spec=pltpu.PrefetchScalarGridSpec(num_sc...  5.7 us
    ppermute x6, starting transfers between devices, spot_sum(): came = [lax.ppermute(held, axis, perm) for perm in perms]  5.63 us
    unnamed x74, local copies, waits for them, and re-layouts  4.82 us
  transfers between devices with their start and end apart: 33, of which 15 were waited for; matrix products, arithmetic and copies ran while one was open for 6% of the time, Pallas kernels for 17%

profile of v1, /device:TPU:0, one launch (start us, length us, event | category | flops | bytes accessed | tf_op | source)
XLA Modules:
  0.0 132.7 jit_solution(10686249363023513647)
XLA Ops:
  1.9 2.5 %collective-permute-start.2 = (s32[5,6]{1,0:T(8,128)S(1)}, s32[5,6]{1,0:T(8,128)S(1)}, u32[]{:S(2)}, u32[]{:S(2)}) collective-permute-start(s32[5,6]{1,0:T(8,128)S(1)} %get-tuple-element.70), channel_id=1, source_target_pairs={{3,0},{4,1},{1,2},{6,3},{7,4},{0,5},{5,6},{2,7},{11,8},{12,9},{9,1... | collective-permute-start | bytes 368 | tf_op jit(solution)/shard_map/ppermute | solution.py:452
  5.0 2.2 %pack.3 = (bf16[2,256,256]{2,1,0:T(8,128)(2,1)}, bf16[2,256,256]{2,1,0:T(8,128)(2,1)}, bf16[2,256,256]{2,1,0:T(8,128)(2,1)}, bf16[2,256,256]{2,1,0:T(8,128)(2,1)}) custom-call(s32[1]{0:T(128)} %bitcast.core_ref.refs_0_, bf16[1,256,1280]{2,1,0:T(8,128)(2,1)} %refs_4_.3, bf16[1,256,1280]{2,1,0:T(8,128)(2,1)} %refs_5_.3, bf16[1,256,1280]{2,1,0:T(8,128)(2,1)} %refs_6_.3, ...), custom_call_target="tpu_custom_call" | custom-call | bytes 2097152 | tf_op jit(solution)/shard_map/pack/pallas_call | solution.py:70
  7.3 1.6 %collective-permute-start.17 = (bf16[2,256,256]{2,1,0:T(8,128)(2,1)}, bf16[2,256,256]{2,1,0:T(8,128)(2,1)S(1)}, u32[]{:S(2)}, u32[]{:S(2)}) collective-permute-start(bf16[2,256,256]{2,1,0:T(8,128)(2,1)} %get-tuple-element.43), channel_id=1, source_target_pairs={{3,0},{4,1},{1,2},{6,3},{7,4},{0,5},{5,6},{2,7},{11,8},{12,9},{9,1... | collective-permute-start | bytes 786440 | tf_op jit(solution)/shard_map/ppermute | solution.py:470
  10.9 3.5 %pack.2 = (bf16[2,256,384]{2,1,0:T(8,128)(2,1)}, bf16[2,256,384]{2,1,0:T(8,128)(2,1)}, bf16[2,256,384]{2,1,0:T(8,128)(2,1)}, bf16[2,256,384]{2,1,0:T(8,128)(2,1)}) custom-call(s32[1]{0:T(128)} %bitcast.core_ref.refs_0_, bf16[1,256,1280]{2,1,0:T(8,128)(2,1)} %refs_4_.3, bf16[1,256,1280]{2,1,0:T(8,128)(2,1)} %refs_5_.3, bf16[1,256,1280]{2,1,0:T(8,128)(2,1)} %refs_6_.3, ...), custom_call_target="tpu_custom_call" | custom-call | bytes 3145728 | tf_op jit(solution)/shard_map/pack/pallas_call | solution.py:70
  14.6 1.6 %collective-permute-start.20 = (bf16[2,256,256]{2,1,0:T(8,128)(2,1)S(1)}, bf16[2,256,256]{2,1,0:T(8,128)(2,1)S(1)}, u32[]{:S(2)}, u32[]{:S(2)}) collective-permute-start(bf16[2,256,256]{2,1,0:T(8,128)(2,1)S(1)} %copy-done.29), channel_id=1, source_target_pairs={{5,0},{2,1},{7,2},{0,3},{1,4},{6,5},{3,6},{4,7},{13,8},{10,9},{15,... | collective-permute-start | bytes 786440 | tf_op jit(solution)/shard_map/ppermute | solution.py:472
  20.1 3.8 %collective-permute-done.16.refs_7_ = bf16[2,256,256]{2,1,0:T(8,128)(2,1)S(1)} collective-permute-done((bf16[2,256,256]{2,1,0:T(8,128)(2,1)S(1)}, bf16[2,256,256]{2,1,0:T(8,128)(2,1)S(1)}, u32[]{:S(2)}, u32[]{:S(2)}) %collective-permute-start.16) | collective-permute-done | bytes 262176 | tf_op jit(solution)/shard_map/ppermute | solution.py:470
  26.6 3.7 %collective-permute-done.19.refs_11_ = bf16[2,256,256]{2,1,0:T(8,128)(2,1)S(1)} collective-permute-done((bf16[2,256,256]{2,1,0:T(8,128)(2,1)S(1)}, bf16[2,256,256]{2,1,0:T(8,128)(2,1)S(1)}, u32[]{:S(2)}, u32[]{:S(2)}) %collective-permute-start.19) | collective-permute-done | bytes 262176 | tf_op jit(solution)/shard_map/ppermute | solution.py:472
  31.1 7.1 %row_stats.3.refs_13_ = f32[2,16,256]{2,1,0:T(8,128)} custom-call(s32[5]{0:T(128)} %slice_bitcast_fusion.refs_0_, s32[70]{0:T(128)} %min.12.refs_1_, s32[70]{0:T(128)} %get-tuple-element.75.refs_2_, s32[70]{0:T(128)} %get-tuple-element.74.refs_3_, f32[5]{0:T(128)} %broadcast_select_fusion.4.refs_4_, bf16[2,256,256]{2,1,0:T(8,128)(2,1)} %get-tuple-element.42.refs_5_, ...), custom_call_target="tpu_custom_call" | custom-call | flops 536870912 | bytes 2097152 | tf_op jit(solution)/shard_map/row_stats/pallas_call | solution.py:190
  38.1 1.4 %collective-permute-start.21 = (f32[2,16,256]{2,1,0:T(8,128)}, f32[2,16,256]{2,1,0:T(8,128)S(1)}, u32[]{:S(2)}, u32[]{:S(2)}) collective-permute-start(f32[2,16,256]{2,1,0:T(8,128)} %row_stats.3.refs_13_), channel_id=1, source_target_pairs={{2,0},{5,1},{0,2},{7,3},{6,4},{1,5},{4,6},{3,7},{10,8},{13,9},{8,1... | collective-permute-start | bytes 98312 | tf_op jit(solution)/shard_map/ppermute | solution.py:481
  40.2 1.0 collective-permute-start.6
  41.2 1.1 collective-permute-done.21.refs_14_
  42.3 1.2 collective-permute-start.7
  43.5 10.2 %gradients.3 = (f32[256,256]{1,0:T(8,128)}, f32[2,256,256]{2,1,0:T(8,128)}, bf16[3,256,256]{2,1,0:T(8,128)(2,1)}, bf16[256,256]{1,0:T(8,128)(2,1)}, bf16[256,256...) custom-call(s32[5]{0:T(128)} %slice_bitcast_fusion.refs_0_, ...), custom_call_target="tpu_custom_call" | custom-call | flops 1342177280 | bytes 4194304 | tf_op jit(solution)/shard_map/gradients/pallas_call | solution.py:313
  53.8 4.6 %collective-permute-done.7.refs_11_ = bf16[2,256,384]{2,1,0:T(8,128)(2,1)S(1)} collective-permute-done((bf16[2,256,384]{2,1,0:T(8,128)(2,1)S(1)}, bf16[2,256,384]{2,1,0:T(8,128)(2,1)S(1)}, u32[]{:S(2)}, u32[]{:S(2)}) %collective-permute-start.7) | collective-permute-done | bytes 393248 | tf_op jit(solution)/shard_map/ppermute | solution.py:472
  59.9 9.7 %row_stats.2.refs_13_ = f32[3,16,256]{2,1,0:T(8,128)} custom-call(s32[5]{0:T(128)} %slice_bitcast_fusion.refs_0_, s32[70]{0:T(128)} %min.12.refs_1_, s32[70]{0:T(128)} %get-tuple-element.75.refs_2_, s32[70]{0:T(128)} %get-tuple-element.74.refs_3_, f32[5]{0:T(128)} %broadcast_select_fusion.4.refs_4_, bf16[2,256,384]{2,1,0:T(8,128)(2,1)} %get-tuple-element.31.refs_5_, ...), custom_call_target="tpu_custom_call" | custom-call | flops 805306368 | bytes 3145728 | tf_op jit(solution)/shard_map/row_stats/pallas_call | solution.py:190
  70.5 3.5 %collective-permute-done.9.refs_14_ = f32[3,16,256]{2,1,0:T(8,128)S(1)} collective-permute-done((f32[3,16,256]{2,1,0:T(8,128)}, f32[3,16,256]{2,1,0:T(8,128)S(1)}, u32[]{:S(2)}, u32[]{:S(2)}) %collective-permute-start.9) | collective-permute-done | bytes 49184 | tf_op jit(solution)/shard_map/ppermute | solution.py:481
  74.6 14.9 %gradients.2 = (f32[256,384]{1,0:T(8,128)}, f32[2,256,384]{2,1,0:T(8,128)}, bf16[3,256,384]{2,1,0:T(8,128)(2,1)}, bf16[256,384]{1,0:T(8,128)(2,1)}, bf16[256,384...) custom-call(s32[5]{0:T(128)} %slice_bitcast_fusion.refs_0_, ...), custom_call_target="tpu_custom_call" | custom-call | flops 2013265920 | bytes 6291456 | tf_op jit(solution)/shard_map/gradients/pallas_call | solution.py:313
  90.5 3.6 %collective-permute-start.29 = (f32[32,10]{0,1:T(8,128)S(1)}, f32[32,10]{0,1:T(8,128)S(1)}, u32[]{:S(2)}, u32[]{:S(2)}) collective-permute-start(f32[32,10]{0,1:T(8,128)S(1)} %broadcast_select_fusion.2), channel_id=1, source_target_pairs={{0,24},{8,0},{16,8},{24,16},{1,25},{9,1},{17,9},{25,17},{2,26},{10... | collective-permute-start | bytes 3848 | tf_op jit(solution)/shard_map/ppermute | solution.py:425
  94.1 1.0 collective-permute-start.27
  95.1 1.0 collective-permute-start.25
  96.2 2.4 %collective-permute-done.28 = f32[32,10]{0,1:T(8,128)S(1)} collective-permute-done((f32[32,10]{0,1:T(8,128)S(1)}, f32[32,10]{0,1:T(8,128)S(1)}, u32[]{:S(2)}, u32[]{:S(2)}) %collective-permute-start.28) | collective-permute-done | bytes 1312 | tf_op jit(solution)/shard_map/ppermute | solution.py:425
  98.6 0.9 collective-permute-done.27
  99.6 3.6 %collective-permute-done.30 = f32[32,10]{0,1:T(8,128)S(1)} collective-permute-done((f32[32,10]{0,1:T(8,128)S(1)}, f32[32,10]{0,1:T(8,128)S(1)}, u32[]{:S(2)}, u32[]{:S(2)}) %collective-permute-start.30) | collective-permute-done | bytes 1312 | tf_op jit(solution)/shard_map/ppermute | solution.py:425
  103.3 1.0 collective-permute-start.31
  104.3 2.6 %collective-permute-done.31 = f32[32,10]{0,1:T(8,128)S(1)} collective-permute-done((f32[32,10]{0,1:T(8,128)S(1)}, f32[32,10]{0,1:T(8,128)S(1)}, u32[]{:S(2)}, u32[]{:S(2)}) %collective-permute-start.31) | collective-permute-done | bytes 1312 | tf_op jit(solution)/shard_map/ppermute | solution.py:425
  106.9 2.3 %collective-permute-done.23.refs_11_ = bf16[256,256]{1,0:T(8,128)(2,1)S(1)} collective-permute-done((bf16[256,256]{1,0:T(8,128)(2,1)S(1)}, bf16[256,256]{1,0:T(8,128)(2,1)S(1)}, u32[]{:S(2)}, u32[]{:S(2)}) %collective-permute-start.23) | collective-permute-done | bytes 131104 | tf_op jit(solution)/shard_map/ppermute | solution.py:490
  109.2 2.1 %collective-permute-done.24.refs_12_ = bf16[256,256]{1,0:T(8,128)(2,1)S(1)} collective-permute-done((bf16[256,256]{1,0:T(8,128)(2,1)S(1)}, bf16[256,256]{1,0:T(8,128)(2,1)S(1)}, u32[]{:S(2)}, u32[]{:S(2)}) %collective-permute-start.24) | collective-permute-done | bytes 131104 | tf_op jit(solution)/shard_map/ppermute | solution.py:490
  111.7 1.0 collective-permute-start.13
  113.3 5.9 %collective-permute-done.11.refs_4_ = bf16[256,384]{1,0:T(8,128)(2,1)S(1)} collective-permute-done((bf16[256,384]{1,0:T(8,128)(2,1)}, bf16[256,384]{1,0:T(8,128)(2,1)S(1)}, u32[]{:S(2)}, u32[]{:S(2)}) %collective-permute-start.11) | collective-permute-done | bytes 196640 | tf_op jit(solution)/shard_map/ppermute | solution.py:490
  119.8 6.8 %collective-permute-done.12.refs_5_ = bf16[256,384]{1,0:T(8,128)(2,1)S(1)} collective-permute-done((bf16[256,384]{1,0:T(8,128)(2,1)}, bf16[256,384]{1,0:T(8,128)(2,1)S(1)}, u32[]{:S(2)}, u32[]{:S(2)}) %collective-permute-start.12) | collective-permute-done | bytes 196640 | tf_op jit(solution)/shard_map/ppermute | solution.py:490
  126.7 1.1 collective-permute-done.14.refs_7_
  128.8 3.9 %closing_sums.1 = (bf16[1,256,1280]{2,1,0:T(8,128)(2,1)}, bf16[1,256,1280]{2,1,0:T(8,128)(2,1)}, bf16[1,256,1280]{2,1,0:T(8,128)(2,1)}) custom-call(s32[1]{0:T(128)} %bitcast.core_ref.refs_0_, f32[256,384]{1,0:T(8,128)} %get-tuple-element.35.refs_1_, f32[2,256,384]{2,1,0:T(8,128)} %get-tuple-element.36.refs_2_, bf16[3,256,384]{2,1,0:T(8,128)(2,1)} %copy-done, ...), custom_call_target="tpu_custom_call" | custom-call | flops 1966080 | bytes 6881280 | tf_op jit(solution)/shard_map/closing_sums/pallas_call | solution.py:362
  (170 shorter events, 18.7 us)
Async XLA Ops:
  1.9 12.5 %collective-permute-start.2 = (s32[5,6]{1,0:T(8,128)S(1)}, s32[5,6]{1,0:T(8,128)S(1)}, u32[]{:S(2)}, u32[]{:S(2)}) collective-permute-start(s32[5,6]{1,0:T(8,128)S(1)} %get-tuple-element.70), channel_id=1, source_target_pairs={{3,0},{4,1},{1,2},{6,3},{7,4},{0,5},{5,6},{2,7},{11,8},{12,9},{9,1... | collective-permute-start | bytes 368 | tf_op jit(solution)/shard_map/ppermute | solution.py:452
  4.4 12.0 %collective-permute-start = (s32[5,6]{1,0:T(8,128)S(1)}, s32[5,6]{1,0:T(8,128)S(1)}, u32[]{:S(2)}, u32[]{:S(2)}) collective-permute-start(s32[5,6]{1,0:T(8,128)S(1)} %get-tuple-element.70), channel_id=1, source_target_pairs={{1,0},{0,1},{3,2},{2,3},{5,4},{4,5},{7,6},{6,7},{9,8},{8,9},{11,10... | collective-permute-start | bytes 368 | tf_op jit(solution)/shard_map/ppermute | solution.py:451
  7.2 12.8 %collective-permute-start.15 = (bf16[2,256,256]{2,1,0:T(8,128)(2,1)}, bf16[2,256,256]{2,1,0:T(8,128)(2,1)S(1)}, u32[]{:S(2)}, u32[]{:S(2)}) collective-permute-start(bf16[2,256,256]{2,1,0:T(8,128)(2,1)} %get-tuple-element.43), channel_id=1, source_target_pairs={{1,0},{0,1},{3,2},{2,3},{5,4},{4,5},{7,6},{6,7},{9,8},{8,9},{11,10... | collective-permute-start | bytes 786440 | tf_op jit(solution)/shard_map/ppermute | solution.py:466
  7.3 19.2 %collective-permute-start.17 = (bf16[2,256,256]{2,1,0:T(8,128)(2,1)}, bf16[2,256,256]{2,1,0:T(8,128)(2,1)S(1)}, u32[]{:S(2)}, u32[]{:S(2)}) collective-permute-start(bf16[2,256,256]{2,1,0:T(8,128)(2,1)} %get-tuple-element.43), channel_id=1, source_target_pairs={{3,0},{4,1},{1,2},{6,3},{7,4},{0,5},{5,6},{2,7},{11,8},{12,9},{9,1... | collective-permute-start | bytes 786440 | tf_op jit(solution)/shard_map/ppermute | solution.py:470
  8.9 5.6 %collective-permute-start.1 = (s32[5,6]{1,0:T(8,128)S(1)}, s32[5,6]{1,0:T(8,128)S(1)}, u32[]{:S(2)}, u32[]{:S(2)}) collective-permute-start(s32[5,6]{1,0:T(8,128)S(1)} %get-tuple-element.66), channel_id=1, source_target_pairs={{2,0},{5,1},{0,2},{7,3},{6,4},{1,5},{4,6},{3,7},{10,8},{13,9},{8,1... | collective-permute-start | bytes 368 | tf_op jit(solution)/shard_map/ppermute | solution.py:452
  14.4 12.1 %collective-permute-start.18 = (bf16[2,256,256]{2,1,0:T(8,128)(2,1)S(1)}, bf16[2,256,256]{2,1,0:T(8,128)(2,1)S(1)}, u32[]{:S(2)}, u32[]{:S(2)}) collective-permute-start(bf16[2,256,256]{2,1,0:T(8,128)(2,1)S(1)} %copy-done.29), channel_id=1, source_target_pairs={{1,0},{0,1},{3,2},{2,3},{5,4},{4,5},{7,6},{6,7},{9,8},{8,9},{11,10... | collective-permute-start | bytes 786440 | tf_op jit(solution)/shard_map/ppermute | solution.py:467
  14.6 15.7 %collective-permute-start.20 = (bf16[2,256,256]{2,1,0:T(8,128)(2,1)S(1)}, bf16[2,256,256]{2,1,0:T(8,128)(2,1)S(1)}, u32[]{:S(2)}, u32[]{:S(2)}) collective-permute-start(bf16[2,256,256]{2,1,0:T(8,128)(2,1)S(1)} %copy-done.29), channel_id=1, source_target_pairs={{5,0},{2,1},{7,2},{0,3},{1,4},{6,5},{3,6},{4,7},{13,8},{10,9},{15,... | collective-permute-start | bytes 786440 | tf_op jit(solution)/shard_map/ppermute | solution.py:472
  16.3 7.6 %collective-permute-start.16 = (bf16[2,256,256]{2,1,0:T(8,128)(2,1)S(1)}, bf16[2,256,256]{2,1,0:T(8,128)(2,1)S(1)}, u32[]{:S(2)}, u32[]{:S(2)}) collective-permute-start(bf16[2,256,256]{2,1,0:T(8,128)(2,1)S(1)} %copy-done.14), channel_id=1, source_target_pairs={{2,0},{5,1},{0,2},{7,3},{6,4},{1,5},{4,6},{3,7},{10,8},{13,9},{8,1... | collective-permute-start | bytes 786440 | tf_op jit(solution)/shard_map/ppermute | solution.py:470
  20.1 23.4 %collective-permute-start.3 = (bf16[2,256,384]{2,1,0:T(8,128)(2,1)}, bf16[2,256,384]{2,1,0:T(8,128)(2,1)S(1)}, u32[]{:S(2)}, u32[]{:S(2)}) collective-permute-start(bf16[2,256,384]{2,1,0:T(8,128)(2,1)} %get-tuple-element.32), channel_id=1, source_target_pairs={{1,0},{0,1},{3,2},{2,3},{5,4},{4,5},{7,6},{6,7},{9,8},{8,9},{11,10... | collective-permute-start | bytes 1179656 | tf_op jit(solution)/shard_map/ppermute | solution.py:466
  23.9 6.4 %collective-permute-start.19 = (bf16[2,256,256]{2,1,0:T(8,128)(2,1)S(1)}, bf16[2,256,256]{2,1,0:T(8,128)(2,1)S(1)}, u32[]{:S(2)}, u32[]{:S(2)}) collective-permute-start(bf16[2,256,256]{2,1,0:T(8,128)(2,1)S(1)} %copy-done.15), channel_id=1, source_target_pairs={{4,0},{3,1},{6,2},{1,3},{0,4},{7,5},{2,6},{5,7},{12,8},{11,9},{14,... | collective-permute-start | bytes 786440 | tf_op jit(solution)/shard_map/ppermute | solution.py:472
  38.1 4.1 %collective-permute-start.21 = (f32[2,16,256]{2,1,0:T(8,128)}, f32[2,16,256]{2,1,0:T(8,128)S(1)}, u32[]{:S(2)}, u32[]{:S(2)}) collective-permute-start(f32[2,16,256]{2,1,0:T(8,128)} %row_stats.3.refs_13_), channel_id=1, source_target_pairs={{2,0},{5,1},{0,2},{7,3},{6,4},{1,5},{4,6},{3,7},{10,8},{13,9},{8,1... | collective-permute-start | bytes 98312 | tf_op jit(solution)/shard_map/ppermute | solution.py:481
  39.5 14.2 %collective-permute-start.5 = (bf16[2,256,384]{2,1,0:T(8,128)(2,1)}, bf16[2,256,384]{2,1,0:T(8,128)(2,1)S(1)}, u32[]{:S(2)}, u32[]{:S(2)}) collective-permute-start(bf16[2,256,384]{2,1,0:T(8,128)(2,1)} %get-tuple-element.32), channel_id=1, source_target_pairs={{3,0},{4,1},{1,2},{6,3},{7,4},{0,5},{5,6},{2,7},{11,8},{12,9},{9,1... | collective-permute-start | bytes 1179656 | tf_op jit(solution)/shard_map/ppermute | solution.py:470
  39.5 14.2 %collective-permute-start.4 = (bf16[2,256,384]{2,1,0:T(8,128)(2,1)S(1)}, bf16[2,256,384]{2,1,0:T(8,128)(2,1)S(1)}, u32[]{:S(2)}, u32[]{:S(2)}) collective-permute-start(bf16[2,256,384]{2,1,0:T(8,128)(2,1)S(1)} %copy-done.1), channel_id=1, source_target_pairs={{2,0},{5,1},{0,2},{7,3},{6,4},{1,5},{4,6},{3,7},{10,8},{13,9},{8,1... | collective-permute-start | bytes 1179656 | tf_op jit(solution)/shard_map/ppermute | solution.py:470
  40.2 13.6 %collective-permute-start.6 = (bf16[2,256,384]{2,1,0:T(8,128)(2,1)}, bf16[2,256,384]{2,1,0:T(8,128)(2,1)S(1)}, u32[]{:S(2)}, u32[]{:S(2)}) collective-permute-start(bf16[2,256,384]{2,1,0:T(8,128)(2,1)} %get-tuple-element.34), channel_id=1, source_target_pairs={{1,0},{0,1},{3,2},{2,3},{5,4},{4,5},{7,6},{6,7},{9,8},{8,9},{11,10... | collective-permute-start | bytes 1179656 | tf_op jit(solution)/shard_map/ppermute | solution.py:467
  42.3 16.1 %collective-permute-start.7 = (bf16[2,256,384]{2,1,0:T(8,128)(2,1)S(1)}, bf16[2,256,384]{2,1,0:T(8,128)(2,1)S(1)}, u32[]{:S(2)}, u32[]{:S(2)}) collective-permute-start(bf16[2,256,384]{2,1,0:T(8,128)(2,1)S(1)} %copy-done.2), channel_id=1, source_target_pairs={{4,0},{3,1},{6,2},{1,3},{0,4},{7,5},{2,6},{5,7},{12,8},{11,9},{14,... | collective-permute-start | bytes 1179656 | tf_op jit(solution)/shard_map/ppermute | solution.py:472
  43.5 15.6 %collective-permute-start.8 = (bf16[2,256,384]{2,1,0:T(8,128)(2,1)}, bf16[2,256,384]{2,1,0:T(8,128)(2,1)S(1)}, u32[]{:S(2)}, u32[]{:S(2)}) collective-permute-start(bf16[2,256,384]{2,1,0:T(8,128)(2,1)} %get-tuple-element.34), channel_id=1, source_target_pairs={{5,0},{2,1},{7,2},{0,3},{1,4},{6,5},{3,6},{4,7},{13,8},{10,9},{15,... | collective-permute-start | bytes 1179656 | tf_op jit(solution)/shard_map/ppermute | solution.py:472
  69.7 4.3 %collective-permute-start.9 = (f32[3,16,256]{2,1,0:T(8,128)}, f32[3,16,256]{2,1,0:T(8,128)S(1)}, u32[]{:S(2)}, u32[]{:S(2)}) collective-permute-start(f32[3,16,256]{2,1,0:T(8,128)} %row_stats.2.refs_13_), channel_id=1, source_target_pairs={{2,0},{5,1},{0,2},{7,3},{6,4},{1,5},{4,6},{3,7},{10,8},{13,9},{8,1... | collective-permute-start | bytes 147464 | tf_op jit(solution)/shard_map/ppermute | solution.py:481
  90.5 5.6 %collective-permute-start.29 = (f32[32,10]{0,1:T(8,128)S(1)}, f32[32,10]{0,1:T(8,128)S(1)}, u32[]{:S(2)}, u32[]{:S(2)}) collective-permute-start(f32[32,10]{0,1:T(8,128)S(1)} %broadcast_select_fusion.2), channel_id=1, source_target_pairs={{0,24},{8,0},{16,8},{24,16},{1,25},{9,1},{17,9},{25,17},{2,26},{10... | collective-permute-start | bytes 3848 | tf_op jit(solution)/shard_map/ppermute | solution.py:425
  94.1 4.5 %collective-permute-start.28 = (f32[32,10]{0,1:T(8,128)S(1)}, f32[32,10]{0,1:T(8,128)S(1)}, u32[]{:S(2)}, u32[]{:S(2)}) collective-permute-start(f32[32,10]{0,1:T(8,128)S(1)} %broadcast_select_fusion.2), channel_id=1, source_target_pairs={{0,16},{8,24},{16,0},{24,8},{1,17},{9,25},{17,1},{25,9},{2,18},{10... | collective-permute-start | bytes 3848 | tf_op jit(solution)/shard_map/ppermute | solution.py:425
  94.1 5.4 %collective-permute-start.27 = (f32[32,10]{0,1:T(8,128)S(1)}, f32[32,10]{0,1:T(8,128)S(1)}, u32[]{:S(2)}, u32[]{:S(2)}) collective-permute-start(f32[32,10]{0,1:T(8,128)S(1)} %broadcast_select_fusion.2), channel_id=1, source_target_pairs={{0,8},{8,16},{16,24},{24,0},{1,9},{9,17},{17,25},{25,1},{2,10},{10... | collective-permute-start | bytes 3848 | tf_op jit(solution)/shard_map/ppermute | solution.py:425
  95.1 16.6 %collective-permute-start.25 = (bf16[2,256,256]{2,1,0:T(8,128)(2,1)S(1)}, bf16[2,256,256]{2,1,0:T(8,128)(2,1)S(1)}, u32[]{:S(2)}, u32[]{:S(2)}) collective-permute-start(bf16[2,256,256]{2,1,0:T(8,128)(2,1)S(1)} %copy-done.31), channel_id=1, source_target_pairs={{0,4},{1,3},{2,6},{3,1},{4,0},{5,7},{6,2},{7,5},{8,12},{9,11},{10,... | collective-permute-start | bytes 786440 | tf_op jit(solution)/shard_map/ppermute | solution.py:490
  96.1 16.6 %collective-permute-start.26 = (bf16[2,256,256]{2,1,0:T(8,128)(2,1)S(1)}, bf16[2,256,256]{2,1,0:T(8,128)(2,1)S(1)}, u32[]{:S(2)}, u32[]{:S(2)}) collective-permute-start(bf16[2,256,256]{2,1,0:T(8,128)(2,1)S(1)} %copy-done.30), channel_id=1, source_target_pairs={{0,5},{1,2},{2,7},{3,0},{4,1},{5,6},{6,3},{7,4},{8,13},{9,10},{10,... | collective-permute-start | bytes 786440 | tf_op jit(solution)/shard_map/ppermute | solution.py:490
  96.1 31.7 %collective-permute-start.10 = (bf16[3,256,384]{2,1,0:T(8,128)(2,1)}, bf16[3,256,384]{2,1,0:T(8,128)(2,1)S(1)}, u32[]{:S(2)}, u32[]{:S(2)}) collective-permute-start(bf16[3,256,384]{2,1,0:T(8,128)(2,1)} %get-tuple-element.37), channel_id=1, source_target_pairs={{1,0},{0,1},{3,2},{2,3},{5,4},{4,5},{7,6},{6,7},{9,8},{8,9},{11,10... | collective-permute-start | bytes 1769480 | tf_op jit(solution)/shard_map/ppermute | solution.py:494
  99.6 3.7 %collective-permute-start.30 = (f32[32,10]{0,1:T(8,128)S(1)}, f32[32,10]{0,1:T(8,128)S(1)}, u32[]{:S(2)}, u32[]{:S(2)}) collective-permute-start(f32[32,10]{0,1:T(8,128)S(1)} %add_add_fusion), channel_id=1, source_target_pairs={{2,0},{5,1},{0,2},{7,3},{6,4},{1,5},{4,6},{3,7},{10,8},{13,9},{8,1... | collective-permute-start | bytes 3848 | tf_op jit(solution)/shard_map/ppermute | solution.py:425
  103.3 3.7 %collective-permute-start.31 = (f32[32,10]{0,1:T(8,128)S(1)}, f32[32,10]{0,1:T(8,128)S(1)}, u32[]{:S(2)}, u32[]{:S(2)}) collective-permute-start(f32[32,10]{0,1:T(8,128)S(1)} %add.314), channel_id=1, source_target_pairs={{4,0},{3,1},{6,2},{1,3},{0,4},{7,5},{2,6},{5,7},{12,8},{11,9},{14,... | collective-permute-start | bytes 3848 | tf_op jit(solution)/shard_map/ppermute | solution.py:425
  104.3 5.0 %collective-permute-start.23 = (bf16[256,256]{1,0:T(8,128)(2,1)S(1)}, bf16[256,256]{1,0:T(8,128)(2,1)S(1)}, u32[]{:S(2)}, u32[]{:S(2)}) collective-permute-start(bf16[256,256]{1,0:T(8,128)(2,1)S(1)} %copy-done.33), channel_id=1, source_target_pairs={{0,2},{1,5},{2,0},{3,7},{4,6},{5,1},{6,4},{7,3},{8,10},{9,13},{10,... | collective-permute-start | bytes 393224 | tf_op jit(solution)/shard_map/ppermute | solution.py:490
  106.9 4.4 %collective-permute-start.24 = (bf16[256,256]{1,0:T(8,128)(2,1)S(1)}, bf16[256,256]{1,0:T(8,128)(2,1)S(1)}, u32[]{:S(2)}, u32[]{:S(2)}) collective-permute-start(bf16[256,256]{1,0:T(8,128)(2,1)S(1)} %copy-done.32), channel_id=1, source_target_pairs={{0,3},{1,4},{2,1},{3,6},{4,7},{5,0},{6,5},{7,2},{8,11},{9,12},{10,... | collective-permute-start | bytes 393224 | tf_op jit(solution)/shard_map/ppermute | solution.py:490
  111.3 15.4 %collective-permute-start.22 = (bf16[3,256,256]{2,1,0:T(8,128)(2,1)S(1)}, bf16[3,256,256]{2,1,0:T(8,128)(2,1)S(1)}, u32[]{:S(2)}, u32[]{:S(2)}) collective-permute-start(bf16[3,256,256]{2,1,0:T(8,128)(2,1)S(1)} %copy-done.28), channel_id=1, source_target_pairs={{1,0},{0,1},{3,2},{2,3},{5,4},{4,5},{7,6},{6,7},{9,8},{8,9},{11,10... | collective-permute-start | bytes 1179656 | tf_op jit(solution)/shard_map/ppermute | solution.py:494
  111.3 7.9 %collective-permute-start.11 = (bf16[256,384]{1,0:T(8,128)(2,1)}, bf16[256,384]{1,0:T(8,128)(2,1)S(1)}, u32[]{:S(2)}, u32[]{:S(2)}) collective-permute-start(bf16[256,384]{1,0:T(8,128)(2,1)} %get-tuple-element.38), channel_id=1, source_target_pairs={{0,2},{1,5},{2,0},{3,7},{4,6},{5,1},{6,4},{7,3},{8,10},{9,13},{10,... | collective-permute-start | bytes 589832 | tf_op jit(solution)/shard_map/ppermute | solution.py:490
  111.7 15.0 %collective-permute-start.13 = (bf16[2,256,384]{2,1,0:T(8,128)(2,1)}, bf16[2,256,384]{2,1,0:T(8,128)(2,1)S(1)}, u32[]{:S(2)}, u32[]{:S(2)}) collective-permute-start(bf16[2,256,384]{2,1,0:T(8,128)(2,1)} %get-tuple-element.40), channel_id=1, source_target_pairs={{0,4},{1,3},{2,6},{3,1},{4,0},{5,7},{6,2},{7,5},{8,12},{9,11},{10,... | collective-permute-start | bytes 1179656 | tf_op jit(solution)/shard_map/ppermute | solution.py:490
  112.7 15.1 %collective-permute-start.14 = (bf16[2,256,384]{2,1,0:T(8,128)(2,1)}, bf16[2,256,384]{2,1,0:T(8,128)(2,1)S(1)}, u32[]{:S(2)}, u32[]{:S(2)}) collective-permute-start(bf16[2,256,384]{2,1,0:T(8,128)(2,1)} %get-tuple-element.41), channel_id=1, source_target_pairs={{0,5},{1,2},{2,7},{3,0},{4,1},{5,6},{6,3},{7,4},{8,13},{9,10},{10,... | collective-permute-start | bytes 1179656 | tf_op jit(solution)/shard_map/ppermute | solution.py:490
  119.2 7.5 %collective-permute-start.12 = (bf16[256,384]{1,0:T(8,128)(2,1)}, bf16[256,384]{1,0:T(8,128)(2,1)S(1)}, u32[]{:S(2)}, u32[]{:S(2)}) collective-permute-start(bf16[256,384]{1,0:T(8,128)(2,1)} %get-tuple-element.39), channel_id=1, source_target_pairs={{0,3},{1,4},{2,1},{3,6},{4,7},{5,0},{6,5},{7,2},{8,11},{9,12},{10,... | collective-permute-start | bytes 589832 | tf_op jit(solution)/shard_map/ppermute | solution.py:490
  (37 other events, 335.6 us)

commit v2 on v0

v2 whole, which is shorter than its diff:
```python
import math

import jax
import jax.numpy as jnp
from jax import lax
from jax.experimental import pallas as pl
from jax.experimental.pallas import tpu as pltpu
from jax.sharding import PartitionSpec as P

BLOCK = 128
CORES = 2
FAR = -1e30
VMEM_BYTES = 24 * 1024 * 1024
FEW_BYTES = 2 * 1024 * 1024
UNROLL = 5
EXTRA = 16
SMALL = pl.CostEstimate(flops=1, bytes_accessed=1, transcendentals=0)
NT = (((1,), (1,)), ((), ()))
NN = (((1,), (0,)), ((), ()))
TN = (((0,), (0,)), ((), ()))


def chunk_sizes(heads):
    first = (heads + 1) // 2
    return (first, heads - first) if heads > first else (first,)


def grid_side(groups):
    side = math.isqrt(groups // CORES)
    assert CORES * side * side == groups
    return side


def moved(index, side, along_query, shift, cross):
    core, col, row = index % CORES, index // CORES % side, index // (CORES * side)
    along_col = (core == 0) == along_query
    if along_col:
        col = (col + shift) % side
    else:
        row = (row + shift) % side
    return (row * side + col) * CORES + (core ^ cross)


def gather_perm(groups, side, along_query, shift, cross):
    return [(moved(i, side, along_query, shift, cross), i) for i in range(groups)]


def return_perm(groups, side, along_query, shift, cross):
    return [(i, moved(i, side, along_query, shift, cross)) for i in range(groups)]


def dot(lhs, rhs, dims):
    return lax.dot_general(lhs, rhs, dims, preferred_element_type=jnp.float32)


def whole(count):
    return [pl.BlockSpec(memory_space=pltpu.VMEM)] * count


def pack_kernel(first, heads, every, half, q_ref, g_ref, k_ref, v_ref, *rest):
    qd_own, kv_own, qd_oth, kv_oth = rest[:4]
    sems = rest[-1]
    fields = (q_ref, g_ref, k_ref, v_ref)
    core = lax.axis_index("ctx") % CORES
    copies = []

    def copy(ref, which, head, out):
        start = (core if which == 0 else 1 - core) * half + head * BLOCK
        columns = pl.ds(pl.multiple_of(start, BLOCK), BLOCK)
        copies.append(pltpu.make_async_copy(ref.at[0, :, columns], out, sems.at[len(copies)]))

    for head in range(heads):
        for which, outs in enumerate(((qd_own, kv_own), (qd_oth, kv_oth))):
            for place, ref in enumerate(fields):
                copy(ref, which, first + head, outs[place // 2].at[head, place % 2])
    for head in range(every):
        for place, ref in enumerate(fields):
            copy(ref, 1, head, rest[4].at[head, place])
    for each in copies:
        each.start()
    for each in copies:
        each.wait()


def pack(fields, first, heads, every, half):
    tokens = fields[0].shape[1]
    shapes = [(heads, 2, tokens, BLOCK)] * 4 + [(every, 4, tokens, BLOCK)] * (every > 0)
    return pl.pallas_call(
        lambda *refs: pack_kernel(first, heads, every, half, *refs),
        in_specs=[pl.BlockSpec(memory_space=pltpu.HBM)] * 4,
        out_specs=whole(len(shapes)),
        out_shape=[jax.ShapeDtypeStruct(shape, jnp.bfloat16) for shape in shapes],
        scratch_shapes=[pltpu.SemaphoreType.DMA((heads * 8 + every * 4,))],
        compiler_params=pltpu.CompilerParams(vmem_limit_bytes=VMEM_BYTES),
        cost_estimate=SMALL,
        name="pack",
    )(*fields)


def spread(spans, slots, refs, query_side, key_side):
    place = 0
    for span, (first, heads) in enumerate(spans):
        here = refs[span * 2 * slots : (span + 1) * 2 * slots]
        qd_refs, kv_refs = here[:slots], here[slots:]
        parts = kv_refs[0].shape[2] // BLOCK
        for head in range(heads):
            for slot in range(slots):
                from_core = slot == 1
                row = head + (first if from_core else 0)
                for kind in range(2):
                    lead = kind + (2 if from_core else 0)
                    query_side[kind][place] = qd_refs[slot][row, kind]
                    for part in range(parts):
                        key_side[kind][place * parts + part] = kv_refs[slot][
                            row, lead, pl.ds(part * BLOCK, BLOCK), :
                        ]
                place += 1


def paired(ref, one, two):
    return jnp.concatenate([ref[one], ref[two]], axis=0)


def tile_products(tile, tiles, query_side, key_side):
    bound = tiles[0]
    real = tile < bound
    code = tiles[1 + jnp.minimum(tile, bound - 1)]
    query, one, two = code & 255, (code >> 8) & 255, (code >> 16) - 1
    both = real & (two >= 0)
    two = jnp.maximum(two, 0)
    raw = dot(paired(key_side[0], one, two), query_side[0][query], NT)
    scores = jnp.concatenate(
        [raw[:BLOCK] + jnp.where(real, 0.0, FAR), raw[BLOCK:] + jnp.where(both, 0.0, FAR)], axis=0
    )
    dprobs = dot(paired(key_side[1], one, two), query_side[1][query], NT)
    return query, one, two, scores, dprobs


def walk(tiles, query_side, key_side, work):
    def step(index, carry):
        made = [
            tile_products(UNROLL * index + i, tiles, query_side, key_side) for i in range(UNROLL)
        ]
        for one in made:
            work(*one)
        return carry

    lax.fori_loop(0, (tiles[0] + UNROLL - 1) // UNROLL, step, 0)


def tile_scratch(heads, slots, tokens):
    query_side = pltpu.VMEM((heads * slots, tokens, BLOCK), jnp.bfloat16)
    key_side = pltpu.VMEM((heads * slots * (tokens // BLOCK), BLOCK, BLOCK), jnp.bfloat16)
    return [query_side] * 2 + [key_side] * 2 + [pltpu.VMEM((heads * slots, 8, tokens), jnp.float32)]


def stats_kernel(first, heads, slots, scaling, tiles, sink_ref, *refs):
    out_ref, q_all, g_all, k_all, v_all, rows = refs[-6:]
    query_side, key_side = (q_all, g_all), (k_all, v_all)
    spread([(first, heads)], slots, refs, query_side, key_side)
    zero = jnp.zeros((1, out_ref.shape[2]), jnp.float32)
    for head in range(heads):
        for slot in range(slots):
            rows[head * slots + slot, 0:1, :] = zero + sink_ref[first + head]
            rows[head * slots + slot, 1:2, :] = zero
            rows[head * slots + slot, 2:3, :] = zero

    def work(query, one, two, scores, dprobs):
        old = rows[query, 0:1, :]
        top = jnp.maximum(old, jnp.max(scores, axis=0, keepdims=True) * scaling)
        parts = jnp.exp(scores * scaling - top)
        shrink = jnp.exp(old - top)
        rows[query, 0:1, :] = top
        rows[query, 1:2, :] = rows[query, 1:2, :] * shrink + jnp.sum(parts, axis=0, keepdims=True)
        rows[query, 2:3, :] = rows[query, 2:3, :] * shrink + jnp.sum(
            parts * dprobs, axis=0, keepdims=True
        )

    walk(tiles, query_side, key_side, work)
    for head in range(heads):
        for slot in range(slots):
            for kind in range(3):
                out_ref[head, pl.ds(kind * slots + slot, 1), :] = rows[
                    head * slots + slot, kind : kind + 1, :
                ]


def stats(tiles, sink, qd, kv, first, heads, scaling):
    slots, tokens = len(qd), qd[0].shape[2]
    rows = -(-3 * slots // 8) * 8
    return pl.pallas_call(
        lambda *refs: stats_kernel(first, heads, slots, scaling, *refs),
        in_specs=[pl.BlockSpec(memory_space=pltpu.SMEM)] * 2 + whole(2 * slots),
        out_specs=whole(1)[0],
        out_shape=jax.ShapeDtypeStruct((heads, rows, tokens), jnp.float32),
        scratch_shapes=tile_scratch(heads, slots, tokens),
        compiler_params=pltpu.CompilerParams(vmem_limit_bytes=VMEM_BYTES),
        cost_estimate=SMALL,
        name="row_stats",
    )(tiles, sink, *qd, *kv)


def settle(parts, sink):
    top = parts[0][0]
    for part in parts[1:]:
        top = jnp.maximum(top, part[0])
    total, mixed = jnp.exp(sink - top), jnp.zeros_like(top)
    for part in parts:
        grow = jnp.exp(part[0] - top)
        total = total + part[1] * grow
        mixed = mixed + part[2] * grow
    return top + jnp.log(total), mixed / total


def stat_place(slot, shift, side):
    return (slot // CORES - shift) % side * CORES + slot % CORES


def stat_rows(refs, head, slot, slots):
    side = len(refs)
    return [
        [ref[head, pl.ds(kind * slots + stat_place(slot, shift, side), 1), :] for kind in range(3)]
        for shift, ref in enumerate(refs)
    ]


def ordered(items, at, side):
    made = []
    for place in range(side):
        value = items[place]
        for own in range(1, side):
            value = jnp.where(at == own, items[(place - own) % side], value)
        made.append(value)
    return made


def coordinates(side):
    rest, core = halved(lax.axis_index("ctx"), CORES)
    row, col = halved(rest, side)
    return core, jnp.where(core == 0, col, row), jnp.where(core == 0, row, col)


def sink_terms(stat_groups, slots, side, sink_ref, at_query):
    lane = lax.broadcasted_iota(jnp.int32, (1, BLOCK), 1)
    terms = jnp.zeros((1, BLOCK), jnp.float32)
    done = 0
    for stat_refs in stat_groups:
        for head in range(stat_refs[0].shape[0]):
            sink = sink_ref[done]
            chips = []
            for shift in range(side):
                total = 0.0
                for cross in range(CORES):
                    rows = stat_rows(stat_refs, head, shift * CORES + cross, slots)
                    kinds = [ordered(kind, at_query, side) for kind in zip(*rows)]
                    log_norm, row_delta = settle(list(zip(*kinds)), sink)
                    total = total + jnp.exp(sink - log_norm) * row_delta
                chips.append(total)
            total = jnp.sum(sum(ordered(chips, at_query, side)))
            terms = terms - jnp.where(lane == done, total, 0.0)
            done += 1
    return terms


def put_terms(ref, terms):
    high = terms.astype(jnp.bfloat16)
    rest = terms - high.astype(jnp.float32)
    middle = rest.astype(jnp.bfloat16)
    low = (rest - middle.astype(jnp.float32)).astype(jnp.bfloat16)
    row = lax.broadcasted_iota(jnp.int32, (EXTRA, BLOCK), 0)
    rows = [part.astype(jnp.float32) for part in (high, middle, low)]
    block = jnp.zeros((EXTRA, BLOCK), jnp.float32)
    for place, part in enumerate(rows):
        block = jnp.where(row == place, part, block)
    ref[pl.ds(ref.shape[0] - EXTRA, EXTRA), :] = block.astype(jnp.bfloat16)


def get_terms(ref):
    block = ref[...].astype(jnp.float32)
    return block[0:1] + block[1:2] + block[2:3]


def grads_kernel(first, heads, slots, side, scaling, groups, tiles, sink_ref, *refs):
    stat_groups = [refs[2 * slots + i * side :][:side] for i in range(groups)]
    stat_refs = stat_groups[-1]
    rest = refs[2 * slots + groups * side :]
    remote = slots - CORES
    if first:
        done = rest[0].shape[0]
        rest[3][:done, :] = rest[0][...]
        rest = rest[1:]
    dq_home, dkv_home, core_out = rest[:3]
    dq_out, dkv_out = rest[3 : 3 + remote], rest[3 + remote : 3 + 2 * remote]
    q_all, g_all, k_all, v_all, rows, dkeys, dvalues, dquery = rest[-8:]
    query_side, key_side = (q_all, g_all), (k_all, v_all)
    spread([(first, heads)], slots, refs, query_side, key_side)
    dkeys[...] = jnp.zeros_like(dkeys)
    dvalues[...] = jnp.zeros_like(dvalues)
    dquery[...] = jnp.zeros_like(dquery)
    for head in range(heads):
        for slot in range(slots):
            log_norm, row_delta = settle(
                stat_rows(stat_refs, head, slot, slots), sink_ref[first + head]
            )
            rows[head * slots + slot, 0:1, :] = log_norm
            rows[head * slots + slot, 1:2, :] = row_delta

    def work(query, one, two, scores, dprobs):
        weights = jnp.exp(scores * scaling - rows[query, 0:1, :])
        probs = weights.astype(jnp.bfloat16)
        dscores = (weights * (dprobs - rows[query, 1:2, :])).astype(jnp.bfloat16)
        dquery[query] += dot(paired(k_all, one, two), dscores, TN)
        dkey = dot(dscores, q_all[query], NN)
        dvalue = dot(probs, g_all[query], NN)
        dkeys[one] += dkey[:BLOCK]
        dkeys[two] += dkey[BLOCK:]
        dvalues[one] += dvalue[:BLOCK]
        dvalues[two] += dvalue[BLOCK:]

    walk(tiles, query_side, key_side, work)
    tokens = dq_home.shape[1]
    parts = tokens // BLOCK
    for head in range(heads):
        for slot in range(slots):
            place = head * slots + slot
            total = dquery[place].T * scaling
            if slot == 0:
                dq_home[head] = total
            elif slot < CORES:
                core_out[pl.ds((first + head) * 3 * tokens, tokens), :] = total.astype(jnp.bfloat16)
            else:
                dq_out[slot - CORES][pl.ds(head * tokens, tokens), :] = total.astype(jnp.bfloat16)
            for part in range(parts):
                span = pl.ds(part * BLOCK, BLOCK)
                dkey = dkeys[place * parts + part] * scaling
                dvalue = dvalues[place * parts + part]
                if slot == 0:
                    dkv_home[head, 0, span, :] = dkey
                    dkv_home[head, 1, span, :] = dvalue
                    continue
                if slot < CORES:
                    ref, start = core_out, ((first + head) * 3 + 1) * tokens + part * BLOCK
                else:
                    ref, start = dkv_out[slot - CORES], head * 2 * tokens + part * BLOCK
                ref[pl.ds(start, BLOCK), :] = dkey.astype(jnp.bfloat16)
                ref[pl.ds(start + tokens, BLOCK), :] = dvalue.astype(jnp.bfloat16)
    if groups > 1:
        _, at_query, _ = coordinates(side)
        terms = sink_terms(stat_groups, slots, side, sink_ref, at_query)
        terms_out = rest[3 + 2 * remote]
        terms_out[...] = jnp.broadcast_to(terms, terms_out.shape)
        for ref in (core_out, *dkv_out):
            put_terms(ref, terms)


def grads(tiles, sink, qd, kv, partials, before, first, heads, scaling):
    slots, tokens = len(qd), qd[0].shape[2]
    side, groups = len(partials[0]), len(partials)
    extra = EXTRA if groups > 1 else 0
    remote = slots - CORES
    blocks = heads * slots * (tokens // BLOCK)
    low, high = jnp.bfloat16, jnp.float32
    befores = [] if before is None else [before]
    operands = qd + kv + [each for group in partials for each in group] + befores
    shapes = [
        ((heads, tokens, BLOCK), high),
        ((heads, 2, tokens, BLOCK), high),
        (((first + heads) * 3 * tokens + extra, BLOCK), low),
    ]
    shapes += [((heads * tokens, BLOCK), low)] * remote
    shapes += [((heads * 2 * tokens + extra, BLOCK), low)] * remote
    shapes += [((8, BLOCK), high)] * (groups > 1)
    return pl.pallas_call(
        lambda *refs: grads_kernel(first, heads, slots, side, scaling, groups, *refs),
        in_specs=[pl.BlockSpec(memory_space=pltpu.SMEM)] * 2 + whole(len(operands)),
        out_specs=whole(len(shapes)),
        out_shape=[jax.ShapeDtypeStruct(shape, kind) for shape, kind in shapes],
        scratch_shapes=tile_scratch(heads, slots, tokens)
        + [pltpu.VMEM((blocks, BLOCK, BLOCK), high)] * 2
        + [pltpu.VMEM((heads * slots, BLOCK, tokens), high)],
        compiler_params=pltpu.CompilerParams(vmem_limit_bytes=VMEM_BYTES),
        cost_estimate=pl.CostEstimate(
            flops=heads * 4 * 10**9, bytes_accessed=1, transcendentals=0
        ),
        name="gradients",
    )(tiles, sink, *operands)


def gate(arrays, after):
    count = len(arrays)
    return pl.pallas_call(
        lambda *refs: None,
        in_specs=[pl.BlockSpec(memory_space=pl.ANY)] * (count + len(after)),
        out_specs=[pl.BlockSpec(memory_space=pl.ANY)] * count,
        out_shape=[jax.ShapeDtypeStruct(each.shape, each.dtype) for each in arrays],
        input_output_aliases={place: place for place in range(count)},
        compiler_params=pltpu.CompilerParams(vmem_limit_bytes=FEW_BYTES),
        cost_estimate=SMALL,
        name="gate",
    )(*arrays, *after)


def close_kernel(sizes, side, half, from_core, *refs):
    per = 2 + 4 * (side - 1)
    outs = refs[per * len(sizes) :]
    core = lax.axis_index("ctx") % CORES
    first = 0
    for chunk, heads in enumerate(sizes):
        dq_home, dkv_home, *far = refs[per * chunk : per * (chunk + 1)]
        dq_far, dkv_far = far[: 2 * (side - 1)], far[2 * (side - 1) :]
        tokens = dq_home.shape[1]
        for head in range(heads):
            mine = pl.ds(pl.multiple_of(core * half + first, BLOCK), BLOCK)
            other = pl.ds(pl.multiple_of((1 - core) * half + first, BLOCK), BLOCK)
            for place, out in enumerate(outs):
                if place == 0:
                    parts = [dq_home[head]]
                    parts += [ref[pl.ds(head * tokens, tokens), :] for ref in dq_far]
                else:
                    span = pl.ds((head * 2 + place - 1) * tokens, tokens)
                    parts = [dkv_home[head, place - 1]] + [ref[span, :] for ref in dkv_far]
                parts = [part.astype(jnp.float32) for part in parts]
                span = pl.ds((first // BLOCK * 3 + place) * tokens, tokens)
                start = from_core[span, :].astype(jnp.float32)
                out[0, :, mine] = sum(parts[1::2], parts[0]).astype(jnp.bfloat16)
                out[0, :, other] = sum(parts[2::2], start).astype(jnp.bfloat16)
            first += BLOCK


def close(pieces, from_core, sizes, side, half, tokens):
    flat = [from_core] + [piece for chunk in pieces for piece in chunk]
    return pl.pallas_call(
        lambda *refs: close_kernel(sizes, side, half, *refs),
        in_specs=whole(len(flat)),
        out_specs=whole(3),
        out_shape=[jax.ShapeDtypeStruct((1, tokens, 2 * half), jnp.bfloat16)] * 3,
        compiler_params=pltpu.CompilerParams(vmem_limit_bytes=VMEM_BYTES),
        cost_estimate=SMALL,
        name="closing_sums",
    )(*flat)


def halved(value, by):
    if by & (by - 1) == 0:
        return value >> (by.bit_length() - 1), value & (by - 1)
    return lax.div(value, jnp.int32(by)), lax.rem(value, jnp.int32(by))


def lists_kernel(spans, half_heads, side, per_group, listed, groups, *refs):
    asked, outs, spots = refs[: 2 * side], refs[2 * side : -1], refs[-1]
    slots = side * CORES
    rest, core = halved(lax.axis_index("ctx"), CORES)
    row, col = halved(rest, side)

    def one_owner(owner, carry):
        rest, its_core = halved(owner, CORES)
        its_row, its_col = halved(rest, side)
        across = jnp.where(core == 0, its_col == col, its_row == row)
        along = jnp.where(core == 0, its_row - row, its_col - col)
        shift = jnp.where(along < 0, along + side, along)
        spot = (shift * CORES + jnp.where(its_core == core, 0, 1)) * per_group
        for part in range(per_group):
            spots[owner * per_group + part] = jnp.where(across, spot + part, -1)
        return carry

    lax.fori_loop(0, groups, one_owner, 0)
    for (first, heads), out in zip(spans, outs):

        def one_head(head, count, first=first, out=out):
            for slot in range(slots):
                query = head * slots + slot
                base = head * (slots * per_group)
                code = query
                for part in range(per_group // 2 if slot < CORES else 0):
                    left = base + slot * per_group + 2 * part
                    out[count] = query + (left << 8) + ((left + 2) << 16)
                    count = count + 1
                held = jnp.int32(0)
                blocks = asked[slot]
                for entry in range(listed):
                    spot = spots[blocks[core * half_heads + first + head, 0, entry]]
                    here = (spot >= 0).astype(jnp.int32)
                    place = base + spot
                    longer = jnp.where(held == 0, query + (place << 8), code + ((place + 1) << 16))
                    code = jnp.where(spot >= 0, longer, code)
                    out[count] = code
                    count = count + (here & held)
                    held = held ^ here
                count = count + held
            return count

        out[0] = lax.fori_loop(0, heads, one_head, jnp.int32(1)) - 1


def tile_lists(asked, spans, half_heads, side, per_group, groups):
    slots, listed = len(asked), asked[0].shape[2]
    assert half_heads * slots * per_group < 255
    most = slots * ((listed + 1) // 2) + CORES * (per_group // 2)
    return pl.pallas_call(
        lambda *refs: lists_kernel(spans, half_heads, side, per_group, listed, groups, *refs),
        in_specs=[pl.BlockSpec(memory_space=pltpu.SMEM)] * slots,
        out_specs=[pl.BlockSpec(memory_space=pltpu.SMEM)] * len(spans),
        out_shape=[jax.ShapeDtypeStruct((heads * most + 8,), jnp.int32) for _, heads in spans],
        scratch_shapes=[pltpu.SMEM((groups * per_group,), jnp.int32)],
        compiler_params=pltpu.CompilerParams(vmem_limit_bytes=FEW_BYTES),
        cost_estimate=SMALL,
        name="tile_lists",
    )(*asked)


def sink_kernel(half_heads, side, terms_ref, core_ref, *refs):
    *far, out = refs
    core, at_query, at_key = coordinates(side)
    mine = [terms_ref[0:1, :]] + [get_terms(ref) for ref in far[0::CORES]]
    other = [get_terms(core_ref)] + [get_terms(ref) for ref in far[1::CORES]]
    mine = sum(ordered(mine, at_key, side))
    other = sum(ordered(other, at_query, side))
    lane = lax.broadcasted_iota(jnp.int32, (1, BLOCK), 1)
    low = jnp.where(core == 0, mine, other)
    high = pltpu.roll(jnp.where(core == 0, other, mine), half_heads, 1)
    terms = jnp.where(lane < half_heads, low, high)
    row = lax.broadcasted_iota(jnp.int32, out.shape, 0)
    out[...] = jnp.where(row == lax.axis_index("dp"), terms, 0.0)


def sink_sum(terms, from_core, far, half_heads, side):
    arrays = [from_core, *far]
    last = [
        pl.BlockSpec((EXTRA, BLOCK), lambda i, end=array.shape[0] // EXTRA - 1: (end, 0))
        for array in arrays
    ]
    shape = (lax.axis_size("dp"), BLOCK)
    return pl.pallas_call(
        lambda *refs: sink_kernel(half_heads, side, *refs),
        grid=(1,),
        in_specs=[pl.BlockSpec((8, BLOCK), lambda i: (0, 0))] + last,
        out_specs=pl.BlockSpec(shape, lambda i: (0, 0)),
        out_shape=jax.ShapeDtypeStruct(shape, jnp.float32),
        compiler_params=pltpu.CompilerParams(vmem_limit_bytes=FEW_BYTES),
        cost_estimate=SMALL,
        name="sink_sum",
    )(terms, *arrays)


def sink_rounds():
    copies = lax.axis_size("dp")
    assert copies & (copies - 1) == 0
    rounds, step = [], 1
    while step < copies:
        radix = 4 if copies % (4 * step) == 0 else 2
        perms = [
            [(i, (i + part * step) % copies) for i in range(copies)] for part in range(1, radix)
        ]
        rounds.append(("dp", perms))
        step *= radix
    return rounds


def sink_round(held, axis, perms):
    return sum([lax.ppermute(held, axis, perm) for perm in perms], held)


def body(query_in, key_in, value_in, grad_out, key_blocks, sink_logits):
    groups = lax.axis_size("ctx")
    side = grid_side(groups)
    slots = side * CORES
    head_count = sink_logits.shape[0]
    tokens = query_in.shape[1]
    per_group = tokens // BLOCK
    assert key_blocks.shape[1] == 1 and query_in.shape[2] == head_count * BLOCK
    assert per_group % 2 == 0 and head_count % CORES == 0
    half_heads = head_count // 2
    half = half_heads * BLOCK
    scaling = 1.0 / math.sqrt(BLOCK)
    sizes = chunk_sizes(half_heads)
    starts = [sum(sizes[:i]) for i in range(len(sizes))]
    core = lax.axis_index("ctx") % CORES
    swap = gather_perm(groups, side, True, 0, 1)
    places = [(shift, cross) for shift in range(1, side) for cross in range(CORES)]
    remote = len(places)
    sink = jnp.where(core == 0, sink_logits[:half_heads], sink_logits[half_heads:])

    from_core = lax.ppermute(key_blocks, "ctx", swap)
    pair = jnp.concatenate([key_blocks, from_core], axis=1)
    asked = [key_blocks, from_core]
    for shift in range(1, side):
        came = lax.ppermute(pair, "ctx", gather_perm(groups, side, True, shift, 0))
        asked += [came[:, cross : cross + 1] for cross in range(CORES)]
    spans = list(zip(starts, sizes))
    tiles = tile_lists(asked, spans, half_heads, side, per_group, groups)

    fields = (query_in, grad_out, key_in, value_in)
    qds, kvs = [], []
    for first, heads in zip(starts, sizes):
        last = first + heads == half_heads
        packed = pack(fields, first, heads, half_heads if last else 0, half)
        if not last:
            fields, packed, pair = lax.optimization_barrier((fields, packed, pair))
        qd_own, kv_own, qd_oth, kv_oth = packed[:4]
        if last:
            from_core = lax.ppermute(packed[4], "ctx", swap)
            tiles, packed = lax.optimization_barrier((tiles, packed))
            qd_own, kv_own, qd_oth, kv_oth = packed[:4]
        qd, kv = [qd_own], [kv_own]
        for shift, cross in places:
            perm = gather_perm(groups, side, True, shift, cross)
            qd.append(lax.ppermute(qd_oth if cross else qd_own, "ctx", perm))
            perm = gather_perm(groups, side, False, shift, cross)
            kv.append(lax.ppermute(kv_oth if cross else kv_own, "ctx", perm))
        qds.append(qd)
        kvs.append(kv)
    for qd, kv in zip(qds, kvs):
        qd.insert(1, from_core)
        kv.insert(1, from_core)

    partials = []
    for chunk, (first, heads) in enumerate(spans):
        partial = stats(tiles[chunk], sink, qds[chunk], kvs[chunk], first, heads, scaling)
        came = [
            lax.ppermute(partial, "ctx", gather_perm(groups, side, True, shift, 0))
            for shift in range(1, side)
        ]
        partials.append([partial] + came)
    pieces, core_out = [], None
    for chunk, (first, heads) in enumerate(spans):
        last = chunk == len(spans) - 1
        results = grads(
            tiles[chunk],
            sink,
            qds[chunk],
            kvs[chunk],
            partials if last else partials[chunk : chunk + 1],
            core_out,
            first,
            heads,
            scaling,
        )
        core_out = results[2]
        if pieces:
            results = results[:2] + gate(results[2 : 3 + 2 * remote], pieces[-1][2:]) + results[-1:]
            core_out = results[2]
        dq_out, dkv_out = results[3 : 3 + remote], results[3 + remote : 3 + 2 * remote]
        back = [
            lax.ppermute(value, "ctx", return_perm(groups, side, along_query, shift, cross))
            for along_query, values in ((True, dq_out), (False, dkv_out))
            for value, (shift, cross) in zip(values, places)
        ]
        pieces.append(list(results[:2]) + back)
    from_core = lax.ppermute(core_out, "ctx", swap)
    held = sink_sum(results[-1], from_core, pieces[-1][2 + remote :], half_heads, side)
    for each in sink_rounds():
        held = sink_round(held, *each)
    grad_sink = jnp.sum(held, axis=0)[:head_count]
    grad_query, grad_key, grad_value = close(pieces, from_core, sizes, side, half, tokens)
    return (grad_query, grad_key, grad_value, grad_sink)


def solution(mesh):
    tokens = P("dp", "ctx", None)
    return jax.shard_map(
        body,
        mesh=mesh,
        in_specs=(tokens, tokens, tokens, tokens, P(None, "ctx", None), P()),
        out_specs=(tokens, tokens, tokens, P()),
        check_vma=False,
    )
```

time: 311 us -> 96.7 us (0.31)
  blocking collectives: 86.7 us -> 0 us
  local copies, waits for them, and re-layouts: 86.5 us -> 8.02 us
  matrix products: 44.9 us -> 0 us
  Pallas kernels: 0 us -> 29.9 us
  waiting for transfers between devices: 51.6 us -> 29.7 us
  other arithmetic: 23.1 us -> 1.35 us
  starting transfers between devices: 14.8 us -> 26.6 us
    psum x1 -> x0, blocking collectives: 86.7 us -> none  [body(): grad_sink = lax.psum(sink_parts.reshape(head_count), ('dp', 'ctx'))]
    all_to_all x3 -> x0, waiting for transfers between devices: 51.6 us -> none  [the longest x1 49.4 us: body(): lax.all_to_all(payload, 'ctx', split_axis=0, concat_axis=0, tiled=True)]
    dot_general x36 -> x0, matrix products: 44.9 us -> none  [the longest x5 7.88 us: backward_group(): jnp.einsum('gsqk,gsqd->gskd', dscores, query_grp, preferred_element_type=...]
    pallas_call x0 -> x10, Pallas kernels: none -> 29.9 us  [the longest x2 13.1 us: grads(): pl.pallas_call(lambda *refs: grads_kernel(first, heads, slots, side, scal...]
    ppermute x0 -> x25, waiting for transfers between devices: none -> 29.7 us  [the longest x8 15.5 us: body(): lax.ppermute(value, 'ctx', return_perm(groups, side, along_query, shift,...]
    ppermute x0 -> x25, starting transfers between devices: none -> 26.6 us  [the longest x4 7.47 us: body(): kv.append(lax.ppermute(kv_oth if cross else kv_own, 'ctx', perm))]
    squeeze x20 -> x0, local copies, waits for them, and re-layouts: 21.6 us -> none  [body(): lax.map(partial(forward_group, scaling=scaling), (query_pairs, local_pair...]
    gather x3 -> x0, local copies, waits for them, and re-layouts: 19.6 us -> none  [the longest x1 7.59 us: body(): list_rows[source_ids]]
  transfers between devices with their start and end apart: 3 -> 25, of which waited for: 2 -> 10; matrix products, arithmetic and copies ran while one was open for 3% -> 2% of each run, Pallas kernels for 0% -> 29%
where the time goes in v2:
time: 96.7 us; the launch traced here: 96.3 us
  Pallas kernels  29.9 us (31%)
  waiting for transfers between devices  29.7 us (31%)
  starting transfers between devices  26.6 us (28%)
  local copies, waits for them, and re-layouts  8.02 us (8%)
  other arithmetic  1.35 us (1%)
    ppermute x8, waiting for transfers between devices, body(): lax.ppermute(value, 'ctx', return_perm(groups, side, along_query, shift,...  15.5 us
    pallas_call x2, Pallas kernels, grads(): pl.pallas_call(lambda *refs: grads_kernel(first, heads, slots, side, scal...  13.1 us
    ppermute x4, waiting for transfers between devices, body(): qd.append(lax.ppermute(qd_oth if cross else qd_own, 'ctx', perm))  11.2 us
    pallas_call x2, Pallas kernels, stats(): pl.pallas_call(lambda *refs: stats_kernel(first, heads, slots, scaling, *...  9.12 us
    ppermute x4, starting transfers between devices, body(): kv.append(lax.ppermute(kv_oth if cross else kv_own, 'ctx', perm))  7.47 us
    unnamed x17, local copies, waits for them, and re-layouts  7.24 us
    ppermute x8, starting transfers between devices, body(): lax.ppermute(value, 'ctx', return_perm(groups, side, along_query, shift,...  7.05 us
    ppermute x3, starting transfers between devices, sink_round(): return sum([lax.ppermute(held, axis, perm) for perm in perms], held)  4.62 us
  transfers between devices with their start and end apart: 25, of which 10 were waited for; matrix products, arithmetic and copies ran while one was open for 2% of the time, Pallas kernels for 29%

profile of v2, /device:TPU:0, one launch (start us, length us, event | category | flops | bytes accessed | tf_op | source)
XLA Modules:
  0.0 96.3 jit_solution(8868634976185927677)
XLA Ops:
  1.9 1.1 %copy-done = bf16[1,256,1280]{2,1,0:T(8,128)(2,1)S(1)} copy-done((bf16[1,256,1280]{2,1,0:T(8,128)(2,1)S(1)}, bf16[1,256,1280]{2,1,0:T(8,128)(2,1)}, u32[]{:S(2)}) %copy-start) | copy-done | bytes 655384
  2.9 1.1 %copy-done.1 = bf16[1,256,1280]{2,1,0:T(8,128)(2,1)S(1)} copy-done((bf16[1,256,1280]{2,1,0:T(8,128)(2,1)S(1)}, bf16[1,256,1280]{2,1,0:T(8,128)(2,1)}, u32[]{:S(2)}) %copy-start.1) | copy-done | bytes 655384
  4.0 1.1 %copy-done.2 = bf16[1,256,1280]{2,1,0:T(8,128)(2,1)S(1)} copy-done((bf16[1,256,1280]{2,1,0:T(8,128)(2,1)S(1)}, bf16[1,256,1280]{2,1,0:T(8,128)(2,1)}, u32[]{:S(2)}) %copy-start.2) | copy-done | bytes 655384
  5.1 1.1 %copy-done.3 = bf16[1,256,1280]{2,1,0:T(8,128)(2,1)S(1)} copy-done((bf16[1,256,1280]{2,1,0:T(8,128)(2,1)S(1)}, bf16[1,256,1280]{2,1,0:T(8,128)(2,1)}, u32[]{:S(2)}) %copy-start.3) | copy-done | bytes 655384
  6.2 1.4 %pack.2 = (bf16[3,2,256,128]{3,2,1,0:T(8,128)(2,1)S(1)}, bf16[3,2,256,128]{3,2,1,0:T(8,128)(2,1)S(1)}, bf16[3,2,256,128]{3,2,1,0:T(8,128)(2,1)}, bf16[3,2,256,128]{3,2,1,0:T(8,128)(2,1)}) custom-call(bf16[1,256,1280]{2,1,0:T(8,128)(2,1)S(1)} %copy-done, bf16[1,256,1280]{2,1,0:T(8,128)(2,1)S(1)} %copy-done.1, bf16[1,256,1280]{2,1,0:T(8,128)(2,1)S(1)} %copy-done.2, ...), custom_call_target="tpu_custom_call" | custom-call | flops 1 | bytes 1 | tf_op jit(solution)/shard_map/pack/pallas_call | solution.py:88
  7.7 1.9 %pack.3 = (bf16[2,2,256,128]{3,2,1,0:T(8,128)(2,1)S(1)}, bf16[2,2,256,128]{3,2,1,0:T(8,128)(2,1)S(1)}, bf16[2,2,256,128]{3,2,1,0:T(8,128)(2,1)S(1)}, bf16[2,2,25...) custom-call(bf16[1,256,1280]{2,1,0:T(8,128)(2,1)S(1)} %copy-done, bf16[1,256,1280]{2,1,0:T(8,128)(2,1)S(1)} %copy-done.1, ...), custom_call_target="tpu_custom_call" | custom-call | flops 1 | bytes 1 | tf_op jit(solution)/shard_map/pack/pallas_call | solution.py:88
  11.8 2.9 %collective-permute-start.1 = (s32[10,2,6]{2,1,0:T(2,128)S(1)}, s32[10,2,6]{2,1,0:T(2,128)}, u32[]{:S(2)}, u32[]{:S(2)}) collective-permute-start(s32[10,2,6]{2,1,0:T(2,128)S(1)} %pad_add_fusion), channel_id=1, source_target_pairs={{2,0},{5,1},{0,2},{7,3},{6,4},{1,5},{4,6},{3,7},{10,8},{13,9},{8,1... | collective-permute-start | bytes 1448 | tf_op jit(solution)/shard_map/ppermute | solution.py:587
  14.7 1.7 %collective-permute-start.10 = (bf16[3,2,256,128]{3,2,1,0:T(8,128)(2,1)}, bf16[3,2,256,128]{3,2,1,0:T(8,128)(2,1)S(1)}, u32[]{:S(2)}, u32[]{:S(2)}) collective-permute-start(bf16[3,2,256,128]{3,2,1,0:T(8,128)(2,1)} %get-tuple-element.76), channel_id=1, source_target_pairs={{5,0},{2,1},{7,2},{0,3},{1,4},{6,5},{3,6},{4,7},{13,8},{10,9},{15,... | collective-permute-start | bytes 1179656 | tf_op jit(solution)/shard_map/ppermute | solution.py:609
  16.5 2.0 %collective-permute-start.9 = (bf16[3,2,256,128]{3,2,1,0:T(8,128)(2,1)S(1)}, bf16[3,2,256,128]{3,2,1,0:T(8,128)(2,1)}, u32[]{:S(2)}, u32[]{:S(2)}) collective-permute-start(bf16[3,2,256,128]{3,2,1,0:T(8,128)(2,1)S(1)} %get-tuple-element.75.refs_6_), channel_id=1, source_target_pairs={{4,0},{3,1},{6,2},{1,3},{0,4},{7,5},{2,6},{5,7},{12,8},{11,9},{14,... | collective-permute-start | bytes 1179656 | tf_op jit(solution)/shard_map/ppermute | solution.py:609
  19.3 2.5 %tile_lists.1 = (s32[50]{0:T(128)S(1)}, s32[36]{0:T(128)S(1)}) custom-call(s32[10,1,6]{2,1,0:T(1,128)S(1)} %copy.17.refs_0_, s32[10,1,6]{2,1,0:T(1,128)S(1)} %collective-permute-done.refs_1_, s32[10,1,6]{2,1,0:T(1,128)S(1)} %get-tuple-element.101.refs_2_, s32[10,1,6]{2,1,0:T(1,128)S(1)} %get-tuple-element.100.refs_3_), custom_call_target="tpu_custom_call" | custom-call | flops 1 | bytes 1 | tf_op jit(solution)/shard_map/tile_lists/pallas_call | solution.py:499
  21.8 4.2 %collective-permute-done.8.refs_5_ = bf16[3,2,256,128]{3,2,1,0:T(8,128)(2,1)S(1)} collective-permute-done((bf16[3,2,256,128]{3,2,1,0:T(8,128)(2,1)}, bf16[3,2,256,128]{3,2,1,0:T(8,128)(2,1)S(1)}, u32[]{:S(2)}, u32[]{:S(2)}) %collective-permute-start.8) | collective-permute-done | bytes 393248 | tf_op jit(solution)/shard_map/ppermute | solution.py:607
  26.3 2.2 %collective-permute-start.6 = (bf16[2,2,256,128]{3,2,1,0:T(8,128)(2,1)}, bf16[2,2,256,128]{3,2,1,0:T(8,128)(2,1)S(1)}, u32[]{:S(2)}, u32[]{:S(2)}) collective-permute-start(bf16[2,2,256,128]{3,2,1,0:T(8,128)(2,1)} %copy-done.6), channel_id=1, source_target_pairs={{5,0},{2,1},{7,2},{0,3},{1,4},{6,5},{3,6},{4,7},{13,8},{10,9},{15,... | collective-permute-start | bytes 786440 | tf_op jit(solution)/shard_map/ppermute | solution.py:609
  28.5 6.5 %collective-permute-done.7.refs_4_ = bf16[3,2,256,128]{3,2,1,0:T(8,128)(2,1)S(1)} collective-permute-done((bf16[3,2,256,128]{3,2,1,0:T(8,128)(2,1)S(1)}, bf16[3,2,256,128]{3,2,1,0:T(8,128)(2,1)S(1)}, u32[]{:S(2)}, u32[]{:S(2)}) %collective-permute-start.7) | collective-permute-done | bytes 393248 | tf_op jit(solution)/shard_map/ppermute | solution.py:607
  35.1 2.1 %collective-permute-start.3 = (bf16[2,2,256,128]{3,2,1,0:T(8,128)(2,1)S(1)}, bf16[2,2,256,128]{3,2,1,0:T(8,128)(2,1)S(1)}, u32[]{:S(2)}, u32[]{:S(2)}) collective-permute-start(bf16[2,2,256,128]{3,2,1,0:T(8,128)(2,1)S(1)} %get-tuple-element.68.refs_2_), channel_id=1, source_target_pairs={{2,0},{5,1},{0,2},{7,3},{6,4},{1,5},{4,6},{3,7},{10,8},{13,9},{8,1... | collective-permute-start | bytes 786440 | tf_op jit(solution)/shard_map/ppermute | solution.py:607
  37.1 1.5 %collective-permute-start.5 = (bf16[2,2,256,128]{3,2,1,0:T(8,128)(2,1)}, bf16[2,2,256,128]{3,2,1,0:T(8,128)(2,1)S(1)}, u32[]{:S(2)}, u32[]{:S(2)}) collective-permute-start(bf16[2,2,256,128]{3,2,1,0:T(8,128)(2,1)} %copy-done.4), channel_id=1, source_target_pairs={{4,0},{3,1},{6,2},{1,3},{0,4},{7,5},{2,6},{5,7},{12,8},{11,9},{14,... | collective-permute-start | bytes 786440 | tf_op jit(solution)/shard_map/ppermute | solution.py:609
  39.5 5.6 %row_stats.2.refs_10_ = f32[3,16,256]{2,1,0:T(8,128)S(1)} custom-call(s32[50]{0:T(128)S(1)} %get-tuple-element.72.refs_0_, f32[5]{0:T(128)S(1)} %broadcast_select_fusion.refs_1_, bf16[3,2,256,128]{3,2,1,0:T(8,128)(2,1)S(1)} %get-tuple-element.73.refs_2_, bf16[5,4,256,128]{3,2,1,0:T(8,128)(2,1)S(1)} %collective-permute-done.2.refs_3_.refs_7_, ...), custom_call_target="tpu_custom_call" | custom-call | flops 1 | bytes 1 | tf_op jit(solution)/shard_map/row_stats/pallas_call | solution.py:191
  46.0 3.6 %row_stats.3.refs_12_ = f32[2,16,256]{2,1,0:T(8,128)S(1)} custom-call(s32[36]{0:T(128)S(1)} %get-tuple-element.67.refs_0_, f32[5]{0:T(128)S(1)} %broadcast_select_fusion.refs_1_, bf16[2,2,256,128]{3,2,1,0:T(8,128)(2,1)S(1)} %get-tuple-element.68.refs_2_, bf16[5,4,256,128]{3,2,1,0:T(8,128)(2,1)S(1)} %collective-permute-done.2.refs_3_.refs_7_, ...), custom_call_target="tpu_custom_call" | custom-call | flops 1 | bytes 1 | tf_op jit(solution)/shard_map/row_stats/pallas_call | solution.py:191
  49.6 1.4 %collective-permute-start.12 = (f32[2,16,256]{2,1,0:T(8,128)S(1)}, f32[2,16,256]{2,1,0:T(8,128)S(1)}, u32[]{:S(2)}, u32[]{:S(2)}) collective-permute-start(f32[2,16,256]{2,1,0:T(8,128)S(1)} %row_stats.3.refs_12_), channel_id=1, source_target_pairs={{2,0},{5,1},{0,2},{7,3},{6,4},{1,5},{4,6},{3,7},{10,8},{13,9},{8,1... | collective-permute-start | bytes 98312 | tf_op jit(solution)/shard_map/ppermute | solution.py:620
  50.9 7.8 %gradients.2 = (f32[3,256,128]{2,1,0:T(8,128)S(1)}, f32[3,2,256,128]{3,2,1,0:T(8,128)S(1)}, bf16[2304,128]{1,0:T(8,128)(2,1)S(1)}, bf16[768,128]{1,0:T(8,128)(2,...) custom-call(s32[50]{0:T(128)S(1)} %get-tuple-element.72.refs_0_, ...), custom_call_target="tpu_custom_call" | custom-call | flops 12000000000 | bytes 1 | tf_op jit(solution)/shard_map/gradients/pallas_call | solution.py:373
  60.1 1.1 %collective-permute-start.15 = (bf16[1536,128]{1,0:T(8,128)(2,1)S(1)}, bf16[1536,128]{1,0:T(8,128)(2,1)S(1)}, u32[]{:S(2)}, u32[]{:S(2)}) collective-permute-start(bf16[1536,128]{1,0:T(8,128)(2,1)S(1)} %get-tuple-element.85), channel_id=1, source_target_pairs={{0,4},{1,3},{2,6},{3,1},{4,0},{5,7},{6,2},{7,5},{8,12},{9,11},{10,... | collective-permute-start | bytes 1179656 | tf_op jit(solution)/shard_map/ppermute | solution.py:644
  61.1 1.2 %collective-permute-start.16 = (bf16[1536,128]{1,0:T(8,128)(2,1)S(1)}, bf16[1536,128]{1,0:T(8,128)(2,1)S(1)}, u32[]{:S(2)}, u32[]{:S(2)}) collective-permute-start(bf16[1536,128]{1,0:T(8,128)(2,1)S(1)} %get-tuple-element.86), channel_id=1, source_target_pairs={{0,5},{1,2},{2,7},{3,0},{4,1},{5,6},{6,3},{7,4},{8,13},{9,10},{10,... | collective-permute-start | bytes 1179656 | tf_op jit(solution)/shard_map/ppermute | solution.py:644
  62.4 5.3 %gradients.3 = (f32[2,256,128]{2,1,0:T(8,128)S(1)}, f32[2,2,256,128]{3,2,1,0:T(8,128)S(1)}, bf16[3856,128]{1,0:T(8,128)(2,1)S(1)}, bf16[512,128]{1,0:T(8,128)(2,...) custom-call(s32[36]{0:T(128)S(1)} %get-tuple-element.67.refs_0_, ...), custom_call_target="tpu_custom_call" | custom-call | flops 8000000000 | bytes 1 | tf_op jit(solution)/shard_map/gradients/pallas_call | solution.py:373
  67.7 1.4 %collective-permute-done.15.refs_7_.refs_5_ = bf16[1536,128]{1,0:T(8,128)(2,1)S(1)} collective-permute-done((bf16[1536,128]{1,0:T(8,128)(2,1)S(1)}, bf16[1536,128]{1,0:T(8,128)(2,1)S(1)}, u32[]{:S(2)}, u32[]{:S(2)}) %collective-permute-start.15) | collective-permute-done | bytes 393248 | tf_op jit(solution)/shard_map/ppermute | solution.py:644
  69.1 5.9 %collective-permute-done.16.refs_8_.refs_6_ = bf16[1536,128]{1,0:T(8,128)(2,1)S(1)} collective-permute-done((bf16[1536,128]{1,0:T(8,128)(2,1)S(1)}, bf16[1536,128]{1,0:T(8,128)(2,1)S(1)}, u32[]{:S(2)}, u32[]{:S(2)}) %collective-permute-start.16) | collective-permute-done | bytes 393248 | tf_op jit(solution)/shard_map/ppermute | solution.py:644
  75.1 1.0 collective-permute-start.20
  76.0 1.1 %collective-permute-start.21 = (bf16[1040,128]{1,0:T(8,128)(2,1)S(1)}, bf16[1040,128]{1,0:T(8,128)(2,1)S(1)}, u32[]{:S(2)}, u32[]{:S(2)}) collective-permute-start(bf16[1040,128]{1,0:T(8,128)(2,1)S(1)} %get-tuple-element.95), channel_id=1, source_target_pairs={{0,5},{1,2},{2,7},{3,0},{4,1},{5,6},{6,3},{7,4},{8,13},{9,10},{10,... | collective-permute-start | bytes 798728 | tf_op jit(solution)/shard_map/ppermute | solution.py:644
  78.6 4.3 %collective-permute-done.20.refs_11_.refs_2_ = bf16[1040,128]{1,0:T(8,128)(2,1)S(1)} collective-permute-done((bf16[1040,128]{1,0:T(8,128)(2,1)S(1)}, bf16[1040,128]{1,0:T(8,128)(2,1)S(1)}, u32[]{:S(2)}, u32[]{:S(2)}) %collective-permute-start.20) | collective-permute-done | bytes 266272 | tf_op jit(solution)/shard_map/ppermute | solution.py:644
  82.9 3.8 %collective-permute-done.21.refs_12_.refs_3_ = bf16[1040,128]{1,0:T(8,128)(2,1)S(1)} collective-permute-done((bf16[1040,128]{1,0:T(8,128)(2,1)S(1)}, bf16[1040,128]{1,0:T(8,128)(2,1)S(1)}, u32[]{:S(2)}, u32[]{:S(2)}) %collective-permute-start.21) | collective-permute-done | bytes 266272 | tf_op jit(solution)/shard_map/ppermute | solution.py:644
  86.8 3.6 %collective-permute-start.24 = (f32[4,128]{1,0:T(4,128)S(1)}, f32[4,128]{1,0:T(4,128)S(1)}, u32[]{:S(2)}, u32[]{:S(2)}) collective-permute-start(f32[4,128]{1,0:T(4,128)S(1)} %sink_sum.1), channel_id=1, source_target_pairs={{0,24},{8,0},{16,8},{24,16},{1,25},{9,1},{17,9},{25,17},{2,26},{10... | collective-permute-start | bytes 6152 | tf_op jit(solution)/shard_map/ppermute | solution.py:560
  90.4 1.0 %collective-permute-start.22 = (f32[4,128]{1,0:T(4,128)S(1)}, f32[4,128]{1,0:T(4,128)S(1)}, u32[]{:S(2)}, u32[]{:S(2)}) collective-permute-start(f32[4,128]{1,0:T(4,128)S(1)} %sink_sum.1), channel_id=1, source_target_pairs={{0,8},{8,16},{16,24},{24,0},{1,9},{9,17},{17,25},{25,1},{2,10},{10... | collective-permute-start | bytes 6152 | tf_op jit(solution)/shard_map/ppermute | solution.py:560
  91.4 1.8 %closing_sums.1 = (bf16[1,256,1280]{2,1,0:T(8,128)(2,1)}, bf16[1,256,1280]{2,1,0:T(8,128)(2,1)}, bf16[1,256,1280]{2,1,0:T(8,128)(2,1)}) custom-call(bf16[3856,128]{1,0:T(8,128)(2,1)S(1)} %collective-permute-done.17.refs_0_.refs_1_, f32[3,256,128]{2,1,0:T(8,128)S(1)} %get-tuple-element.88.refs_1_, f32[3,2,256,128]{3,2,1,0:T(8,128)S(1)} %get-tuple-element.89.refs_2_, ...), custom_call_target="tpu_custom_call" | custom-call | flops 1 | bytes 1 | tf_op jit(solution)/shard_map/closing_sums/pallas_call | solution.py:432
  93.2 1.7 %collective-permute-done.23 = f32[4,128]{1,0:T(4,128)S(1)} collective-permute-done((f32[4,128]{1,0:T(4,128)S(1)}, f32[4,128]{1,0:T(4,128)S(1)}, u32[]{:S(2)}, u32[]{:S(2)}) %collective-permute-start.23) | collective-permute-done | bytes 2080 | tf_op jit(solution)/shard_map/ppermute | solution.py:560
  (49 shorter events, 10.6 us)
Async XLA Ops:
  1.4 6.2 %collective-permute-start = (s32[10,1,6]{2,1,0:T(1,128)S(1)}, s32[10,1,6]{2,1,0:T(1,128)S(1)}, u32[]{:S(2)}, u32[]{:S(2)}) collective-permute-start(s32[10,1,6]{2,1,0:T(1,128)S(1)} %copy.17.refs_0_), channel_id=1, source_target_pairs={{1,0},{0,1},{3,2},{2,3},{5,4},{4,5},{7,6},{6,7},{9,8},{8,9},{11,10... | collective-permute-start | bytes 728 | tf_op jit(solution)/shard_map/ppermute | solution.py:583
  1.9 1.1 %copy-start = (bf16[1,256,1280]{2,1,0:T(8,128)(2,1)S(1)}, bf16[1,256,1280]{2,1,0:T(8,128)(2,1)}, u32[]{:S(2)}) copy-start(bf16[1,256,1280]{2,1,0:T(8,128)(2,1)} %refs_0_.3) | copy-start | bytes 1966084
  2.9 1.1 %copy-start.1 = (bf16[1,256,1280]{2,1,0:T(8,128)(2,1)S(1)}, bf16[1,256,1280]{2,1,0:T(8,128)(2,1)}, u32[]{:S(2)}) copy-start(bf16[1,256,1280]{2,1,0:T(8,128)(2,1)} %refs_1_.2) | copy-start | bytes 1966084
  4.0 1.1 %copy-start.2 = (bf16[1,256,1280]{2,1,0:T(8,128)(2,1)S(1)}, bf16[1,256,1280]{2,1,0:T(8,128)(2,1)}, u32[]{:S(2)}) copy-start(bf16[1,256,1280]{2,1,0:T(8,128)(2,1)} %refs_2_.2) | copy-start | bytes 1966084
  5.1 1.1 %copy-start.3 = (bf16[1,256,1280]{2,1,0:T(8,128)(2,1)S(1)}, bf16[1,256,1280]{2,1,0:T(8,128)(2,1)}, u32[]{:S(2)}) copy-start(bf16[1,256,1280]{2,1,0:T(8,128)(2,1)} %refs_3_.2) | copy-start | bytes 1966084
  9.6 0.7 copy-start.4
  10.3 0.7 copy-start.6
  11.7 27.8 %collective-permute-start.2 = (bf16[5,4,256,128]{3,2,1,0:T(8,128)(2,1)}, bf16[5,4,256,128]{3,2,1,0:T(8,128)(2,1)S(1)}, u32[]{:S(2)}, u32[]{:S(2)}) collective-permute-start(bf16[5,4,256,128]{3,2,1,0:T(8,128)(2,1)} %get-tuple-element.66), channel_id=1, source_target_pairs={{1,0},{0,1},{3,2},{2,3},{5,4},{4,5},{7,6},{6,7},{9,8},{8,9},{11,10... | collective-permute-start | bytes 3932168 | tf_op jit(solution)/shard_map/ppermute | solution.py:601
  11.8 4.7 %collective-permute-start.1 = (s32[10,2,6]{2,1,0:T(2,128)S(1)}, s32[10,2,6]{2,1,0:T(2,128)}, u32[]{:S(2)}, u32[]{:S(2)}) collective-permute-start(s32[10,2,6]{2,1,0:T(2,128)S(1)} %pad_add_fusion), channel_id=1, source_target_pairs={{2,0},{5,1},{0,2},{7,3},{6,4},{1,5},{4,6},{3,7},{10,8},{13,9},{8,1... | collective-permute-start | bytes 1448 | tf_op jit(solution)/shard_map/ppermute | solution.py:587
  14.7 11.3 %collective-permute-start.8 = (bf16[3,2,256,128]{3,2,1,0:T(8,128)(2,1)}, bf16[3,2,256,128]{3,2,1,0:T(8,128)(2,1)S(1)}, u32[]{:S(2)}, u32[]{:S(2)}) collective-permute-start(bf16[3,2,256,128]{3,2,1,0:T(8,128)(2,1)} %get-tuple-element.74), channel_id=1, source_target_pairs={{3,0},{4,1},{1,2},{6,3},{7,4},{0,5},{5,6},{2,7},{11,8},{12,9},{9,1... | collective-permute-start | bytes 1179656 | tf_op jit(solution)/shard_map/ppermute | solution.py:607
  14.7 11.6 %collective-permute-start.10 = (bf16[3,2,256,128]{3,2,1,0:T(8,128)(2,1)}, bf16[3,2,256,128]{3,2,1,0:T(8,128)(2,1)S(1)}, u32[]{:S(2)}, u32[]{:S(2)}) collective-permute-start(bf16[3,2,256,128]{3,2,1,0:T(8,128)(2,1)} %get-tuple-element.76), channel_id=1, source_target_pairs={{5,0},{2,1},{7,2},{0,3},{1,4},{6,5},{3,6},{4,7},{13,8},{10,9},{15,... | collective-permute-start | bytes 1179656 | tf_op jit(solution)/shard_map/ppermute | solution.py:609
  16.4 18.6 %collective-permute-start.7 = (bf16[3,2,256,128]{3,2,1,0:T(8,128)(2,1)S(1)}, bf16[3,2,256,128]{3,2,1,0:T(8,128)(2,1)S(1)}, u32[]{:S(2)}, u32[]{:S(2)}) collective-permute-start(bf16[3,2,256,128]{3,2,1,0:T(8,128)(2,1)S(1)} %get-tuple-element.73.refs_2_), channel_id=1, source_target_pairs={{2,0},{5,1},{0,2},{7,3},{6,4},{1,5},{4,6},{3,7},{10,8},{13,9},{8,1... | collective-permute-start | bytes 1179656 | tf_op jit(solution)/shard_map/ppermute | solution.py:607
  16.5 20.6 %collective-permute-start.9 = (bf16[3,2,256,128]{3,2,1,0:T(8,128)(2,1)S(1)}, bf16[3,2,256,128]{3,2,1,0:T(8,128)(2,1)}, u32[]{:S(2)}, u32[]{:S(2)}) collective-permute-start(bf16[3,2,256,128]{3,2,1,0:T(8,128)(2,1)S(1)} %get-tuple-element.75.refs_6_), channel_id=1, source_target_pairs={{4,0},{3,1},{6,2},{1,3},{0,4},{7,5},{2,6},{5,7},{12,8},{11,9},{14,... | collective-permute-start | bytes 1179656 | tf_op jit(solution)/shard_map/ppermute | solution.py:609
  26.0 19.6 %collective-permute-start.4 = (bf16[2,2,256,128]{3,2,1,0:T(8,128)(2,1)}, bf16[2,2,256,128]{3,2,1,0:T(8,128)(2,1)S(1)}, u32[]{:S(2)}, u32[]{:S(2)}) collective-permute-start(bf16[2,2,256,128]{3,2,1,0:T(8,128)(2,1)} %copy-done.7), channel_id=1, source_target_pairs={{3,0},{4,1},{1,2},{6,3},{7,4},{0,5},{5,6},{2,7},{11,8},{12,9},{9,1... | collective-permute-start | bytes 786440 | tf_op jit(solution)/shard_map/ppermute | solution.py:607
  26.3 19.2 %collective-permute-start.6 = (bf16[2,2,256,128]{3,2,1,0:T(8,128)(2,1)}, bf16[2,2,256,128]{3,2,1,0:T(8,128)(2,1)S(1)}, u32[]{:S(2)}, u32[]{:S(2)}) collective-permute-start(bf16[2,2,256,128]{3,2,1,0:T(8,128)(2,1)} %copy-done.6), channel_id=1, source_target_pairs={{5,0},{2,1},{7,2},{0,3},{1,4},{6,5},{3,6},{4,7},{13,8},{10,9},{15,... | collective-permute-start | bytes 786440 | tf_op jit(solution)/shard_map/ppermute | solution.py:609
  35.1 10.9 %collective-permute-start.3 = (bf16[2,2,256,128]{3,2,1,0:T(8,128)(2,1)S(1)}, bf16[2,2,256,128]{3,2,1,0:T(8,128)(2,1)S(1)}, u32[]{:S(2)}, u32[]{:S(2)}) collective-permute-start(bf16[2,2,256,128]{3,2,1,0:T(8,128)(2,1)S(1)} %get-tuple-element.68.refs_2_), channel_id=1, source_target_pairs={{2,0},{5,1},{0,2},{7,3},{6,4},{1,5},{4,6},{3,7},{10,8},{13,9},{8,1... | collective-permute-start | bytes 786440 | tf_op jit(solution)/shard_map/ppermute | solution.py:607
  37.1 8.9 %collective-permute-start.5 = (bf16[2,2,256,128]{3,2,1,0:T(8,128)(2,1)}, bf16[2,2,256,128]{3,2,1,0:T(8,128)(2,1)S(1)}, u32[]{:S(2)}, u32[]{:S(2)}) collective-permute-start(bf16[2,2,256,128]{3,2,1,0:T(8,128)(2,1)} %copy-done.4), channel_id=1, source_target_pairs={{4,0},{3,1},{6,2},{1,3},{0,4},{7,5},{2,6},{5,7},{12,8},{11,9},{14,... | collective-permute-start | bytes 786440 | tf_op jit(solution)/shard_map/ppermute | solution.py:609
  39.5 6.6 %copy-start.5 = (bf16[2,2,256,128]{3,2,1,0:T(8,128)(2,1)S(1)}, bf16[2,2,256,128]{3,2,1,0:T(8,128)(2,1)}, u32[]{:S(2)}) copy-start(bf16[2,2,256,128]{3,2,1,0:T(8,128)(2,1)} %copy-done.4) | copy-start | bytes 786436
  45.0 5.9 %collective-permute-start.11 = (f32[3,16,256]{2,1,0:T(8,128)S(1)}, f32[3,16,256]{2,1,0:T(8,128)S(1)}, u32[]{:S(2)}, u32[]{:S(2)}) collective-permute-start(f32[3,16,256]{2,1,0:T(8,128)S(1)} %row_stats.2.refs_10_), channel_id=1, source_target_pairs={{2,0},{5,1},{0,2},{7,3},{6,4},{1,5},{4,6},{3,7},{10,8},{13,9},{8,1... | collective-permute-start | bytes 147464 | tf_op jit(solution)/shard_map/ppermute | solution.py:620
  49.6 12.8 %collective-permute-start.12 = (f32[2,16,256]{2,1,0:T(8,128)S(1)}, f32[2,16,256]{2,1,0:T(8,128)S(1)}, u32[]{:S(2)}, u32[]{:S(2)}) collective-permute-start(f32[2,16,256]{2,1,0:T(8,128)S(1)} %row_stats.3.refs_12_), channel_id=1, source_target_pairs={{2,0},{5,1},{0,2},{7,3},{6,4},{1,5},{4,6},{3,7},{10,8},{13,9},{8,1... | collective-permute-start | bytes 98312 | tf_op jit(solution)/shard_map/ppermute | solution.py:620
  58.8 8.9 %collective-permute-start.13 = (bf16[768,128]{1,0:T(8,128)(2,1)S(1)}, bf16[768,128]{1,0:T(8,128)(2,1)S(1)}, u32[]{:S(2)}, u32[]{:S(2)}) collective-permute-start(bf16[768,128]{1,0:T(8,128)(2,1)S(1)} %get-tuple-element.83), channel_id=1, source_target_pairs={{0,2},{1,5},{2,0},{3,7},{4,6},{5,1},{6,4},{7,3},{8,10},{9,13},{10,... | collective-permute-start | bytes 589832 | tf_op jit(solution)/shard_map/ppermute | solution.py:644
  59.6 8.1 %collective-permute-start.14 = (bf16[768,128]{1,0:T(8,128)(2,1)S(1)}, bf16[768,128]{1,0:T(8,128)(2,1)S(1)}, u32[]{:S(2)}, u32[]{:S(2)}) collective-permute-start(bf16[768,128]{1,0:T(8,128)(2,1)S(1)} %get-tuple-element.84), channel_id=1, source_target_pairs={{0,3},{1,4},{2,1},{3,6},{4,7},{5,0},{6,5},{7,2},{8,11},{9,12},{10,... | collective-permute-start | bytes 589832 | tf_op jit(solution)/shard_map/ppermute | solution.py:644
  60.1 9.1 %collective-permute-start.15 = (bf16[1536,128]{1,0:T(8,128)(2,1)S(1)}, bf16[1536,128]{1,0:T(8,128)(2,1)S(1)}, u32[]{:S(2)}, u32[]{:S(2)}) collective-permute-start(bf16[1536,128]{1,0:T(8,128)(2,1)S(1)} %get-tuple-element.85), channel_id=1, source_target_pairs={{0,4},{1,3},{2,6},{3,1},{4,0},{5,7},{6,2},{7,5},{8,12},{9,11},{10,... | collective-permute-start | bytes 1179656 | tf_op jit(solution)/shard_map/ppermute | solution.py:644
  61.1 13.9 %collective-permute-start.16 = (bf16[1536,128]{1,0:T(8,128)(2,1)S(1)}, bf16[1536,128]{1,0:T(8,128)(2,1)S(1)}, u32[]{:S(2)}, u32[]{:S(2)}) collective-permute-start(bf16[1536,128]{1,0:T(8,128)(2,1)S(1)} %get-tuple-element.86), channel_id=1, source_target_pairs={{0,5},{1,2},{2,7},{3,0},{4,1},{5,6},{6,3},{7,4},{8,13},{9,10},{10,... | collective-permute-start | bytes 1179656 | tf_op jit(solution)/shard_map/ppermute | solution.py:644
  75.1 11.6 %collective-permute-start.17 = (bf16[3856,128]{1,0:T(8,128)(2,1)S(1)}, bf16[3856,128]{1,0:T(8,128)(2,1)S(1)}, u32[]{:S(2)}, u32[]{:S(2)}) collective-permute-start(bf16[3856,128]{1,0:T(8,128)(2,1)S(1)} %get-tuple-element.87), channel_id=1, source_target_pairs={{1,0},{0,1},{3,2},{2,3},{5,4},{4,5},{7,6},{6,7},{9,8},{8,9},{11,10... | collective-permute-start | bytes 2961416 | tf_op jit(solution)/shard_map/ppermute | solution.py:649
  75.1 7.8 %collective-permute-start.20 = (bf16[1040,128]{1,0:T(8,128)(2,1)S(1)}, bf16[1040,128]{1,0:T(8,128)(2,1)S(1)}, u32[]{:S(2)}, u32[]{:S(2)}) collective-permute-start(bf16[1040,128]{1,0:T(8,128)(2,1)S(1)} %get-tuple-element.94), channel_id=1, source_target_pairs={{0,4},{1,3},{2,6},{3,1},{4,0},{5,7},{6,2},{7,5},{8,12},{9,11},{10,... | collective-permute-start | bytes 798728 | tf_op jit(solution)/shard_map/ppermute | solution.py:644
  76.0 10.7 %collective-permute-start.21 = (bf16[1040,128]{1,0:T(8,128)(2,1)S(1)}, bf16[1040,128]{1,0:T(8,128)(2,1)S(1)}, u32[]{:S(2)}, u32[]{:S(2)}) collective-permute-start(bf16[1040,128]{1,0:T(8,128)(2,1)S(1)} %get-tuple-element.95), channel_id=1, source_target_pairs={{0,5},{1,2},{2,7},{3,0},{4,1},{5,6},{6,3},{7,4},{8,13},{9,10},{10,... | collective-permute-start | bytes 798728 | tf_op jit(solution)/shard_map/ppermute | solution.py:644
  77.1 14.3 %collective-permute-start.18 = (bf16[512,128]{1,0:T(8,128)(2,1)S(1)}, bf16[512,128]{1,0:T(8,128)(2,1)S(1)}, u32[]{:S(2)}, u32[]{:S(2)}) collective-permute-start(bf16[512,128]{1,0:T(8,128)(2,1)S(1)} %get-tuple-element.92), channel_id=1, source_target_pairs={{0,2},{1,5},{2,0},{3,7},{4,6},{5,1},{6,4},{7,3},{8,10},{9,13},{10,... | collective-permute-start | bytes 393224 | tf_op jit(solution)/shard_map/ppermute | solution.py:644
  77.9 13.5 %collective-permute-start.19 = (bf16[512,128]{1,0:T(8,128)(2,1)S(1)}, bf16[512,128]{1,0:T(8,128)(2,1)S(1)}, u32[]{:S(2)}, u32[]{:S(2)}) collective-permute-start(bf16[512,128]{1,0:T(8,128)(2,1)S(1)} %get-tuple-element.93), channel_id=1, source_target_pairs={{0,3},{1,4},{2,1},{3,6},{4,7},{5,0},{6,5},{7,2},{8,11},{9,12},{10,... | collective-permute-start | bytes 393224 | tf_op jit(solution)/shard_map/ppermute | solution.py:644
  86.8 6.4 %collective-permute-start.24 = (f32[4,128]{1,0:T(4,128)S(1)}, f32[4,128]{1,0:T(4,128)S(1)}, u32[]{:S(2)}, u32[]{:S(2)}) collective-permute-start(f32[4,128]{1,0:T(4,128)S(1)} %sink_sum.1), channel_id=1, source_target_pairs={{0,24},{8,0},{16,8},{24,16},{1,25},{9,1},{17,9},{25,17},{2,26},{10... | collective-permute-start | bytes 6152 | tf_op jit(solution)/shard_map/ppermute | solution.py:560
  90.4 4.5 %collective-permute-start.23 = (f32[4,128]{1,0:T(4,128)S(1)}, f32[4,128]{1,0:T(4,128)S(1)}, u32[]{:S(2)}, u32[]{:S(2)}) collective-permute-start(f32[4,128]{1,0:T(4,128)S(1)} %sink_sum.1), channel_id=1, source_target_pairs={{0,16},{8,24},{16,0},{24,8},{1,17},{9,25},{17,1},{25,9},{2,18},{10... | collective-permute-start | bytes 6152 | tf_op jit(solution)/shard_map/ppermute | solution.py:560
  90.4 5.4 %collective-permute-start.22 = (f32[4,128]{1,0:T(4,128)S(1)}, f32[4,128]{1,0:T(4,128)S(1)}, u32[]{:S(2)}, u32[]{:S(2)}) collective-permute-start(f32[4,128]{1,0:T(4,128)S(1)} %sink_sum.1), channel_id=1, source_target_pairs={{0,8},{8,16},{16,24},{24,0},{1,9},{9,17},{17,25},{25,1},{2,10},{10... | collective-permute-start | bytes 6152 | tf_op jit(solution)/shard_map/ppermute | solution.py:560
  (1 other events, 0.7 us)

commit v3 on v2

--- a/solution.py
+++ b/solution.py
@@ -12,6 +12,7 @@
 FAR = -1e30
 VMEM_BYTES = 24 * 1024 * 1024
 FEW_BYTES = 2 * 1024 * 1024
+MOST_BYTES = 62 * 1024 * 1024
 UNROLL = 5
 EXTRA = 16
 SMALL = pl.CostEstimate(flops=1, bytes_accessed=1, transcendentals=0)
@@ -21,8 +22,28 @@
 
 
 def chunk_sizes(heads):
+    return (heads - 1, 1) if heads > 1 else (1,)
+
+
+def part_spans(sizes, part_sizes):
+    where = [(chunk, offset) for chunk, size in enumerate(sizes) for offset in range(size)]
+    parts, done = [], 0
+    for count in part_sizes:
+        spans = []
+        for head in range(done, done + count):
+            chunk, offset = where[head]
+            if spans and spans[-1][0] == chunk:
+                spans[-1] = spans[-1][:3] + (spans[-1][3] + 1,)
+            else:
+                spans.append((chunk, offset, head, 1))
+        parts.append(spans)
+        done += count
+    return parts
+
+
+def part_sizes(heads):
     first = (heads + 1) // 2
-    return (first, heads - first) if heads > first else (first,)
+    return [size for size in (first, heads - first) if size]
 
 
 def grid_side(groups):
@@ -57,56 +78,70 @@
     return [pl.BlockSpec(memory_space=pltpu.VMEM)] * count
 
 
-def pack_kernel(first, heads, every, half, q_ref, g_ref, k_ref, v_ref, *rest):
-    qd_own, kv_own, qd_oth, kv_oth = rest[:4]
-    sems = rest[-1]
-    fields = (q_ref, g_ref, k_ref, v_ref)
+def pack_kernel(blocks, half, q_ref, g_ref, k_ref, v_ref, *rest):
+    outs, (held, came, left) = rest[:-3], rest[-3:]
     core = lax.axis_index("ctx") % CORES
-    copies = []
-
-    def copy(ref, which, head, out):
+    arriving, leaving = [], []
+    for count, (which, head, field, _) in enumerate(blocks):
         start = (core if which == 0 else 1 - core) * half + head * BLOCK
         columns = pl.ds(pl.multiple_of(start, BLOCK), BLOCK)
-        copies.append(pltpu.make_async_copy(ref.at[0, :, columns], out, sems.at[len(copies)]))
-
-    for head in range(heads):
-        for which, outs in enumerate(((qd_own, kv_own), (qd_oth, kv_oth))):
-            for place, ref in enumerate(fields):
-                copy(ref, which, first + head, outs[place // 2].at[head, place % 2])
-    for head in range(every):
-        for place, ref in enumerate(fields):
-            copy(ref, 1, head, rest[4].at[head, place])
-    for each in copies:
-        each.start()
-    for each in copies:
-        each.wait()
-
-
-def pack(fields, first, heads, every, half):
+        copy = pltpu.make_async_copy(
+            (q_ref, g_ref, k_ref, v_ref)[field].at[0, :, columns], held.at[count], came.at[count]
+        )
+        copy.start()
+        arriving.append(copy)
+    for count, (copy, (*_, targets)) in enumerate(zip(arriving, blocks)):
+        copy.wait()
+        for out, row, place in targets:
+            leaving.append(
+                pltpu.make_async_copy(
+                    held.at[count], outs[out].at[row, place], left.at[len(leaving)]
+                )
+            )
+            leaving[-1].start()
+    for copy in leaving:
+        copy.wait()
+
+
+def pack(fields, sizes, half):
     tokens = fields[0].shape[1]
-    shapes = [(heads, 2, tokens, BLOCK)] * 4 + [(every, 4, tokens, BLOCK)] * (every > 0)
+    blocks, first = [], 0
+    for chunk, heads in enumerate(sizes):
+        for row in range(heads):
+            for which in range(2):
+                for field in range(4):
+                    targets = [(4 * chunk + 2 * which + field // 2, row, field % 2)]
+                    targets += [(4 * len(sizes), first + row, field)] * which
+                    blocks.append((which, first + row, field, targets))
+        first += heads
+    shapes = [(size, 2, tokens, BLOCK) for size in sizes for _ in range(4)]
+    shapes.append((first, 4, tokens, BLOCK))
     return pl.pallas_call(
-        lambda *refs: pack_kernel(first, heads, every, half, *refs),
-        in_specs=[pl.BlockSpec(memory_space=pltpu.HBM)] * 4,
-        out_specs=whole(len(shapes)),
+        lambda *refs: pack_kernel(blocks, half, *refs),
+        in_specs=[pl.BlockSpec(memory_space=pl.ANY)] * 4,
+        out_specs=[pl.BlockSpec(memory_space=pl.ANY)] * len(shapes),
         out_shape=[jax.ShapeDtypeStruct(shape, jnp.bfloat16) for shape in shapes],
-        scratch_shapes=[pltpu.SemaphoreType.DMA((heads * 8 + every * 4,))],
-        compiler_params=pltpu.CompilerParams(vmem_limit_bytes=VMEM_BYTES),
-        cost_estimate=SMALL,
+        scratch_shapes=[
+            pltpu.VMEM((len(blocks), tokens, BLOCK), jnp.bfloat16),
+            pltpu.SemaphoreType.DMA((len(blocks),)),
+            pltpu.SemaphoreType.DMA((sum(len(block[-1]) for block in blocks),)),
+        ],
+        compiler_params=pltpu.CompilerParams(vmem_limit_bytes=MOST_BYTES),
+        cost_estimate=pl.CostEstimate(flops=4 * 10**9, bytes_accessed=1, transcendentals=0),
         name="pack",
     )(*fields)
 
 
 def spread(spans, slots, refs, query_side, key_side):
     place = 0
-    for span, (first, heads) in enumerate(spans):
+    for span, (_, offset, first, heads) in enumerate(spans):
         here = refs[span * 2 * slots : (span + 1) * 2 * slots]
         qd_refs, kv_refs = here[:slots], here[slots:]
         parts = kv_refs[0].shape[2] // BLOCK
         for head in range(heads):
             for slot in range(slots):
                 from_core = slot == 1
-                row = head + (first if from_core else 0)
+                row = head + (first if from_core else offset)
                 for kind in range(2):
                     lead = kind + (2 if from_core else 0)
                     query_side[kind][place] = qd_refs[slot][row, kind]
@@ -157,7 +192,7 @@
 def stats_kernel(first, heads, slots, scaling, tiles, sink_ref, *refs):
     out_ref, q_all, g_all, k_all, v_all, rows = refs[-6:]
     query_side, key_side = (q_all, g_all), (k_all, v_all)
-    spread([(first, heads)], slots, refs, query_side, key_side)
+    spread([(0, 0, first, heads)], slots, refs, query_side, key_side)
     zero = jnp.zeros((1, out_ref.shape[2]), jnp.float32)
     for head in range(heads):
         for slot in range(slots):
@@ -240,28 +275,6 @@
     return core, jnp.where(core == 0, col, row), jnp.where(core == 0, row, col)
 
 
-def sink_terms(stat_groups, slots, side, sink_ref, at_query):
-    lane = lax.broadcasted_iota(jnp.int32, (1, BLOCK), 1)
-    terms = jnp.zeros((1, BLOCK), jnp.float32)
-    done = 0
-    for stat_refs in stat_groups:
-        for head in range(stat_refs[0].shape[0]):
-            sink = sink_ref[done]
-            chips = []
-            for shift in range(side):
-                total = 0.0
-                for cross in range(CORES):
-                    rows = stat_rows(stat_refs, head, shift * CORES + cross, slots)
-                    kinds = [ordered(kind, at_query, side) for kind in zip(*rows)]
-                    log_norm, row_delta = settle(list(zip(*kinds)), sink)
-                    total = total + jnp.exp(sink - log_norm) * row_delta
-                chips.append(total)
-            total = jnp.sum(sum(ordered(chips, at_query, side)))
-            terms = terms - jnp.where(lane == done, total, 0.0)
-            done += 1
-    return terms
-
-
 def put_terms(ref, terms):
     high = terms.astype(jnp.bfloat16)
     rest = terms - high.astype(jnp.float32)
@@ -272,38 +285,41 @@
     block = jnp.zeros((EXTRA, BLOCK), jnp.float32)
     for place, part in enumerate(rows):
         block = jnp.where(row == place, part, block)
-    ref[pl.ds(ref.shape[0] - EXTRA, EXTRA), :] = block.astype(jnp.bfloat16)
+    ref[...] = block.astype(jnp.bfloat16)
 
 
 def get_terms(ref):
-    block = ref[...].astype(jnp.float32)
+    block = ref[pl.ds(ref.shape[0] - EXTRA, EXTRA), :].astype(jnp.float32)
     return block[0:1] + block[1:2] + block[2:3]
 
 
-def grads_kernel(first, heads, slots, side, scaling, groups, tiles, sink_ref, *refs):
-    stat_groups = [refs[2 * slots + i * side :][:side] for i in range(groups)]
-    stat_refs = stat_groups[-1]
-    rest = refs[2 * slots + groups * side :]
+def grads_kernel(spans, slots, side, scaling, lead, joins, tiles, sink_ref, *refs):
+    first, heads = spans[0][2], sum(span[-1] for span in spans)
+    per_span = 2 * slots + side
+    rest = refs[per_span * len(spans) :]
     remote = slots - CORES
-    if first:
-        done = rest[0].shape[0]
-        rest[3][:done, :] = rest[0][...]
-        rest = rest[1:]
-    dq_home, dkv_home, core_out = rest[:3]
-    dq_out, dkv_out = rest[3 : 3 + remote], rest[3 + remote : 3 + 2 * remote]
+    outs = rest[-11 - 2 * remote : -8]
+    for before, place in zip(rest, joins):
+        outs[place][: before.shape[0]] = before[...]
+    dq_home, dkv_home, core_out = outs[:3]
+    dq_out, dkv_out = outs[3 : 3 + remote], outs[3 + remote :]
     q_all, g_all, k_all, v_all, rows, dkeys, dvalues, dquery = rest[-8:]
     query_side, key_side = (q_all, g_all), (k_all, v_all)
-    spread([(first, heads)], slots, refs, query_side, key_side)
+    spread(spans, slots, refs, query_side, key_side)
     dkeys[...] = jnp.zeros_like(dkeys)
     dvalues[...] = jnp.zeros_like(dvalues)
     dquery[...] = jnp.zeros_like(dquery)
-    for head in range(heads):
-        for slot in range(slots):
-            log_norm, row_delta = settle(
-                stat_rows(stat_refs, head, slot, slots), sink_ref[first + head]
-            )
-            rows[head * slots + slot, 0:1, :] = log_norm
-            rows[head * slots + slot, 1:2, :] = row_delta
+    place = 0
+    for span, (_, offset, start, count) in enumerate(spans):
+        stat_refs = refs[2 * slots * len(spans) + side * span :][:side]
+        for head in range(count):
+            for slot in range(slots):
+                log_norm, row_delta = settle(
+                    stat_rows(stat_refs, offset + head, slot, slots), sink_ref[start + head]
+                )
+                rows[place, 0:1, :] = log_norm
+                rows[place, 1:2, :] = row_delta
+                place += 1
 
     def work(query, one, two, scores, dprobs):
         weights = jnp.exp(scores * scaling - rows[query, 0:1, :])
@@ -325,54 +341,53 @@
             place = head * slots + slot
             total = dquery[place].T * scaling
             if slot == 0:
-                dq_home[head] = total
+                dq_home[lead + head] = total
             elif slot < CORES:
                 core_out[pl.ds((first + head) * 3 * tokens, tokens), :] = total.astype(jnp.bfloat16)
             else:
-                dq_out[slot - CORES][pl.ds(head * tokens, tokens), :] = total.astype(jnp.bfloat16)
+                dq_out[slot - CORES][pl.ds((lead + head) * tokens, tokens), :] = total.astype(jnp.bfloat16)
             for part in range(parts):
                 span = pl.ds(part * BLOCK, BLOCK)
                 dkey = dkeys[place * parts + part] * scaling
                 dvalue = dvalues[place * parts + part]
                 if slot == 0:
-                    dkv_home[head, 0, span, :] = dkey
-                    dkv_home[head, 1, span, :] = dvalue
+                    dkv_home[lead + head, 0, span, :] = dkey
+                    dkv_home[lead + head, 1, span, :] = dvalue
                     continue
                 if slot < CORES:
                     ref, start = core_out, ((first + head) * 3 + 1) * tokens + part * BLOCK
                 else:
-                    ref, start = dkv_out[slot - CORES], head * 2 * tokens + part * BLOCK
+                    ref, start = dkv_out[slot - CORES], (lead + head) * 2 * tokens + part * BLOCK
                 ref[pl.ds(start, BLOCK), :] = dkey.astype(jnp.bfloat16)
                 ref[pl.ds(start + tokens, BLOCK), :] = dvalue.astype(jnp.bfloat16)
-    if groups > 1:
-        _, at_query, _ = coordinates(side)
-        terms = sink_terms(stat_groups, slots, side, sink_ref, at_query)
-        terms_out = rest[3 + 2 * remote]
-        terms_out[...] = jnp.broadcast_to(terms, terms_out.shape)
-        for ref in (core_out, *dkv_out):
-            put_terms(ref, terms)
-
-
-def grads(tiles, sink, qd, kv, partials, before, first, heads, scaling):
-    slots, tokens = len(qd), qd[0].shape[2]
-    side, groups = len(partials[0]), len(partials)
-    extra = EXTRA if groups > 1 else 0
+
+
+def grads(tiles, sink, qds, kvs, partials, before, join, after, spans, last, scaling):
+    slots, tokens = len(qds[0]), qds[0][0].shape[2]
+    first, heads = spans[0][2], sum(span[-1] for span in spans)
+    side = len(partials[0])
+    extra = EXTRA if last else 0
     remote = slots - CORES
     blocks = heads * slots * (tokens // BLOCK)
     low, high = jnp.bfloat16, jnp.float32
-    befores = [] if before is None else [before]
-    operands = qd + kv + [each for group in partials for each in group] + befores
+    joins = [] if before is None else list(range(len(before))) if join else [2]
+    lead = before[0].shape[0] if join else 0
+    count = lead + heads
+    operands = [each for chunk, *_ in spans for each in qds[chunk] + kvs[chunk]]
+    operands += [each for chunk, *_ in spans for each in partials[chunk]]
+    operands += [before[place] for place in joins]
     shapes = [
-        ((heads, tokens, BLOCK), high),
-        ((heads, 2, tokens, BLOCK), high),
+        ((count, tokens, BLOCK), high),
+        ((count, 2, tokens, BLOCK), high),
         (((first + heads) * 3 * tokens + extra, BLOCK), low),
     ]
-    shapes += [((heads * tokens, BLOCK), low)] * remote
-    shapes += [((heads * 2 * tokens + extra, BLOCK), low)] * remote
-    shapes += [((8, BLOCK), high)] * (groups > 1)
+    shapes += [((count * tokens, BLOCK), low)] * remote
+    shapes += [((count * 2 * tokens + extra, BLOCK), low)] * remote
     return pl.pallas_call(
-        lambda *refs: grads_kernel(first, heads, slots, side, scaling, groups, *refs),
-        in_specs=[pl.BlockSpec(memory_space=pltpu.SMEM)] * 2 + whole(len(operands)),
+        lambda *refs: grads_kernel(spans, slots, side, scaling, lead, joins, *refs),
+        in_specs=[pl.BlockSpec(memory_space=pltpu.SMEM)] * 2
+        + whole(len(operands))
+        + [pl.BlockSpec(memory_space=pl.ANY)] * len(after),
         out_specs=whole(len(shapes)),
         out_shape=[jax.ShapeDtypeStruct(shape, kind) for shape, kind in shapes],
         scratch_shapes=tile_scratch(heads, slots, tokens)
@@ -383,7 +398,7 @@
             flops=heads * 4 * 10**9, bytes_accessed=1, transcendentals=0
         ),
         name="gradients",
-    )(tiles, sink, *operands)
+    )(tiles, sink, *operands, *after)
 
 
 def gate(arrays, after):
@@ -400,9 +415,9 @@
     )(*arrays, *after)
 
 
-def close_kernel(sizes, side, half, from_core, *refs):
+def close_kernel(sizes, side, half, sums_ref, from_core, *refs):
     per = 2 + 4 * (side - 1)
-    outs = refs[per * len(sizes) :]
+    *outs, sink_out = refs[per * len(sizes) :]
     core = lax.axis_index("ctx") % CORES
     first = 0
     for chunk, heads in enumerate(sizes):
@@ -425,15 +440,26 @@
                 out[0, :, mine] = sum(parts[1::2], parts[0]).astype(jnp.bfloat16)
                 out[0, :, other] = sum(parts[2::2], start).astype(jnp.bfloat16)
             first += BLOCK
-
-
-def close(pieces, from_core, sizes, side, half, tokens):
-    flat = [from_core] + [piece for chunk in pieces for piece in chunk]
+    half_heads = half // BLOCK
+    _, at_query, at_key = coordinates(side)
+    far = refs[per * len(sizes) - 2 * (side - 1) : per * len(sizes)]
+    mine = [sums_ref[0:1, :]] + [get_terms(ref) for ref in far[0::2]]
+    other = [get_terms(from_core)] + [get_terms(ref) for ref in far[1::2]]
+    mine, other = sum(ordered(mine, at_key, side)), sum(ordered(other, at_query, side))
+    low = jnp.where(core == 0, mine, other)
+    high = pltpu.roll(jnp.where(core == 0, other, mine), half_heads, 1)
+    lane = lax.broadcasted_iota(jnp.int32, (1, BLOCK), 1)
+    sink_out[...] = jnp.where(lane < half_heads, low, high)[:, : 2 * half_heads]
+
+
+def close(pieces, from_core, sums, sizes, side, half, tokens):
+    flat = [sums, from_core] + [piece for chunk in pieces for piece in chunk]
     return pl.pallas_call(
         lambda *refs: close_kernel(sizes, side, half, *refs),
         in_specs=whole(len(flat)),
-        out_specs=whole(3),
-        out_shape=[jax.ShapeDtypeStruct((1, tokens, 2 * half), jnp.bfloat16)] * 3,
+        out_specs=whole(4),
+        out_shape=[jax.ShapeDtypeStruct((1, tokens, 2 * half), jnp.bfloat16)] * 3
+        + [jax.ShapeDtypeStruct((1, 2 * half // BLOCK), jnp.float32)],
         compiler_params=pltpu.CompilerParams(vmem_limit_bytes=VMEM_BYTES),
         cost_estimate=SMALL,
         name="closing_sums",
@@ -447,8 +473,16 @@
 
 
 def lists_kernel(spans, half_heads, side, per_group, listed, groups, *refs):
-    asked, outs, spots = refs[: 2 * side], refs[2 * side : -1], refs[-1]
     slots = side * CORES
+    asked, refs = refs[:slots], refs[slots:]
+    own = (len(refs) - 2 - len(spans)) // 2
+    outs, stages, spots, sems = refs[own : own + len(spans)], refs[own + len(spans) : -2], refs[-2], refs[-1]
+    copies = [
+        pltpu.make_async_copy(source, stage, sems.at[place])
+        for place, (source, stage) in enumerate(zip(refs, stages))
+    ]
+    for copy in copies:
+        copy.start()
     rest, core = halved(lax.axis_index("ctx"), CORES)
     row, col = halved(rest, side)
 
@@ -490,70 +524,108 @@
             return count
 
         out[0] = lax.fori_loop(0, heads, one_head, jnp.int32(1)) - 1
-
-
-def tile_lists(asked, spans, half_heads, side, per_group, groups):
+    for copy in copies:
+        copy.wait()
+
+
+def tile_lists(asked, own, spans, half_heads, side, per_group, groups):
     slots, listed = len(asked), asked[0].shape[2]
     assert half_heads * slots * per_group < 255
     most = slots * ((listed + 1) // 2) + CORES * (per_group // 2)
     return pl.pallas_call(
         lambda *refs: lists_kernel(spans, half_heads, side, per_group, listed, groups, *refs),
-        in_specs=[pl.BlockSpec(memory_space=pltpu.SMEM)] * slots,
-        out_specs=[pl.BlockSpec(memory_space=pltpu.SMEM)] * len(spans),
-        out_shape=[jax.ShapeDtypeStruct((heads * most + 8,), jnp.int32) for _, heads in spans],
-        scratch_shapes=[pltpu.SMEM((groups * per_group,), jnp.int32)],
+        in_specs=[pl.BlockSpec(memory_space=pltpu.SMEM)] * slots
+        + [pl.BlockSpec(memory_space=pl.ANY)] * len(own),
+        out_specs=[pl.BlockSpec(memory_space=pltpu.SMEM)] * len(spans) + whole(len(own)),
+        out_shape=[jax.ShapeDtypeStruct((heads * most + 8,), jnp.int32) for _, heads in spans]
+        + [jax.ShapeDtypeStruct(each.shape, each.dtype) for each in own],
+        scratch_shapes=[
+            pltpu.SMEM((groups * per_group,), jnp.int32),
+            pltpu.SemaphoreType.DMA((len(own),)),
+        ],
+        compiler_params=pltpu.CompilerParams(vmem_limit_bytes=VMEM_BYTES),
+        cost_estimate=SMALL,
+        name="tile_lists",
+    )(*asked, *own)
+
+
+def sink_kernel(sizes, slots, side, sink_ref, *refs):
+    out = refs[-1]
+    _, at_query, _ = coordinates(side)
+    lane = lax.broadcasted_iota(jnp.int32, (1, BLOCK), 1)
+    terms = jnp.zeros((1, BLOCK), jnp.float32)
+    done = 0
+    for chunk, heads in enumerate(sizes):
+        stat_refs = refs[chunk * side : (chunk + 1) * side]
+        for head in range(heads):
+            sink = sink_ref[done]
+            chips = []
+            for shift in range(side):
+                total = 0.0
+                for cross in range(CORES):
+                    rows = stat_rows(stat_refs, head, shift * CORES + cross, slots)
+                    kinds = [ordered(kind, at_query, side) for kind in zip(*rows)]
+                    log_norm, row_delta = settle(list(zip(*kinds)), sink)
+                    total = total + jnp.exp(sink - log_norm) * row_delta
+                chips.append(total)
+            total = jnp.sum(sum(ordered(chips, at_query, side)))
+            terms = terms - jnp.where(lane == done, total, 0.0)
+            done += 1
+    row = lax.broadcasted_iota(jnp.int32, out.shape, 0)
+    out[...] = jnp.where(row == lax.axis_index("dp"), terms, 0.0)
+
+
+def sink_terms(partials, sink, sizes, slots, side, after):
+    operands = [part for parts in partials for part in parts]
+    return pl.pallas_call(
+        lambda *refs: sink_kernel(sizes, slots, side, *refs),
+        in_specs=[pl.BlockSpec(memory_space=pltpu.SMEM)]
+        + whole(len(operands))
+        + [pl.BlockSpec(memory_space=pl.ANY)] * len(after),
+        out_specs=whole(1)[0],
+        out_shape=jax.ShapeDtypeStruct((lax.axis_size("dp"), BLOCK), jnp.float32),
         compiler_params=pltpu.CompilerParams(vmem_limit_bytes=FEW_BYTES),
         cost_estimate=SMALL,
-        name="tile_lists",
-    )(*asked)
-
-
-def sink_kernel(half_heads, side, terms_ref, core_ref, *refs):
-    *far, out = refs
-    core, at_query, at_key = coordinates(side)
-    mine = [terms_ref[0:1, :]] + [get_terms(ref) for ref in far[0::CORES]]
-    other = [get_terms(core_ref)] + [get_terms(ref) for ref in far[1::CORES]]
-    mine = sum(ordered(mine, at_key, side))
-    other = sum(ordered(other, at_query, side))
-    lane = lax.broadcasted_iota(jnp.int32, (1, BLOCK), 1)
-    low = jnp.where(core == 0, mine, other)
-    high = pltpu.roll(jnp.where(core == 0, other, mine), half_heads, 1)
-    terms = jnp.where(lane < half_heads, low, high)
-    row = lax.broadcasted_iota(jnp.int32, out.shape, 0)
-    out[...] = jnp.where(row == lax.axis_index("dp"), terms, 0.0)
-
-
-def sink_sum(terms, from_core, far, half_heads, side):
-    arrays = [from_core, *far]
-    last = [
-        pl.BlockSpec((EXTRA, BLOCK), lambda i, end=array.shape[0] // EXTRA - 1: (end, 0))
-        for array in arrays
+        name="sink_terms",
+    )(sink, *operands, *after)
+
+
+def sink_mark(held, messages, arrays, after):
+    count = len(messages)
+
+    def kernel(held_ref, *refs):
+        total = jnp.sum(held_ref[...], axis=0, keepdims=True)
+        sum_ref, *outs = refs[count + len(arrays) + len(after) :]
+        sum_ref[...] = jnp.broadcast_to(total, sum_ref.shape)
+        for out in outs[:count]:
+            put_terms(out, total)
+
+    any_spec = pl.BlockSpec(memory_space=pl.ANY)
+    ends = [
+        pl.BlockSpec((EXTRA, BLOCK), lambda i, end=each.shape[0] // EXTRA - 1: (end, 0))
+        for each in messages
     ]
-    shape = (lax.axis_size("dp"), BLOCK)
+    passed = [*messages, *arrays]
     return pl.pallas_call(
-        lambda *refs: sink_kernel(half_heads, side, *refs),
+        kernel,
         grid=(1,),
-        in_specs=[pl.BlockSpec((8, BLOCK), lambda i: (0, 0))] + last,
-        out_specs=pl.BlockSpec(shape, lambda i: (0, 0)),
-        out_shape=jax.ShapeDtypeStruct(shape, jnp.float32),
+        in_specs=[pl.BlockSpec(held.shape, lambda i: (0, 0))]
+        + [any_spec] * (len(passed) + len(after)),
+        out_specs=[pl.BlockSpec((8, BLOCK), lambda i: (0, 0))] + ends + [any_spec] * len(arrays),
+        out_shape=[jax.ShapeDtypeStruct((8, BLOCK), jnp.float32)]
+        + [jax.ShapeDtypeStruct(each.shape, each.dtype) for each in passed],
+        input_output_aliases={place + 1: place + 1 for place in range(len(passed))},
         compiler_params=pltpu.CompilerParams(vmem_limit_bytes=FEW_BYTES),
         cost_estimate=SMALL,
-        name="sink_sum",
-    )(terms, *arrays)
+        name="sink_mark",
+    )(held, *passed, *after)
 
 
 def sink_rounds():
     copies = lax.axis_size("dp")
     assert copies & (copies - 1) == 0
-    rounds, step = [], 1
-    while step < copies:
-        radix = 4 if copies % (4 * step) == 0 else 2
-        perms = [
-            [(i, (i + part * step) % copies) for i in range(copies)] for part in range(1, radix)
-        ]
-        rounds.append(("dp", perms))
-        step *= radix
-    return rounds
+    steps = [1 << bit for bit in range(copies.bit_length() - 1)]
+    return [("dp", [[(i, (i + step) % copies) for i in range(copies)]]) for step in steps]
 
 
 def sink_round(held, axis, perms):
@@ -587,21 +659,21 @@
         came = lax.ppermute(pair, "ctx", gather_perm(groups, side, True, shift, 0))
         asked += [came[:, cross : cross + 1] for cross in range(CORES)]
     spans = list(zip(starts, sizes))
-    tiles = tile_lists(asked, spans, half_heads, side, per_group, groups)
-
+    parts = part_spans(sizes, part_sizes(half_heads))
+    part_heads = [(part[0][2], sum(span[-1] for span in part)) for part in parts]
     fields = (query_in, grad_out, key_in, value_in)
+    packed = pack(fields, sizes, half)
+    own = [packed[4 * chunk + pair] for chunk in range(len(sizes)) for pair in range(2)]
+    made = tile_lists(asked, own, spans + part_heads, half_heads, side, per_group, groups)
+    tiles, own = made[: len(spans) + len(parts)], made[len(spans) + len(parts) :]
+    from_core = lax.ppermute(packed[-1], "ctx", swap)
     qds, kvs = [], []
-    for first, heads in zip(starts, sizes):
-        last = first + heads == half_heads
-        packed = pack(fields, first, heads, half_heads if last else 0, half)
-        if not last:
-            fields, packed, pair = lax.optimization_barrier((fields, packed, pair))
-        qd_own, kv_own, qd_oth, kv_oth = packed[:4]
-        if last:
-            from_core = lax.ppermute(packed[4], "ctx", swap)
-            tiles, packed = lax.optimization_barrier((tiles, packed))
-            qd_own, kv_own, qd_oth, kv_oth = packed[:4]
-        qd, kv = [qd_own], [kv_own]
+    for chunk in range(len(sizes)):
+        here = packed[4 * chunk : 4 * chunk + 4]
+        if chunk:
+            here = gate(here, [*tiles, from_core])
+        qd_own, kv_own, qd_oth, kv_oth = here
+        qd, kv = [own[2 * chunk]], [own[2 * chunk + 1]]
         for shift, cross in places:
             perm = gather_perm(groups, side, True, shift, cross)
             qd.append(lax.ppermute(qd_oth if cross else qd_own, "ctx", perm))
@@ -621,37 +693,51 @@
             for shift in range(1, side)
         ]
         partials.append([partial] + came)
-    pieces, core_out = [], None
-    for chunk, (first, heads) in enumerate(spans):
-        last = chunk == len(spans) - 1
+    rounds = sink_rounds()
+    results, pieces, after = None, [], []
+    for number, part in enumerate(parts):
+        last = number == len(parts) - 1
+        if number == 1 or last and not pieces:
+            held = sink_terms(partials, sink, sizes, slots, side, [] if last else results[:1])
+        if number >= 1 and rounds:
+            after = [held]
+            held = sink_round(held, *rounds.pop(0))
         results = grads(
-            tiles[chunk],
+            tiles[len(spans) + number],
             sink,
-            qds[chunk],
-            kvs[chunk],
-            partials if last else partials[chunk : chunk + 1],
-            core_out,
-            first,
-            heads,
+            qds,
+            kvs,
+            partials,
+            results,
+            number >= 2,
+            after,
+            part,
+            last,
             scaling,
         )
-        core_out = results[2]
-        if pieces:
-            results = results[:2] + gate(results[2 : 3 + 2 * remote], pieces[-1][2:]) + results[-1:]
-            core_out = results[2]
-        dq_out, dkv_out = results[3 : 3 + remote], results[3 + remote : 3 + 2 * remote]
+        if number >= 1 and not last:
+            continue
+        sent = results[3:]
+        if last:
+            for each in rounds:
+                held = sink_round(held, *each)
+            arriving = pieces[-1][2:] if pieces else []
+            sums, core_out, *sent = sink_mark(
+                held, [results[2], *sent[remote:]], sent[:remote], arriving
+            )
+            sent = sent[remote:] + sent[:remote]
         back = [
             lax.ppermute(value, "ctx", return_perm(groups, side, along_query, shift, cross))
-            for along_query, values in ((True, dq_out), (False, dkv_out))
+            for along_query, values in ((True, sent[:remote]), (False, sent[remote:]))
             for value, (shift, cross) in zip(values, places)
         ]
         pieces.append(list(results[:2]) + back)
     from_core = lax.ppermute(core_out, "ctx", swap)
-    held = sink_sum(results[-1], from_core, pieces[-1][2 + remote :], half_heads, side)
-    for each in sink_rounds():
-        held = sink_round(held, *each)
-    grad_sink = jnp.sum(held, axis=0)[:head_count]
-    grad_query, grad_key, grad_value = close(pieces, from_core, sizes, side, half, tokens)
+    sent_sizes = [part_sizes(half_heads)[0], half_heads - part_sizes(half_heads)[0]]
+    grad_query, grad_key, grad_value, sinks = close(
+        pieces, from_core, sums, [size for size in sent_sizes if size], side, half, tokens
+    )
+    grad_sink = sinks.reshape(head_count)
     return (grad_query, grad_key, grad_value, grad_sink)
 
 

time: 96.7 us -> 85 us (0.88)
  waiting for transfers between devices: 29.7 us -> 22 us
  local copies, waits for them, and re-layouts: 8.02 us -> 3.1 us
  Pallas kernels: 29.9 us -> 31.4 us
  other arithmetic: 1.35 us -> 0.1 us
    ppermute x4, waiting for transfers between devices: 11.2 us -> 0.01 us  [body(): qd.append(lax.ppermute(qd_oth if cross else qd_own, 'ctx', perm))]
    ppermute x1, waiting for transfers between devices: 0.01 us -> 7.4 us  [body(): came = lax.ppermute(pair, 'ctx', gather_perm(groups, side, True, shift, 0))]
    unnamed x17 -> x15, local copies, waits for them, and re-layouts: 7.24 us -> 3.09 us
    ppermute x8, waiting for transfers between devices: 15.5 us -> 11.4 us  [body(): lax.ppermute(value, 'ctx', return_perm(groups, side, along_query, shift,...]
    ppermute x3 -> x2, waiting for transfers between devices: 2.61 us -> 0.01 us  [sink_round(): return sum([lax.ppermute(held, axis, perm) for perm in perms], held)]
    ppermute x2, waiting for transfers between devices: 0.01 us -> 2.33 us  [body(): lax.ppermute(partial, 'ctx', gather_perm(groups, side, True, shift, 0))]
    ppermute x4, starting transfers between devices: 2.12 us -> 4.12 us  [body(): qd.append(lax.ppermute(qd_oth if cross else qd_own, 'ctx', perm))]
    ppermute x1, starting transfers between devices: 2.94 us -> 1.57 us  [body(): came = lax.ppermute(pair, 'ctx', gather_perm(groups, side, True, shift, 0))]
  transfers between devices with their start and end apart: 25 -> 24, of which waited for: 10 -> 9; matrix products, arithmetic and copies ran while one was open for 2% -> 0% of each run, Pallas kernels for 29% -> 30%
where the time goes in v3:
time: 85 us; the launch traced here: 84.7 us
  Pallas kernels  31.4 us (37%)
  starting transfers between devices  27.2 us (32%)
  waiting for transfers between devices  22 us (26%)
  local copies, waits for them, and re-layouts  3.1 us (4%)
    pallas_call x2, Pallas kernels, grads(): pl.pallas_call(lambda *refs: grads_kernel(spans, slots, side, scaling, le...  12.8 us
    ppermute x8, waiting for transfers between devices, body(): lax.ppermute(value, 'ctx', return_perm(groups, side, along_query, shift,...  11.4 us
    pallas_call x2, Pallas kernels, stats(): pl.pallas_call(lambda *refs: stats_kernel(first, heads, slots, scaling, *...  8.63 us
    ppermute x1, waiting for transfers between devices, body(): came = lax.ppermute(pair, 'ctx', gather_perm(groups, side, True, shift, 0))  7.4 us
    ppermute x8, starting transfers between devices, body(): lax.ppermute(value, 'ctx', return_perm(groups, side, along_query, shift,...  7.05 us
    ppermute x4, starting transfers between devices, body(): kv.append(lax.ppermute(kv_oth if cross else kv_own, 'ctx', perm))  6.17 us
    ppermute x2, starting transfers between devices, sink_round(): return sum([lax.ppermute(held, axis, perm) for perm in perms], held)  4.25 us
    ppermute x4, starting transfers between devices, body(): qd.append(lax.ppermute(qd_oth if cross else qd_own, 'ctx', perm))  4.12 us
  transfers between devices with their start and end apart: 24, of which 9 were waited for; matrix products, arithmetic and copies ran while one was open for 0% of the time, Pallas kernels for 30%

profile of v3, /device:TPU:0, one launch (start us, length us, event | category | flops | bytes accessed | tf_op | source)
XLA Modules:
  0.0 84.7 jit_solution(18074031969758602045)
XLA Ops:
  0.6 3.7 %pack.1 = (bf16[4,2,256,128]{3,2,1,0:T(8,128)(2,1)}, bf16[4,2,256,128]{3,2,1,0:T(8,128)(2,1)}, bf16[4,2,256,128]{3,2,1,0:T(8,128)(2,1)}, bf16[4,2,256,128]{3,2,1...) custom-call(bf16[1,256,1280]{2,1,0:T(8,128)(2,1)} %refs_0_.2, ...), custom_call_target="tpu_custom_call" | custom-call | flops 4000000000 | bytes 1 | tf_op jit(solution)/shard_map/pack/pallas_call | solution.py:119
  4.8 2.6 %collective-permute-start.3 = (bf16[4,2,256,128]{3,2,1,0:T(8,128)(2,1)}, bf16[4,2,256,128]{3,2,1,0:T(8,128)(2,1)S(1)}, u32[]{:S(2)}, u32[]{:S(2)}) collective-permute-start(bf16[4,2,256,128]{3,2,1,0:T(8,128)(2,1)} %get-tuple-element.49.refs_4_), channel_id=1, source_target_pairs={{2,0},{5,1},{0,2},{7,3},{6,4},{1,5},{4,6},{3,7},{10,8},{13,9},{8,1... | collective-permute-start | bytes 1572872 | tf_op jit(solution)/shard_map/ppermute | solution.py:679
  7.4 1.5 %collective-permute-start.5 = (bf16[4,2,256,128]{3,2,1,0:T(8,128)(2,1)}, bf16[4,2,256,128]{3,2,1,0:T(8,128)(2,1)S(1)}, u32[]{:S(2)}, u32[]{:S(2)}) collective-permute-start(bf16[4,2,256,128]{3,2,1,0:T(8,128)(2,1)} %get-tuple-element.50.refs_5_), channel_id=1, source_target_pairs={{4,0},{3,1},{6,2},{1,3},{0,4},{7,5},{2,6},{5,7},{12,8},{11,9},{14,... | collective-permute-start | bytes 1572872 | tf_op jit(solution)/shard_map/ppermute | solution.py:681
  9.7 0.8 collective-permute-done.refs_1_
  10.5 1.6 %collective-permute-start.1 = (s32[10,2,6]{2,1,0:T(2,128)S(1)}, s32[10,2,6]{2,1,0:T(2,128)S(1)}, u32[]{:S(2)}, u32[]{:S(2)}) collective-permute-start(s32[10,2,6]{2,1,0:T(2,128)S(1)} %pad_add_fusion), channel_id=1, source_target_pairs={{2,0},{5,1},{0,2},{7,3},{6,4},{1,5},{4,6},{3,7},{10,8},{13,9},{8,1... | collective-permute-start | bytes 1448 | tf_op jit(solution)/shard_map/ppermute | solution.py:659
  12.1 7.4 %collective-permute-done.1 = s32[10,2,6]{2,1,0:T(2,128)S(1)} collective-permute-done((s32[10,2,6]{2,1,0:T(2,128)S(1)}, s32[10,2,6]{2,1,0:T(2,128)S(1)}, u32[]{:S(2)}, u32[]{:S(2)}) %collective-permute-start.1) | collective-permute-done | bytes 512 | tf_op jit(solution)/shard_map/ppermute | solution.py:659
  19.5 1.8 %collective-permute-start.6 = (bf16[4,2,256,128]{3,2,1,0:T(8,128)(2,1)}, bf16[4,2,256,128]{3,2,1,0:T(8,128)(2,1)S(1)}, u32[]{:S(2)}, u32[]{:S(2)}) collective-permute-start(bf16[4,2,256,128]{3,2,1,0:T(8,128)(2,1)} %get-tuple-element.58), channel_id=1, source_target_pairs={{5,0},{2,1},{7,2},{0,3},{1,4},{6,5},{3,6},{4,7},{13,8},{10,9},{15,... | collective-permute-start | bytes 1572872 | tf_op jit(solution)/shard_map/ppermute | solution.py:681
  21.3 1.0 %copy-done = bf16[4,2,256,128]{3,2,1,0:T(8,128)(2,1)S(1)} copy-done((bf16[4,2,256,128]{3,2,1,0:T(8,128)(2,1)S(1)}, bf16[4,2,256,128]{3,2,1,0:T(8,128)(2,1)}, u32[]{:S(2)}) %copy-start) | copy-done | bytes 524312
  22.3 1.0 %copy-done.1 = bf16[4,2,256,128]{3,2,1,0:T(8,128)(2,1)S(1)} copy-done((bf16[4,2,256,128]{3,2,1,0:T(8,128)(2,1)S(1)}, bf16[4,2,256,128]{3,2,1,0:T(8,128)(2,1)}, u32[]{:S(2)}) %copy-start.1) | copy-done | bytes 524312
  23.3 0.9 %copy-done.2 = bf16[1,2,256,128]{3,2,1,0:T(8,128)(2,1)S(1)} copy-done((bf16[1,2,256,128]{3,2,1,0:T(8,128)(2,1)S(1)}, bf16[1,2,256,128]{3,2,1,0:T(8,128)(2,1)}, u32[]{:S(2)}) %copy-start.2) | copy-done | bytes 131096
  24.3 3.7 %tile_lists.1 = (s32[64]{0:T(128)S(1)}, s32[22]{0:T(128)S(1)}, s32[50]{0:T(128)S(1)}, s32[36]{0:T(128)S(1)}, bf16[4,2,256,128]{3,2,1,0:T(8,128)(2,1)S(1)}, /*ind...) custom-call(s32[10,1,6]{2,1,0:T(1,128)S(1)} %copy.21.refs_0_, ...), custom_call_target="tpu_custom_call" | custom-call | flops 1 | bytes 1 | tf_op jit(solution)/shard_map/tile_lists/pallas_call | solution.py:535
  28.0 1.4 %collective-permute-start.10 = (bf16[1,2,256,128]{3,2,1,0:T(8,128)(2,1)S(1)}, bf16[1,2,256,128]{3,2,1,0:T(8,128)(2,1)S(1)}, u32[]{:S(2)}, u32[]{:S(2)}) collective-permute-start(bf16[1,2,256,128]{3,2,1,0:T(8,128)(2,1)S(1)} %get-tuple-element.68), channel_id=1, source_target_pairs={{4,0},{3,1},{6,2},{1,3},{0,4},{7,5},{2,6},{5,7},{12,8},{11,9},{14,... | collective-permute-start | bytes 393224 | tf_op jit(solution)/shard_map/ppermute | solution.py:681
  29.4 1.5 %collective-permute-start.11 = (bf16[1,2,256,128]{3,2,1,0:T(8,128)(2,1)S(1)}, bf16[1,2,256,128]{3,2,1,0:T(8,128)(2,1)S(1)}, u32[]{:S(2)}, u32[]{:S(2)}) collective-permute-start(bf16[1,2,256,128]{3,2,1,0:T(8,128)(2,1)S(1)} %get-tuple-element.69), channel_id=1, source_target_pairs={{5,0},{2,1},{7,2},{0,3},{1,4},{6,5},{3,6},{4,7},{13,8},{10,9},{15,... | collective-permute-start | bytes 393224 | tf_op jit(solution)/shard_map/ppermute | solution.py:681
  30.9 1.6 %collective-permute-start.8 = (bf16[1,2,256,128]{3,2,1,0:T(8,128)(2,1)}, bf16[1,2,256,128]{3,2,1,0:T(8,128)(2,1)S(1)}, u32[]{:S(2)}, u32[]{:S(2)}) collective-permute-start(bf16[1,2,256,128]{3,2,1,0:T(8,128)(2,1)} %get-tuple-element.65), channel_id=1, source_target_pairs={{2,0},{5,1},{0,2},{7,3},{6,4},{1,5},{4,6},{3,7},{10,8},{13,9},{8,1... | collective-permute-start | bytes 393224 | tf_op jit(solution)/shard_map/ppermute | solution.py:679
  32.5 6.6 %row_stats.2.refs_1_.refs_10_.refs_18_ = f32[4,16,256]{2,1,0:T(8,128)S(1)} custom-call(s32[64]{0:T(128)S(1)} %get-tuple-element.53.refs_0_.refs_4_, f32[5]{0:T(128)S(1)} %broadcast_select_fusion.refs_1_.refs_0_, bf16[4,2,256,128]{3,2,1,0:T(8,128)(2,1)S(1)} %get-tuple-element.54.refs_2_, ...), custom_call_target="tpu_custom_call" | custom-call | flops 1 | bytes 1 | tf_op jit(solution)/shard_map/row_stats/pallas_call | solution.py:226
  39.8 2.1 %row_stats.3.refs_3_.refs_20_ = f32[1,16,256]{2,1,0:T(8,128)S(1)} custom-call(s32[22]{0:T(128)S(1)} %get-tuple-element.59.refs_5_.refs_0_, f32[5]{0:T(128)S(1)} %broadcast_select_fusion.refs_1_.refs_0_, bf16[1,2,256,128]{3,2,1,0:T(8,128)(2,1)S(1)} %get-tuple-element.60.refs_2_.refs_10_, ...), custom_call_target="tpu_custom_call" | custom-call | flops 1 | bytes 1 | tf_op jit(solution)/shard_map/row_stats/pallas_call | solution.py:226
  41.9 1.5 %collective-permute-start.12 = (f32[1,16,256]{2,1,0:T(8,128)S(1)}, f32[1,16,256]{2,1,0:T(8,128)S(1)}, u32[]{:S(2)}, u32[]{:S(2)}) collective-permute-start(f32[1,16,256]{2,1,0:T(8,128)S(1)} %row_stats.3.refs_3_.refs_20_), channel_id=1, source_target_pairs={{2,0},{5,1},{0,2},{7,3},{6,4},{1,5},{4,6},{3,7},{10,8},{13,9},{8,1... | collective-permute-start | bytes 49160 | tf_op jit(solution)/shard_map/ppermute | solution.py:692
  43.4 2.2 %collective-permute-done.12.refs_4_.refs_21_ = f32[1,16,256]{2,1,0:T(8,128)S(1)} collective-permute-done((f32[1,16,256]{2,1,0:T(8,128)S(1)}, f32[1,16,256]{2,1,0:T(8,128)S(1)}, u32[]{:S(2)}, u32[]{:S(2)}) %collective-permute-start.12) | collective-permute-done | bytes 16416 | tf_op jit(solution)/shard_map/ppermute | solution.py:692
  46.5 1.7 %collective-permute-start.13 = (f32[4,128]{1,0:T(4,128)S(1)}, f32[4,128]{1,0:T(4,128)S(1)}, u32[]{:S(2)}, u32[]{:S(2)}) collective-permute-start(f32[4,128]{1,0:T(4,128)S(1)} %sink_terms.1.refs_23_), channel_id=1, source_target_pairs={{0,8},{8,16},{16,24},{24,0},{1,9},{9,17},{17,25},{25,1},{2,10},{10... | collective-permute-start | bytes 6152 | tf_op jit(solution)/shard_map/ppermute | solution.py:632
  48.1 7.4 %gradients.2 = (f32[3,256,128]{2,1,0:T(8,128)S(1)}, f32[3,2,256,128]{3,2,1,0:T(8,128)S(1)}, bf16[2304,128]{1,0:T(8,128)(2,1)S(1)}, bf16[768,128]{1,0:T(8,128)(2,...) custom-call(s32[50]{0:T(128)S(1)} %get-tuple-element.63.refs_6_.refs_0_, ...), custom_call_target="tpu_custom_call" | custom-call | flops 12000000000 | bytes 1 | tf_op jit(solution)/shard_map/gradients/pallas_call | solution.py:386
  55.6 1.2 %collective-permute-start.18 = (bf16[1536,128]{1,0:T(8,128)(2,1)S(1)}, bf16[1536,128]{1,0:T(8,128)(2,1)S(1)}, u32[]{:S(2)}, u32[]{:S(2)}) collective-permute-start(bf16[1536,128]{1,0:T(8,128)(2,1)S(1)} %get-tuple-element.79), channel_id=1, source_target_pairs={{0,5},{1,2},{2,7},{3,0},{4,1},{5,6},{6,3},{7,4},{8,13},{9,10},{10,... | collective-permute-start | bytes 1179656 | tf_op jit(solution)/shard_map/ppermute | solution.py:730
  56.8 0.8 collective-permute-start.15
  57.6 1.4 %collective-permute-start.16 = (bf16[768,128]{1,0:T(8,128)(2,1)S(1)}, bf16[768,128]{1,0:T(8,128)(2,1)S(1)}, u32[]{:S(2)}, u32[]{:S(2)}) collective-permute-start(bf16[768,128]{1,0:T(8,128)(2,1)S(1)} %get-tuple-element.77), channel_id=1, source_target_pairs={{0,3},{1,4},{2,1},{3,6},{4,7},{5,0},{6,5},{7,2},{8,11},{9,12},{10,... | collective-permute-start | bytes 589832 | tf_op jit(solution)/shard_map/ppermute | solution.py:730
  59.1 2.6 %collective-permute-start.14 = (f32[4,128]{1,0:T(4,128)S(1)}, f32[4,128]{1,0:T(4,128)S(1)}, u32[]{:S(2)}, u32[]{:S(2)}) collective-permute-start(f32[4,128]{1,0:T(4,128)S(1)} %add.11), channel_id=1, source_target_pairs={{0,16},{8,24},{16,0},{24,8},{1,17},{9,25},{17,1},{25,9},{2,18},{10... | collective-permute-start | bytes 6152 | tf_op jit(solution)/shard_map/ppermute | solution.py:632
  61.7 5.4 %gradients.3 = (f32[2,256,128]{2,1,0:T(8,128)S(1)}, f32[2,2,256,128]{3,2,1,0:T(8,128)S(1)}, bf16[3856,128]{1,0:T(8,128)(2,1)S(1)}, bf16[512,128]{1,0:T(8,128)(2,...) custom-call(s32[36]{0:T(128)S(1)} %get-tuple-element.64.refs_7_.refs_0_, ...), custom_call_target="tpu_custom_call" | custom-call | flops 8000000000 | bytes 1 | tf_op jit(solution)/shard_map/gradients/pallas_call | solution.py:386
  67.9 3.0 %collective-permute-done.18.refs_8_.refs_7_ = bf16[1536,128]{1,0:T(8,128)(2,1)S(1)} collective-permute-done((bf16[1536,128]{1,0:T(8,128)(2,1)S(1)}, bf16[1536,128]{1,0:T(8,128)(2,1)S(1)}, u32[]{:S(2)}, u32[]{:S(2)}) %collective-permute-start.18) | collective-permute-done | bytes 393248 | tf_op jit(solution)/shard_map/ppermute | solution.py:730
  71.7 0.9 %collective-permute-start.23 = (bf16[1040,128]{1,0:T(8,128)(2,1)S(1)}, bf16[1040,128]{1,0:T(8,128)(2,1)S(1)}, u32[]{:S(2)}, u32[]{:S(2)}) collective-permute-start(bf16[1040,128]{1,0:T(8,128)(2,1)S(1)} %get-tuple-element.89), channel_id=1, source_target_pairs={{0,5},{1,2},{2,7},{3,0},{4,1},{5,6},{6,3},{7,4},{8,13},{9,10},{10,... | collective-permute-start | bytes 798728 | tf_op jit(solution)/shard_map/ppermute | solution.py:730
  73.4 1.7 %collective-permute-start.21 = (bf16[512,128]{1,0:T(8,128)(2,1)S(1)}, bf16[512,128]{1,0:T(8,128)(2,1)S(1)}, u32[]{:S(2)}, u32[]{:S(2)}) collective-permute-start(bf16[512,128]{1,0:T(8,128)(2,1)S(1)} %get-tuple-element.87), channel_id=1, source_target_pairs={{0,3},{1,4},{2,1},{3,6},{4,7},{5,0},{6,5},{7,2},{8,11},{9,12},{10,... | collective-permute-start | bytes 393224 | tf_op jit(solution)/shard_map/ppermute | solution.py:730
  75.2 3.9 %collective-permute-done.20.refs_10_ = bf16[512,128]{1,0:T(8,128)(2,1)S(1)} collective-permute-done((bf16[512,128]{1,0:T(8,128)(2,1)S(1)}, bf16[512,128]{1,0:T(8,128)(2,1)S(1)}, u32[]{:S(2)}, u32[]{:S(2)}) %collective-permute-start.20) | collective-permute-done | bytes 131104 | tf_op jit(solution)/shard_map/ppermute | solution.py:730
  79.1 2.1 %collective-permute-done.21.refs_11_ = bf16[512,128]{1,0:T(8,128)(2,1)S(1)} collective-permute-done((bf16[512,128]{1,0:T(8,128)(2,1)S(1)}, bf16[512,128]{1,0:T(8,128)(2,1)S(1)}, u32[]{:S(2)}, u32[]{:S(2)}) %collective-permute-start.21) | collective-permute-done | bytes 131104 | tf_op jit(solution)/shard_map/ppermute | solution.py:730
  81.2 1.7 %collective-permute-done.23.refs_13_ = bf16[1040,128]{1,0:T(8,128)(2,1)S(1)} collective-permute-done((bf16[1040,128]{1,0:T(8,128)(2,1)S(1)}, bf16[1040,128]{1,0:T(8,128)(2,1)S(1)}, u32[]{:S(2)}, u32[]{:S(2)}) %collective-permute-start.23) | collective-permute-done | bytes 266272 | tf_op jit(solution)/shard_map/ppermute | solution.py:730
  82.9 1.8 %closing_sums.1 = (bf16[1,256,1280]{2,1,0:T(8,128)(2,1)}, bf16[1,256,1280]{2,1,0:T(8,128)(2,1)}, bf16[1,256,1280]{2,1,0:T(8,128)(2,1)}, f32[1,10]{1,0:T(1,128)}) custom-call(f32[8,128]{1,0:T(8,128)S(1)} %get-tuple-element.80.refs_0_, bf16[3856,128]{1,0:T(8,128)(2,1)S(1)} %collective-permute-done.19.refs_1_, f32[3,256,128]{2,1,0:T(8,128)S(1)} %get-tuple-element.82.refs_2_, ...), custom_call_target="tpu_custom_call" | custom-call | flops 1 | bytes 1 | tf_op jit(solution)/shard_map/closing_sums/pallas_call | solution.py:457
  (46 shorter events, 5.4 us)
Async XLA Ops:
  0.6 8.3 %copy-start.5 = (s32[10,1,6]{0,1,2:T(1,128)S(1)}, s32[10,1,6]{0,1,2:T(1,128)}, u32[]{:S(2)}) copy-start(s32[10,1,6]{0,1,2:T(1,128)} %param.10) | copy-start | bytes 724
  4.3 23.6 %collective-permute-start.2 = (bf16[5,4,256,128]{3,2,1,0:T(8,128)(2,1)}, bf16[5,4,256,128]{3,2,1,0:T(8,128)(2,1)S(1)}, u32[]{:S(2)}, u32[]{:S(2)}) collective-permute-start(bf16[5,4,256,128]{3,2,1,0:T(8,128)(2,1)} %get-tuple-element.55), channel_id=1, source_target_pairs={{1,0},{0,1},{3,2},{2,3},{5,4},{4,5},{7,6},{6,7},{9,8},{8,9},{11,10... | collective-permute-start | bytes 3932168 | tf_op jit(solution)/shard_map/ppermute | solution.py:669
  4.8 24.6 %collective-permute-start.3 = (bf16[4,2,256,128]{3,2,1,0:T(8,128)(2,1)}, bf16[4,2,256,128]{3,2,1,0:T(8,128)(2,1)S(1)}, u32[]{:S(2)}, u32[]{:S(2)}) collective-permute-start(bf16[4,2,256,128]{3,2,1,0:T(8,128)(2,1)} %get-tuple-element.49.refs_4_), channel_id=1, source_target_pairs={{2,0},{5,1},{0,2},{7,3},{6,4},{1,5},{4,6},{3,7},{10,8},{13,9},{8,1... | collective-permute-start | bytes 1572872 | tf_op jit(solution)/shard_map/ppermute | solution.py:679
  7.4 23.5 %collective-permute-start.5 = (bf16[4,2,256,128]{3,2,1,0:T(8,128)(2,1)}, bf16[4,2,256,128]{3,2,1,0:T(8,128)(2,1)S(1)}, u32[]{:S(2)}, u32[]{:S(2)}) collective-permute-start(bf16[4,2,256,128]{3,2,1,0:T(8,128)(2,1)} %get-tuple-element.50.refs_5_), channel_id=1, source_target_pairs={{4,0},{3,1},{6,2},{1,3},{0,4},{7,5},{2,6},{5,7},{12,8},{11,9},{14,... | collective-permute-start | bytes 1572872 | tf_op jit(solution)/shard_map/ppermute | solution.py:681
  8.9 23.5 %collective-permute-start.4 = (bf16[4,2,256,128]{3,2,1,0:T(8,128)(2,1)}, bf16[4,2,256,128]{3,2,1,0:T(8,128)(2,1)S(1)}, u32[]{:S(2)}, u32[]{:S(2)}) collective-permute-start(bf16[4,2,256,128]{3,2,1,0:T(8,128)(2,1)} %get-tuple-element.56), channel_id=1, source_target_pairs={{3,0},{4,1},{1,2},{6,3},{7,4},{0,5},{5,6},{2,7},{11,8},{12,9},{9,1... | collective-permute-start | bytes 1572872 | tf_op jit(solution)/shard_map/ppermute | solution.py:679
  9.0 1.5 %collective-permute-start = (s32[10,1,6]{2,1,0:T(1,128)S(1)}, s32[10,1,6]{2,1,0:T(1,128)S(1)}, u32[]{:S(2)}, u32[]{:S(2)}) collective-permute-start(s32[10,1,6]{2,1,0:T(1,128)S(1)} %copy.21.refs_0_), channel_id=1, source_target_pairs={{1,0},{0,1},{3,2},{2,3},{5,4},{4,5},{7,6},{6,7},{9,8},{8,9},{11,10... | collective-permute-start | bytes 728 | tf_op jit(solution)/shard_map/ppermute | solution.py:655
  10.5 9.0 %collective-permute-start.1 = (s32[10,2,6]{2,1,0:T(2,128)S(1)}, s32[10,2,6]{2,1,0:T(2,128)S(1)}, u32[]{:S(2)}, u32[]{:S(2)}) collective-permute-start(s32[10,2,6]{2,1,0:T(2,128)S(1)} %pad_add_fusion), channel_id=1, source_target_pairs={{2,0},{5,1},{0,2},{7,3},{6,4},{1,5},{4,6},{3,7},{10,8},{13,9},{8,1... | collective-permute-start | bytes 1448 | tf_op jit(solution)/shard_map/ppermute | solution.py:659
  19.5 13.0 %collective-permute-start.6 = (bf16[4,2,256,128]{3,2,1,0:T(8,128)(2,1)}, bf16[4,2,256,128]{3,2,1,0:T(8,128)(2,1)S(1)}, u32[]{:S(2)}, u32[]{:S(2)}) collective-permute-start(bf16[4,2,256,128]{3,2,1,0:T(8,128)(2,1)} %get-tuple-element.58), channel_id=1, source_target_pairs={{5,0},{2,1},{7,2},{0,3},{1,4},{6,5},{3,6},{4,7},{13,8},{10,9},{15,... | collective-permute-start | bytes 1572872 | tf_op jit(solution)/shard_map/ppermute | solution.py:681
  21.3 1.0 %copy-start = (bf16[4,2,256,128]{3,2,1,0:T(8,128)(2,1)S(1)}, bf16[4,2,256,128]{3,2,1,0:T(8,128)(2,1)}, u32[]{:S(2)}) copy-start(bf16[4,2,256,128]{3,2,1,0:T(8,128)(2,1)} %get-tuple-element.50.refs_5_) | copy-start | bytes 1572868
  22.3 1.0 %copy-start.1 = (bf16[4,2,256,128]{3,2,1,0:T(8,128)(2,1)S(1)}, bf16[4,2,256,128]{3,2,1,0:T(8,128)(2,1)}, u32[]{:S(2)}) copy-start(bf16[4,2,256,128]{3,2,1,0:T(8,128)(2,1)} %get-tuple-element.49.refs_4_) | copy-start | bytes 1572868
  23.3 0.9 %copy-start.2 = (bf16[1,2,256,128]{3,2,1,0:T(8,128)(2,1)S(1)}, bf16[1,2,256,128]{3,2,1,0:T(8,128)(2,1)}, u32[]{:S(2)}) copy-start(bf16[1,2,256,128]{3,2,1,0:T(8,128)(2,1)} %get-tuple-element.52.refs_7_.refs_1_) | copy-start | bytes 393220
  24.2 3.7 %copy-start.3 = (bf16[1,2,256,128]{3,2,1,0:T(8,128)(2,1)S(1)}, bf16[1,2,256,128]{3,2,1,0:T(8,128)(2,1)}, u32[]{:S(2)}) copy-start(bf16[1,2,256,128]{3,2,1,0:T(8,128)(2,1)} %get-tuple-element.61.refs_2_) | copy-start | bytes 393220
  24.2 3.7 %copy-start.4 = (bf16[1,2,256,128]{3,2,1,0:T(8,128)(2,1)S(1)}, bf16[1,2,256,128]{3,2,1,0:T(8,128)(2,1)}, u32[]{:S(2)}) copy-start(bf16[1,2,256,128]{3,2,1,0:T(8,128)(2,1)} %get-tuple-element.62.refs_3_) | copy-start | bytes 393220
  24.3 8.2 %copy-start.6 = (f32[10]{0:T(128)S(1)}, f32[10]{0:T(128)}, u32[]{:S(2)}) copy-start(f32[10]{0:T(128)} %param.11) | copy-start | bytes 124
  28.0 11.8 %collective-permute-start.10 = (bf16[1,2,256,128]{3,2,1,0:T(8,128)(2,1)S(1)}, bf16[1,2,256,128]{3,2,1,0:T(8,128)(2,1)S(1)}, u32[]{:S(2)}, u32[]{:S(2)}) collective-permute-start(bf16[1,2,256,128]{3,2,1,0:T(8,128)(2,1)S(1)} %get-tuple-element.68), channel_id=1, source_target_pairs={{4,0},{3,1},{6,2},{1,3},{0,4},{7,5},{2,6},{5,7},{12,8},{11,9},{14,... | collective-permute-start | bytes 393224 | tf_op jit(solution)/shard_map/ppermute | solution.py:681
  29.4 10.4 %collective-permute-start.11 = (bf16[1,2,256,128]{3,2,1,0:T(8,128)(2,1)S(1)}, bf16[1,2,256,128]{3,2,1,0:T(8,128)(2,1)S(1)}, u32[]{:S(2)}, u32[]{:S(2)}) collective-permute-start(bf16[1,2,256,128]{3,2,1,0:T(8,128)(2,1)S(1)} %get-tuple-element.69), channel_id=1, source_target_pairs={{5,0},{2,1},{7,2},{0,3},{1,4},{6,5},{3,6},{4,7},{13,8},{10,9},{15,... | collective-permute-start | bytes 393224 | tf_op jit(solution)/shard_map/ppermute | solution.py:681
  30.9 8.9 %collective-permute-start.8 = (bf16[1,2,256,128]{3,2,1,0:T(8,128)(2,1)}, bf16[1,2,256,128]{3,2,1,0:T(8,128)(2,1)S(1)}, u32[]{:S(2)}, u32[]{:S(2)}) collective-permute-start(bf16[1,2,256,128]{3,2,1,0:T(8,128)(2,1)} %get-tuple-element.65), channel_id=1, source_target_pairs={{2,0},{5,1},{0,2},{7,3},{6,4},{1,5},{4,6},{3,7},{10,8},{13,9},{8,1... | collective-permute-start | bytes 393224 | tf_op jit(solution)/shard_map/ppermute | solution.py:679
  32.4 7.4 %collective-permute-start.9 = (bf16[1,2,256,128]{3,2,1,0:T(8,128)(2,1)S(1)}, bf16[1,2,256,128]{3,2,1,0:T(8,128)(2,1)S(1)}, u32[]{:S(2)}, u32[]{:S(2)}) collective-permute-start(bf16[1,2,256,128]{3,2,1,0:T(8,128)(2,1)S(1)} %get-tuple-element.66), channel_id=1, source_target_pairs={{3,0},{4,1},{1,2},{6,3},{7,4},{0,5},{5,6},{2,7},{11,8},{12,9},{9,1... | collective-permute-start | bytes 393224 | tf_op jit(solution)/shard_map/ppermute | solution.py:679
  39.1 4.3 %collective-permute-start.7 = (f32[4,16,256]{2,1,0:T(8,128)S(1)}, f32[4,16,256]{2,1,0:T(8,128)S(1)}, u32[]{:S(2)}, u32[]{:S(2)}) collective-permute-start(f32[4,16,256]{2,1,0:T(8,128)S(1)} %row_stats.2.refs_1_.refs_10_.refs_18_), channel_id=1, source_target_pairs={{2,0},{5,1},{0,2},{7,3},{6,4},{1,5},{4,6},{3,7},{10,8},{13,9},{8,1... | collective-permute-start | bytes 196616 | tf_op jit(solution)/shard_map/ppermute | solution.py:692
  41.9 3.8 %collective-permute-start.12 = (f32[1,16,256]{2,1,0:T(8,128)S(1)}, f32[1,16,256]{2,1,0:T(8,128)S(1)}, u32[]{:S(2)}, u32[]{:S(2)}) collective-permute-start(f32[1,16,256]{2,1,0:T(8,128)S(1)} %row_stats.3.refs_3_.refs_20_), channel_id=1, source_target_pairs={{2,0},{5,1},{0,2},{7,3},{6,4},{1,5},{4,6},{3,7},{10,8},{13,9},{8,1... | collective-permute-start | bytes 49160 | tf_op jit(solution)/shard_map/ppermute | solution.py:692
  46.5 12.6 %collective-permute-start.13 = (f32[4,128]{1,0:T(4,128)S(1)}, f32[4,128]{1,0:T(4,128)S(1)}, u32[]{:S(2)}, u32[]{:S(2)}) collective-permute-start(f32[4,128]{1,0:T(4,128)S(1)} %sink_terms.1.refs_23_), channel_id=1, source_target_pairs={{0,8},{8,16},{16,24},{24,0},{1,9},{9,17},{17,25},{25,1},{2,10},{10... | collective-permute-start | bytes 6152 | tf_op jit(solution)/shard_map/ppermute | solution.py:632
  55.5 12.3 %collective-permute-start.17 = (bf16[1536,128]{1,0:T(8,128)(2,1)S(1)}, bf16[1536,128]{1,0:T(8,128)(2,1)S(1)}, u32[]{:S(2)}, u32[]{:S(2)}) collective-permute-start(bf16[1536,128]{1,0:T(8,128)(2,1)S(1)} %get-tuple-element.78), channel_id=1, source_target_pairs={{0,4},{1,3},{2,6},{3,1},{4,0},{5,7},{6,2},{7,5},{8,12},{9,11},{10,... | collective-permute-start | bytes 1179656 | tf_op jit(solution)/shard_map/ppermute | solution.py:730
  55.6 15.3 %collective-permute-start.18 = (bf16[1536,128]{1,0:T(8,128)(2,1)S(1)}, bf16[1536,128]{1,0:T(8,128)(2,1)S(1)}, u32[]{:S(2)}, u32[]{:S(2)}) collective-permute-start(bf16[1536,128]{1,0:T(8,128)(2,1)S(1)} %get-tuple-element.79), channel_id=1, source_target_pairs={{0,5},{1,2},{2,7},{3,0},{4,1},{5,6},{6,3},{7,4},{8,13},{9,10},{10,... | collective-permute-start | bytes 1179656 | tf_op jit(solution)/shard_map/ppermute | solution.py:730
  56.8 10.3 %collective-permute-start.15 = (bf16[768,128]{1,0:T(8,128)(2,1)S(1)}, bf16[768,128]{1,0:T(8,128)(2,1)S(1)}, u32[]{:S(2)}, u32[]{:S(2)}) collective-permute-start(bf16[768,128]{1,0:T(8,128)(2,1)S(1)} %get-tuple-element.76), channel_id=1, source_target_pairs={{0,2},{1,5},{2,0},{3,7},{4,6},{5,1},{6,4},{7,3},{8,10},{9,13},{10,... | collective-permute-start | bytes 589832 | tf_op jit(solution)/shard_map/ppermute | solution.py:730
  57.6 10.2 %collective-permute-start.16 = (bf16[768,128]{1,0:T(8,128)(2,1)S(1)}, bf16[768,128]{1,0:T(8,128)(2,1)S(1)}, u32[]{:S(2)}, u32[]{:S(2)}) collective-permute-start(bf16[768,128]{1,0:T(8,128)(2,1)S(1)} %get-tuple-element.77), channel_id=1, source_target_pairs={{0,3},{1,4},{2,1},{3,6},{4,7},{5,0},{6,5},{7,2},{8,11},{9,12},{10,... | collective-permute-start | bytes 589832 | tf_op jit(solution)/shard_map/ppermute | solution.py:730
  59.1 8.0 %collective-permute-start.14 = (f32[4,128]{1,0:T(4,128)S(1)}, f32[4,128]{1,0:T(4,128)S(1)}, u32[]{:S(2)}, u32[]{:S(2)}) collective-permute-start(f32[4,128]{1,0:T(4,128)S(1)} %add.11), channel_id=1, source_target_pairs={{0,16},{8,24},{16,0},{24,8},{1,17},{9,25},{17,1},{25,9},{2,18},{10... | collective-permute-start | bytes 6152 | tf_op jit(solution)/shard_map/ppermute | solution.py:632
  70.9 12.0 %collective-permute-start.19 = (bf16[3856,128]{1,0:T(8,128)(2,1)S(1)}, bf16[3856,128]{1,0:T(8,128)(2,1)S(1)}, u32[]{:S(2)}, u32[]{:S(2)}) collective-permute-start(bf16[3856,128]{1,0:T(8,128)(2,1)S(1)} %get-tuple-element.81), channel_id=1, source_target_pairs={{1,0},{0,1},{3,2},{2,3},{5,4},{4,5},{7,6},{6,7},{9,8},{8,9},{11,10... | collective-permute-start | bytes 2961416 | tf_op jit(solution)/shard_map/ppermute | solution.py:735
  71.7 9.5 %collective-permute-start.22 = (bf16[1040,128]{1,0:T(8,128)(2,1)S(1)}, bf16[1040,128]{1,0:T(8,128)(2,1)S(1)}, u32[]{:S(2)}, u32[]{:S(2)}) collective-permute-start(bf16[1040,128]{1,0:T(8,128)(2,1)S(1)} %get-tuple-element.88), channel_id=1, source_target_pairs={{0,4},{1,3},{2,6},{3,1},{4,0},{5,7},{6,2},{7,5},{8,12},{9,11},{10,... | collective-permute-start | bytes 798728 | tf_op jit(solution)/shard_map/ppermute | solution.py:730
  71.7 11.2 %collective-permute-start.23 = (bf16[1040,128]{1,0:T(8,128)(2,1)S(1)}, bf16[1040,128]{1,0:T(8,128)(2,1)S(1)}, u32[]{:S(2)}, u32[]{:S(2)}) collective-permute-start(bf16[1040,128]{1,0:T(8,128)(2,1)S(1)} %get-tuple-element.89), channel_id=1, source_target_pairs={{0,5},{1,2},{2,7},{3,0},{4,1},{5,6},{6,3},{7,4},{8,13},{9,10},{10,... | collective-permute-start | bytes 798728 | tf_op jit(solution)/shard_map/ppermute | solution.py:730
  72.7 6.4 %collective-permute-start.20 = (bf16[512,128]{1,0:T(8,128)(2,1)S(1)}, bf16[512,128]{1,0:T(8,128)(2,1)S(1)}, u32[]{:S(2)}, u32[]{:S(2)}) collective-permute-start(bf16[512,128]{1,0:T(8,128)(2,1)S(1)} %get-tuple-element.86), channel_id=1, source_target_pairs={{0,2},{1,5},{2,0},{3,7},{4,6},{5,1},{6,4},{7,3},{8,10},{9,13},{10,... | collective-permute-start | bytes 393224 | tf_op jit(solution)/shard_map/ppermute | solution.py:730
  73.4 7.7 %collective-permute-start.21 = (bf16[512,128]{1,0:T(8,128)(2,1)S(1)}, bf16[512,128]{1,0:T(8,128)(2,1)S(1)}, u32[]{:S(2)}, u32[]{:S(2)}) collective-permute-start(bf16[512,128]{1,0:T(8,128)(2,1)S(1)} %get-tuple-element.87), channel_id=1, source_target_pairs={{0,3},{1,4},{2,1},{3,6},{4,7},{5,0},{6,5},{7,2},{8,11},{9,12},{10,... | collective-permute-start | bytes 393224 | tf_op jit(solution)/shard_map/ppermute | solution.py:730

commit v4 on v3

--- a/solution.py
+++ b/solution.py
@@ -13,7 +13,7 @@
 VMEM_BYTES = 24 * 1024 * 1024
 FEW_BYTES = 2 * 1024 * 1024
 MOST_BYTES = 62 * 1024 * 1024
-UNROLL = 5
+MANY, FEW = 10, 5
 EXTRA = 16
 SMALL = pl.CostEstimate(flops=1, bytes_accessed=1, transcendentals=0)
 NT = (((1,), (1,)), ((), ()))
@@ -172,15 +172,22 @@
 
 
 def walk(tiles, query_side, key_side, work):
-    def step(index, carry):
-        made = [
-            tile_products(UNROLL * index + i, tiles, query_side, key_side) for i in range(UNROLL)
-        ]
-        for one in made:
-            work(*one)
-        return carry
-
-    lax.fori_loop(0, (tiles[0] + UNROLL - 1) // UNROLL, step, 0)
+    def steps(start, size, count):
+        def step(index, carry):
+            made = [
+                tile_products(start + size * index + i, tiles, query_side, key_side)
+                for i in range(size)
+            ]
+            for one in made:
+                work(*one)
+            return carry
+
+        lax.fori_loop(0, count, step, 0)
+
+    many, _ = halved(tiles[0], MANY)
+    steps(0, MANY, many)
+    few, _ = halved(tiles[0] - many * MANY + FEW - 1, FEW)
+    steps(many * MANY, FEW, few)
 
 
 def tile_scratch(heads, slots, tokens):
@@ -293,7 +300,7 @@
     return block[0:1] + block[1:2] + block[2:3]
 
 
-def grads_kernel(spans, slots, side, scaling, lead, joins, tiles, sink_ref, *refs):
+def grads_kernel(spans, slots, side, scaling, joins, tiles, sink_ref, *refs):
     first, heads = spans[0][2], sum(span[-1] for span in spans)
     per_span = 2 * slots + side
     rest = refs[per_span * len(spans) :]
@@ -341,28 +348,28 @@
             place = head * slots + slot
             total = dquery[place].T * scaling
             if slot == 0:
-                dq_home[lead + head] = total
+                dq_home[head] = total
             elif slot < CORES:
                 core_out[pl.ds((first + head) * 3 * tokens, tokens), :] = total.astype(jnp.bfloat16)
             else:
-                dq_out[slot - CORES][pl.ds((lead + head) * tokens, tokens), :] = total.astype(jnp.bfloat16)
+                dq_out[slot - CORES][pl.ds((first + head) * tokens, tokens), :] = total.astype(jnp.bfloat16)
             for part in range(parts):
                 span = pl.ds(part * BLOCK, BLOCK)
                 dkey = dkeys[place * parts + part] * scaling
                 dvalue = dvalues[place * parts + part]
                 if slot == 0:
-                    dkv_home[lead + head, 0, span, :] = dkey
-                    dkv_home[lead + head, 1, span, :] = dvalue
+                    dkv_home[head, 0, span, :] = dkey
+                    dkv_home[head, 1, span, :] = dvalue
                     continue
                 if slot < CORES:
                     ref, start = core_out, ((first + head) * 3 + 1) * tokens + part * BLOCK
                 else:
-                    ref, start = dkv_out[slot - CORES], (lead + head) * 2 * tokens + part * BLOCK
+                    ref, start = dkv_out[slot - CORES], head * 2 * tokens + part * BLOCK
                 ref[pl.ds(start, BLOCK), :] = dkey.astype(jnp.bfloat16)
                 ref[pl.ds(start + tokens, BLOCK), :] = dvalue.astype(jnp.bfloat16)
 
 
-def grads(tiles, sink, qds, kvs, partials, before, join, after, spans, last, scaling):
+def grads(tiles, sink, qds, kvs, partials, before, after, spans, last, scaling):
     slots, tokens = len(qds[0]), qds[0][0].shape[2]
     first, heads = spans[0][2], sum(span[-1] for span in spans)
     side = len(partials[0])
@@ -370,21 +377,19 @@
     remote = slots - CORES
     blocks = heads * slots * (tokens // BLOCK)
     low, high = jnp.bfloat16, jnp.float32
-    joins = [] if before is None else list(range(len(before))) if join else [2]
-    lead = before[0].shape[0] if join else 0
-    count = lead + heads
+    joins = [] if before is None else list(range(2, 3 + remote))
     operands = [each for chunk, *_ in spans for each in qds[chunk] + kvs[chunk]]
     operands += [each for chunk, *_ in spans for each in partials[chunk]]
     operands += [before[place] for place in joins]
     shapes = [
-        ((count, tokens, BLOCK), high),
-        ((count, 2, tokens, BLOCK), high),
+        ((heads, tokens, BLOCK), high),
+        ((heads, 2, tokens, BLOCK), high),
         (((first + heads) * 3 * tokens + extra, BLOCK), low),
     ]
-    shapes += [((count * tokens, BLOCK), low)] * remote
-    shapes += [((count * 2 * tokens + extra, BLOCK), low)] * remote
+    shapes += [(((first + heads) * tokens, BLOCK), low)] * remote
+    shapes += [((heads * 2 * tokens + extra, BLOCK), low)] * remote
     return pl.pallas_call(
-        lambda *refs: grads_kernel(spans, slots, side, scaling, lead, joins, *refs),
+        lambda *refs: grads_kernel(spans, slots, side, scaling, joins, *refs),
         in_specs=[pl.BlockSpec(memory_space=pltpu.SMEM)] * 2
         + whole(len(operands))
         + [pl.BlockSpec(memory_space=pl.ANY)] * len(after),
@@ -416,13 +421,13 @@
 
 
 def close_kernel(sizes, side, half, sums_ref, from_core, *refs):
-    per = 2 + 4 * (side - 1)
+    per = 2 + 2 * (side - 1)
+    dq_far, refs = refs[: per - 2], refs[per - 2 :]
     *outs, sink_out = refs[per * len(sizes) :]
     core = lax.axis_index("ctx") % CORES
     first = 0
     for chunk, heads in enumerate(sizes):
-        dq_home, dkv_home, *far = refs[per * chunk : per * (chunk + 1)]
-        dq_far, dkv_far = far[: 2 * (side - 1)], far[2 * (side - 1) :]
+        dq_home, dkv_home, *dkv_far = refs[per * chunk : per * (chunk + 1)]
         tokens = dq_home.shape[1]
         for head in range(heads):
             mine = pl.ds(pl.multiple_of(core * half + first, BLOCK), BLOCK)
@@ -430,7 +435,8 @@
             for place, out in enumerate(outs):
                 if place == 0:
                     parts = [dq_home[head]]
-                    parts += [ref[pl.ds(head * tokens, tokens), :] for ref in dq_far]
+                    span = pl.ds(first // BLOCK * tokens, tokens)
+                    parts += [ref[span, :] for ref in dq_far]
                 else:
                     span = pl.ds((head * 2 + place - 1) * tokens, tokens)
                     parts = [dkv_home[head, place - 1]] + [ref[span, :] for ref in dkv_far]
@@ -452,8 +458,8 @@
     sink_out[...] = jnp.where(lane < half_heads, low, high)[:, : 2 * half_heads]
 
 
-def close(pieces, from_core, sums, sizes, side, half, tokens):
-    flat = [sums, from_core] + [piece for chunk in pieces for piece in chunk]
+def close(pieces, dq_far, from_core, sums, sizes, side, half, tokens):
+    flat = [sums, from_core, *dq_far] + [piece for chunk in pieces for piece in chunk]
     return pl.pallas_call(
         lambda *refs: close_kernel(sizes, side, half, *refs),
         in_specs=whole(len(flat)),
@@ -624,8 +630,15 @@
 def sink_rounds():
     copies = lax.axis_size("dp")
     assert copies & (copies - 1) == 0
-    steps = [1 << bit for bit in range(copies.bit_length() - 1)]
-    return [("dp", [[(i, (i + step) % copies) for i in range(copies)]]) for step in steps]
+    rounds, step = [], 1
+    while step < copies:
+        radix = 4 if copies % (4 * step) == 0 else 2
+        perms = [
+            [(i, (i + part * step) % copies) for i in range(copies)] for part in range(1, radix)
+        ]
+        rounds.append(("dp", perms))
+        step *= radix
+    return rounds
 
 
 def sink_round(held, axis, perms):
@@ -671,7 +684,7 @@
     for chunk in range(len(sizes)):
         here = packed[4 * chunk : 4 * chunk + 4]
         if chunk:
-            here = gate(here, [*tiles, from_core])
+            here = gate(here[:3], [from_core]) + gate(here[3:], [from_core, *tiles])
         qd_own, kv_own, qd_oth, kv_oth = here
         qd, kv = [own[2 * chunk]], [own[2 * chunk + 1]]
         for shift, cross in places:
@@ -709,33 +722,29 @@
             kvs,
             partials,
             results,
-            number >= 2,
             after,
             part,
             last,
             scaling,
         )
-        if number >= 1 and not last:
-            continue
-        sent = results[3:]
+        sent = results[3 + remote :]
         if last:
             for each in rounds:
                 held = sink_round(held, *each)
             arriving = pieces[-1][2:] if pieces else []
-            sums, core_out, *sent = sink_mark(
-                held, [results[2], *sent[remote:]], sent[:remote], arriving
-            )
-            sent = sent[remote:] + sent[:remote]
+            sums, core_out, *sent = sink_mark(held, [results[2], *sent], [], arriving)
         back = [
-            lax.ppermute(value, "ctx", return_perm(groups, side, along_query, shift, cross))
-            for along_query, values in ((True, sent[:remote]), (False, sent[remote:]))
-            for value, (shift, cross) in zip(values, places)
+            lax.ppermute(value, "ctx", return_perm(groups, side, False, shift, cross))
+            for value, (shift, cross) in zip(sent, places)
         ]
         pieces.append(list(results[:2]) + back)
+    dq_far = [
+        lax.ppermute(value, "ctx", return_perm(groups, side, True, shift, cross))
+        for value, (shift, cross) in zip(results[3 : 3 + remote], places)
+    ]
     from_core = lax.ppermute(core_out, "ctx", swap)
-    sent_sizes = [part_sizes(half_heads)[0], half_heads - part_sizes(half_heads)[0]]
     grad_query, grad_key, grad_value, sinks = close(
-        pieces, from_core, sums, [size for size in sent_sizes if size], side, half, tokens
+        pieces, dq_far, from_core, sums, part_sizes(half_heads), side, half, tokens
     )
     grad_sink = sinks.reshape(head_count)
     return (grad_query, grad_key, grad_value, grad_sink)

time: 85 us -> 82.1 us (0.966)
  Pallas kernels: 31.4 us -> 29.9 us
  waiting for transfers between devices: 22 us -> 20.6 us
    ppermute x2, waiting for transfers between devices: 2.33 us -> 0.08 us  [body(): lax.ppermute(partial, 'ctx', gather_perm(groups, side, True, shift, 0))]
    ppermute x2 -> x3, starting transfers between devices: 4.25 us -> 5.56 us  [sink_round(): return sum([lax.ppermute(held, axis, perm) for perm in perms], held)]
    pallas_call x2, Pallas kernels: 8.63 us -> 7.75 us  [stats(): pl.pallas_call(lambda *refs: stats_kernel(first, heads, slots, scaling, *...]
    ppermute x8 -> x6, waiting for transfers between devices: 11.4 us -> 12.3 us  [the longest x2 12.3 us: body(): lax.ppermute(value, 'ctx', return_perm(groups, side, True, shift, cross))]
    ppermute x8 -> x6, starting transfers between devices: 7.05 us -> 6.74 us  [the longest x4 6.01 us: body(): lax.ppermute(value, 'ctx', return_perm(groups, side, False, shift, cross))]
  transfers between devices with their start and end apart: 24 -> 23, of which waited for: 9 -> 5; matrix products, arithmetic and copies ran while one was open for 0% -> 0% of each run, Pallas kernels for 30% -> 30%
where the time goes in v4:
time: 82.1 us; the launch traced here: 81.9 us
  Pallas kernels  29.9 us (36%)
  starting transfers between devices  27.3 us (33%)
  waiting for transfers between devices  20.6 us (25%)
  local copies, waits for them, and re-layouts  3.1 us (4%)
  between operations  0.85 us (1%)
    ppermute x2, waiting for transfers between devices, body(): lax.ppermute(value, 'ctx', return_perm(groups, side, True, shift, cross))  12.3 us
    pallas_call x2, Pallas kernels, grads(): pl.pallas_call(lambda *refs: grads_kernel(spans, slots, side, scaling, jo...  12.2 us
    pallas_call x2, Pallas kernels, stats(): pl.pallas_call(lambda *refs: stats_kernel(first, heads, slots, scaling, *...  7.75 us
    ppermute x1, waiting for transfers between devices, body(): came = lax.ppermute(pair, 'ctx', gather_perm(groups, side, True, shift, 0))  7.4 us
    ppermute x4, starting transfers between devices, body(): lax.ppermute(value, 'ctx', return_perm(groups, side, False, shift, cross))  6.01 us
    ppermute x4, starting transfers between devices, body(): kv.append(lax.ppermute(kv_oth if cross else kv_own, 'ctx', perm))  5.97 us
    ppermute x3, starting transfers between devices, sink_round(): return sum([lax.ppermute(held, axis, perm) for perm in perms], held)  5.56 us
    ppermute x4, starting transfers between devices, body(): qd.append(lax.ppermute(qd_oth if cross else qd_own, 'ctx', perm))  4.12 us
  transfers between devices with their start and end apart: 23, of which 5 were waited for; matrix products, arithmetic and copies ran while one was open for 0% of the time, Pallas kernels for 30%

profile of v4, /device:TPU:0, one launch (start us, length us, event | category | flops | bytes accessed | tf_op | source)
XLA Modules:
  0.0 81.9 jit_solution(248607027779800056)
XLA Ops:
  0.6 3.7 %pack.1 = (bf16[4,2,256,128]{3,2,1,0:T(8,128)(2,1)}, bf16[4,2,256,128]{3,2,1,0:T(8,128)(2,1)}, bf16[4,2,256,128]{3,2,1,0:T(8,128)(2,1)}, bf16[4,2,256,128]{3,2,1...) custom-call(bf16[1,256,1280]{2,1,0:T(8,128)(2,1)} %refs_0_.2, ...), custom_call_target="tpu_custom_call" | custom-call | flops 4000000000 | bytes 1 | tf_op jit(solution)/shard_map/pack/pallas_call | solution.py:119
  4.8 2.6 %collective-permute-start.3 = (bf16[4,2,256,128]{3,2,1,0:T(8,128)(2,1)}, bf16[4,2,256,128]{3,2,1,0:T(8,128)(2,1)S(1)}, u32[]{:S(2)}, u32[]{:S(2)}) collective-permute-start(bf16[4,2,256,128]{3,2,1,0:T(8,128)(2,1)} %get-tuple-element.46.refs_4_), channel_id=1, source_target_pairs={{2,0},{5,1},{0,2},{7,3},{6,4},{1,5},{4,6},{3,7},{10,8},{13,9},{8,1... | collective-permute-start | bytes 1572872 | tf_op jit(solution)/shard_map/ppermute | solution.py:692
  7.4 1.5 %collective-permute-start.5 = (bf16[4,2,256,128]{3,2,1,0:T(8,128)(2,1)}, bf16[4,2,256,128]{3,2,1,0:T(8,128)(2,1)S(1)}, u32[]{:S(2)}, u32[]{:S(2)}) collective-permute-start(bf16[4,2,256,128]{3,2,1,0:T(8,128)(2,1)} %get-tuple-element.47.refs_5_), channel_id=1, source_target_pairs={{4,0},{3,1},{6,2},{1,3},{0,4},{7,5},{2,6},{5,7},{12,8},{11,9},{14,... | collective-permute-start | bytes 1572872 | tf_op jit(solution)/shard_map/ppermute | solution.py:694
  9.0 0.6 collective-permute-start
  9.7 0.8 %collective-permute-done.refs_1_ = s32[10,1,6]{2,1,0:T(1,128)S(1)} collective-permute-done((s32[10,1,6]{2,1,0:T(1,128)S(1)}, s32[10,1,6]{2,1,0:T(1,128)S(1)}, u32[]{:S(2)}, u32[]{:S(2)}) %collective-permute-start) | collective-permute-done | bytes 272 | tf_op jit(solution)/shard_map/ppermute | solution.py:668
  10.5 1.6 %collective-permute-start.1 = (s32[10,2,6]{2,1,0:T(2,128)S(1)}, s32[10,2,6]{2,1,0:T(2,128)S(1)}, u32[]{:S(2)}, u32[]{:S(2)}) collective-permute-start(s32[10,2,6]{2,1,0:T(2,128)S(1)} %pad_add_fusion), channel_id=1, source_target_pairs={{2,0},{5,1},{0,2},{7,3},{6,4},{1,5},{4,6},{3,7},{10,8},{13,9},{8,1... | collective-permute-start | bytes 1448 | tf_op jit(solution)/shard_map/ppermute | solution.py:672
  12.1 7.4 %collective-permute-done.1 = s32[10,2,6]{2,1,0:T(2,128)S(1)} collective-permute-done((s32[10,2,6]{2,1,0:T(2,128)S(1)}, s32[10,2,6]{2,1,0:T(2,128)S(1)}, u32[]{:S(2)}, u32[]{:S(2)}) %collective-permute-start.1) | collective-permute-done | bytes 512 | tf_op jit(solution)/shard_map/ppermute | solution.py:672
  19.5 1.8 %collective-permute-start.6 = (bf16[4,2,256,128]{3,2,1,0:T(8,128)(2,1)}, bf16[4,2,256,128]{3,2,1,0:T(8,128)(2,1)S(1)}, u32[]{:S(2)}, u32[]{:S(2)}) collective-permute-start(bf16[4,2,256,128]{3,2,1,0:T(8,128)(2,1)} %get-tuple-element.55), channel_id=1, source_target_pairs={{5,0},{2,1},{7,2},{0,3},{1,4},{6,5},{3,6},{4,7},{13,8},{10,9},{15,... | collective-permute-start | bytes 1572872 | tf_op jit(solution)/shard_map/ppermute | solution.py:694
  21.3 1.0 %copy-done = bf16[4,2,256,128]{3,2,1,0:T(8,128)(2,1)S(1)} copy-done((bf16[4,2,256,128]{3,2,1,0:T(8,128)(2,1)S(1)}, bf16[4,2,256,128]{3,2,1,0:T(8,128)(2,1)}, u32[]{:S(2)}) %copy-start) | copy-done | bytes 524312
  22.3 1.0 %copy-done.1 = bf16[4,2,256,128]{3,2,1,0:T(8,128)(2,1)S(1)} copy-done((bf16[4,2,256,128]{3,2,1,0:T(8,128)(2,1)S(1)}, bf16[4,2,256,128]{3,2,1,0:T(8,128)(2,1)}, u32[]{:S(2)}) %copy-start.1) | copy-done | bytes 524312
  23.3 0.9 %copy-done.2 = bf16[1,2,256,128]{3,2,1,0:T(8,128)(2,1)S(1)} copy-done((bf16[1,2,256,128]{3,2,1,0:T(8,128)(2,1)S(1)}, bf16[1,2,256,128]{3,2,1,0:T(8,128)(2,1)}, u32[]{:S(2)}) %copy-start.2) | copy-done | bytes 131096
  24.2 3.7 %tile_lists.1 = (s32[64]{0:T(128)S(1)}, s32[22]{0:T(128)S(1)}, s32[50]{0:T(128)S(1)}, s32[36]{0:T(128)S(1)}, bf16[4,2,256,128]{3,2,1,0:T(8,128)(2,1)S(1)}, /*ind...) custom-call(s32[10,1,6]{2,1,0:T(1,128)S(1)} %copy.19.refs_0_, ...), custom_call_target="tpu_custom_call" | custom-call | flops 1 | bytes 1 | tf_op jit(solution)/shard_map/tile_lists/pallas_call | solution.py:541
  28.0 2.7 %collective-permute-start.11 = (bf16[1,2,256,128]{3,2,1,0:T(8,128)(2,1)S(1)}, bf16[1,2,256,128]{3,2,1,0:T(8,128)(2,1)S(1)}, u32[]{:S(2)}, u32[]{:S(2)}) collective-permute-start(bf16[1,2,256,128]{3,2,1,0:T(8,128)(2,1)S(1)} %gate.3), channel_id=1, source_target_pairs={{5,0},{2,1},{7,2},{0,3},{1,4},{6,5},{3,6},{4,7},{13,8},{10,9},{15,... | collective-permute-start | bytes 393224 | tf_op jit(solution)/shard_map/ppermute | solution.py:694
  31.2 1.0 %collective-permute-start.9 = (bf16[1,2,256,128]{3,2,1,0:T(8,128)(2,1)S(1)}, bf16[1,2,256,128]{3,2,1,0:T(8,128)(2,1)S(1)}, u32[]{:S(2)}, u32[]{:S(2)}) collective-permute-start(bf16[1,2,256,128]{3,2,1,0:T(8,128)(2,1)S(1)} %get-tuple-element.60), channel_id=1, source_target_pairs={{3,0},{4,1},{1,2},{6,3},{7,4},{0,5},{5,6},{2,7},{11,8},{12,9},{9,1... | collective-permute-start | bytes 393224 | tf_op jit(solution)/shard_map/ppermute | solution.py:692
  32.3 5.7 %row_stats.2.refs_1_.refs_10_.refs_18_ = f32[4,16,256]{2,1,0:T(8,128)S(1)} custom-call(s32[64]{0:T(128)S(1)} %get-tuple-element.50.refs_0_.refs_2_, f32[5]{0:T(128)S(1)} %broadcast_select_fusion.refs_1_.refs_0_, bf16[4,2,256,128]{3,2,1,0:T(8,128)(2,1)S(1)} %get-tuple-element.51.refs_2_, ...), custom_call_target="tpu_custom_call" | custom-call | flops 1 | bytes 1 | tf_op jit(solution)/shard_map/row_stats/pallas_call | solution.py:233
  38.0 1.2 %collective-permute-start.7 = (f32[4,16,256]{2,1,0:T(8,128)S(1)}, f32[4,16,256]{2,1,0:T(8,128)S(1)}, u32[]{:S(2)}, u32[]{:S(2)}) collective-permute-start(f32[4,16,256]{2,1,0:T(8,128)S(1)} %row_stats.2.refs_1_.refs_10_.refs_18_), channel_id=1, source_target_pairs={{2,0},{5,1},{0,2},{7,3},{6,4},{1,5},{4,6},{3,7},{10,8},{13,9},{8,1... | collective-permute-start | bytes 196616 | tf_op jit(solution)/shard_map/ppermute | solution.py:705
  39.2 2.1 %row_stats.3.refs_3_.refs_20_ = f32[1,16,256]{2,1,0:T(8,128)S(1)} custom-call(s32[22]{0:T(128)S(1)} %get-tuple-element.56.refs_3_.refs_0_, f32[5]{0:T(128)S(1)} %broadcast_select_fusion.refs_1_.refs_0_, bf16[1,2,256,128]{3,2,1,0:T(8,128)(2,1)S(1)} %get-tuple-element.57.refs_2_.refs_10_, ...), custom_call_target="tpu_custom_call" | custom-call | flops 1 | bytes 1 | tf_op jit(solution)/shard_map/row_stats/pallas_call | solution.py:233
  41.3 1.0 %collective-permute-start.12 = (f32[1,16,256]{2,1,0:T(8,128)S(1)}, f32[1,16,256]{2,1,0:T(8,128)S(1)}, u32[]{:S(2)}, u32[]{:S(2)}) collective-permute-start(f32[1,16,256]{2,1,0:T(8,128)S(1)} %row_stats.3.refs_3_.refs_20_), channel_id=1, source_target_pairs={{2,0},{5,1},{0,2},{7,3},{6,4},{1,5},{4,6},{3,7},{10,8},{13,9},{8,1... | collective-permute-start | bytes 49160 | tf_op jit(solution)/shard_map/ppermute | solution.py:705
  42.3 6.9 %gradients.2 = (f32[3,256,128]{2,1,0:T(8,128)S(1)}, f32[3,2,256,128]{3,2,1,0:T(8,128)S(1)}, bf16[2304,128]{1,0:T(8,128)(2,1)S(1)}, bf16[768,128]{1,0:T(8,128)(2,...) custom-call(s32[50]{0:T(128)S(1)} %get-tuple-element.64.refs_4_.refs_0_, ...), custom_call_target="tpu_custom_call" | custom-call | flops 12000000000 | bytes 1 | tf_op jit(solution)/shard_map/gradients/pallas_call | solution.py:391
  49.2 1.6 %collective-permute-start.16 = (bf16[1536,128]{1,0:T(8,128)(2,1)S(1)}, bf16[1536,128]{1,0:T(8,128)(2,1)S(1)}, u32[]{:S(2)}, u32[]{:S(2)}) collective-permute-start(bf16[1536,128]{1,0:T(8,128)(2,1)S(1)} %get-tuple-element.72), channel_id=1, source_target_pairs={{0,4},{1,3},{2,6},{3,1},{4,0},{5,7},{6,2},{7,5},{8,12},{9,11},{10,... | collective-permute-start | bytes 1179656 | tf_op jit(solution)/shard_map/ppermute | solution.py:737
  50.8 1.6 %collective-permute-start.17 = (bf16[1536,128]{1,0:T(8,128)(2,1)S(1)}, bf16[1536,128]{1,0:T(8,128)(2,1)S(1)}, u32[]{:S(2)}, u32[]{:S(2)}) collective-permute-start(bf16[1536,128]{1,0:T(8,128)(2,1)S(1)} %get-tuple-element.73), channel_id=1, source_target_pairs={{0,5},{1,2},{2,7},{3,0},{4,1},{5,6},{6,3},{7,4},{8,13},{9,10},{10,... | collective-permute-start | bytes 1179656 | tf_op jit(solution)/shard_map/ppermute | solution.py:737
  52.4 0.8 sink_terms.1.refs_25_
  53.2 1.6 %collective-permute-start.13 = (f32[4,128]{1,0:T(4,128)S(1)}, f32[4,128]{1,0:T(4,128)S(1)}, u32[]{:S(2)}, u32[]{:S(2)}) collective-permute-start(f32[4,128]{1,0:T(4,128)S(1)} %sink_terms.1.refs_25_), channel_id=1, source_target_pairs={{0,8},{8,16},{16,24},{24,0},{1,9},{9,17},{17,25},{25,1},{2,10},{10... | collective-permute-start | bytes 6152 | tf_op jit(solution)/shard_map/ppermute | solution.py:645
  54.8 2.6 %collective-permute-start.14 = (f32[4,128]{1,0:T(4,128)S(1)}, f32[4,128]{1,0:T(4,128)S(1)}, u32[]{:S(2)}, u32[]{:S(2)}) collective-permute-start(f32[4,128]{1,0:T(4,128)S(1)} %sink_terms.1.refs_25_), channel_id=1, source_target_pairs={{0,16},{8,24},{16,0},{24,8},{1,17},{9,25},{17,1},{25,9},{2,18},{10... | collective-permute-start | bytes 6152 | tf_op jit(solution)/shard_map/ppermute | solution.py:645
  57.4 1.3 %collective-permute-start.15 = (f32[4,128]{1,0:T(4,128)S(1)}, f32[4,128]{1,0:T(4,128)S(1)}, u32[]{:S(2)}, u32[]{:S(2)}) collective-permute-start(f32[4,128]{1,0:T(4,128)S(1)} %sink_terms.1.refs_25_), channel_id=1, source_target_pairs={{0,24},{8,0},{16,8},{24,16},{1,25},{9,1},{17,9},{25,17},{2,26},{10... | collective-permute-start | bytes 6152 | tf_op jit(solution)/shard_map/ppermute | solution.py:645
  58.8 5.3 %gradients.3 = (f32[2,256,128]{2,1,0:T(8,128)S(1)}, f32[2,2,256,128]{3,2,1,0:T(8,128)S(1)}, bf16[3856,128]{1,0:T(8,128)(2,1)S(1)}, bf16[1280,128]{1,0:T(8,128)(2...) custom-call(s32[36]{0:T(128)S(1)} %get-tuple-element.65.refs_5_.refs_0_, ...), custom_call_target="tpu_custom_call" | custom-call | flops 8000000000 | bytes 1 | tf_op jit(solution)/shard_map/gradients/pallas_call | solution.py:391
  64.3 0.7 collective-permute-start.19
  65.0 1.7 %collective-permute-start.21 = (bf16[1040,128]{1,0:T(8,128)(2,1)S(1)}, bf16[1040,128]{1,0:T(8,128)(2,1)S(1)}, u32[]{:S(2)}, u32[]{:S(2)}) collective-permute-start(bf16[1040,128]{1,0:T(8,128)(2,1)S(1)} %get-tuple-element.82), channel_id=1, source_target_pairs={{0,4},{1,3},{2,6},{3,1},{4,0},{5,7},{6,2},{7,5},{8,12},{9,11},{10,... | collective-permute-start | bytes 798728 | tf_op jit(solution)/shard_map/ppermute | solution.py:737
  66.7 1.1 %collective-permute-start.22 = (bf16[1040,128]{1,0:T(8,128)(2,1)S(1)}, bf16[1040,128]{1,0:T(8,128)(2,1)S(1)}, u32[]{:S(2)}, u32[]{:S(2)}) collective-permute-start(bf16[1040,128]{1,0:T(8,128)(2,1)S(1)} %get-tuple-element.83), channel_id=1, source_target_pairs={{0,5},{1,2},{2,7},{3,0},{4,1},{5,6},{6,3},{7,4},{8,13},{9,10},{10,... | collective-permute-start | bytes 798728 | tf_op jit(solution)/shard_map/ppermute | solution.py:737
  67.8 7.0 %collective-permute-done.19.refs_2_ = bf16[1280,128]{1,0:T(8,128)(2,1)S(1)} collective-permute-done((bf16[1280,128]{1,0:T(8,128)(2,1)S(1)}, bf16[1280,128]{1,0:T(8,128)(2,1)S(1)}, u32[]{:S(2)}, u32[]{:S(2)}) %collective-permute-start.19) | collective-permute-done | bytes 327712 | tf_op jit(solution)/shard_map/ppermute | solution.py:742
  74.9 5.2 %collective-permute-done.20.refs_3_ = bf16[1280,128]{1,0:T(8,128)(2,1)S(1)} collective-permute-done((bf16[1280,128]{1,0:T(8,128)(2,1)S(1)}, bf16[1280,128]{1,0:T(8,128)(2,1)S(1)}, u32[]{:S(2)}, u32[]{:S(2)}) %collective-permute-start.20) | collective-permute-done | bytes 327712 | tf_op jit(solution)/shard_map/ppermute | solution.py:742
  80.1 1.8 %closing_sums.1 = (bf16[1,256,1280]{2,1,0:T(8,128)(2,1)}, bf16[1,256,1280]{2,1,0:T(8,128)(2,1)}, bf16[1,256,1280]{2,1,0:T(8,128)(2,1)}, f32[1,10]{1,0:T(1,128)}) custom-call(f32[8,128]{1,0:T(8,128)S(1)} %get-tuple-element.74.refs_0_, bf16[3856,128]{1,0:T(8,128)(2,1)S(1)} %collective-permute-done.18.refs_1_, ...), custom_call_target="tpu_custom_call" | custom-call | flops 1 | bytes 1 | tf_op jit(solution)/shard_map/closing_sums/pallas_call | solution.py:463
  (44 shorter events, 1.6 us)
Async XLA Ops:
  0.6 8.3 %copy-start.5 = (s32[10,1,6]{0,1,2:T(1,128)S(1)}, s32[10,1,6]{0,1,2:T(1,128)}, u32[]{:S(2)}) copy-start(s32[10,1,6]{0,1,2:T(1,128)} %param.10) | copy-start | bytes 724
  4.3 23.6 %collective-permute-start.2 = (bf16[5,4,256,128]{3,2,1,0:T(8,128)(2,1)}, bf16[5,4,256,128]{3,2,1,0:T(8,128)(2,1)S(1)}, u32[]{:S(2)}, u32[]{:S(2)}) collective-permute-start(bf16[5,4,256,128]{3,2,1,0:T(8,128)(2,1)} %get-tuple-element.52), channel_id=1, source_target_pairs={{1,0},{0,1},{3,2},{2,3},{5,4},{4,5},{7,6},{6,7},{9,8},{8,9},{11,10... | collective-permute-start | bytes 3932168 | tf_op jit(solution)/shard_map/ppermute | solution.py:682
  4.8 25.8 %collective-permute-start.3 = (bf16[4,2,256,128]{3,2,1,0:T(8,128)(2,1)}, bf16[4,2,256,128]{3,2,1,0:T(8,128)(2,1)S(1)}, u32[]{:S(2)}, u32[]{:S(2)}) collective-permute-start(bf16[4,2,256,128]{3,2,1,0:T(8,128)(2,1)} %get-tuple-element.46.refs_4_), channel_id=1, source_target_pairs={{2,0},{5,1},{0,2},{7,3},{6,4},{1,5},{4,6},{3,7},{10,8},{13,9},{8,1... | collective-permute-start | bytes 1572872 | tf_op jit(solution)/shard_map/ppermute | solution.py:692
  7.4 23.3 %collective-permute-start.5 = (bf16[4,2,256,128]{3,2,1,0:T(8,128)(2,1)}, bf16[4,2,256,128]{3,2,1,0:T(8,128)(2,1)S(1)}, u32[]{:S(2)}, u32[]{:S(2)}) collective-permute-start(bf16[4,2,256,128]{3,2,1,0:T(8,128)(2,1)} %get-tuple-element.47.refs_5_), channel_id=1, source_target_pairs={{4,0},{3,1},{6,2},{1,3},{0,4},{7,5},{2,6},{5,7},{12,8},{11,9},{14,... | collective-permute-start | bytes 1572872 | tf_op jit(solution)/shard_map/ppermute | solution.py:694
  8.9 22.3 %collective-permute-start.4 = (bf16[4,2,256,128]{3,2,1,0:T(8,128)(2,1)}, bf16[4,2,256,128]{3,2,1,0:T(8,128)(2,1)S(1)}, u32[]{:S(2)}, u32[]{:S(2)}) collective-permute-start(bf16[4,2,256,128]{3,2,1,0:T(8,128)(2,1)} %get-tuple-element.53), channel_id=1, source_target_pairs={{3,0},{4,1},{1,2},{6,3},{7,4},{0,5},{5,6},{2,7},{11,8},{12,9},{9,1... | collective-permute-start | bytes 1572872 | tf_op jit(solution)/shard_map/ppermute | solution.py:692
  9.0 1.5 %collective-permute-start = (s32[10,1,6]{2,1,0:T(1,128)S(1)}, s32[10,1,6]{2,1,0:T(1,128)S(1)}, u32[]{:S(2)}, u32[]{:S(2)}) collective-permute-start(s32[10,1,6]{2,1,0:T(1,128)S(1)} %copy.19.refs_0_), channel_id=1, source_target_pairs={{1,0},{0,1},{3,2},{2,3},{5,4},{4,5},{7,6},{6,7},{9,8},{8,9},{11,10... | collective-permute-start | bytes 728 | tf_op jit(solution)/shard_map/ppermute | solution.py:668
  10.5 9.0 %collective-permute-start.1 = (s32[10,2,6]{2,1,0:T(2,128)S(1)}, s32[10,2,6]{2,1,0:T(2,128)S(1)}, u32[]{:S(2)}, u32[]{:S(2)}) collective-permute-start(s32[10,2,6]{2,1,0:T(2,128)S(1)} %pad_add_fusion), channel_id=1, source_target_pairs={{2,0},{5,1},{0,2},{7,3},{6,4},{1,5},{4,6},{3,7},{10,8},{13,9},{8,1... | collective-permute-start | bytes 1448 | tf_op jit(solution)/shard_map/ppermute | solution.py:672
  19.5 12.8 %collective-permute-start.6 = (bf16[4,2,256,128]{3,2,1,0:T(8,128)(2,1)}, bf16[4,2,256,128]{3,2,1,0:T(8,128)(2,1)S(1)}, u32[]{:S(2)}, u32[]{:S(2)}) collective-permute-start(bf16[4,2,256,128]{3,2,1,0:T(8,128)(2,1)} %get-tuple-element.55), channel_id=1, source_target_pairs={{5,0},{2,1},{7,2},{0,3},{1,4},{6,5},{3,6},{4,7},{13,8},{10,9},{15,... | collective-permute-start | bytes 1572872 | tf_op jit(solution)/shard_map/ppermute | solution.py:694
  21.2 1.0 %copy-start = (bf16[4,2,256,128]{3,2,1,0:T(8,128)(2,1)S(1)}, bf16[4,2,256,128]{3,2,1,0:T(8,128)(2,1)}, u32[]{:S(2)}) copy-start(bf16[4,2,256,128]{3,2,1,0:T(8,128)(2,1)} %get-tuple-element.47.refs_5_) | copy-start | bytes 1572868
  22.3 1.0 %copy-start.1 = (bf16[4,2,256,128]{3,2,1,0:T(8,128)(2,1)S(1)}, bf16[4,2,256,128]{3,2,1,0:T(8,128)(2,1)}, u32[]{:S(2)}) copy-start(bf16[4,2,256,128]{3,2,1,0:T(8,128)(2,1)} %get-tuple-element.46.refs_4_) | copy-start | bytes 1572868
  23.3 0.9 %copy-start.2 = (bf16[1,2,256,128]{3,2,1,0:T(8,128)(2,1)S(1)}, bf16[1,2,256,128]{3,2,1,0:T(8,128)(2,1)}, u32[]{:S(2)}) copy-start(bf16[1,2,256,128]{3,2,1,0:T(8,128)(2,1)} %get-tuple-element.49.refs_7_.refs_1_) | copy-start | bytes 393220
  24.2 3.7 %copy-start.3 = (bf16[1,2,256,128]{3,2,1,0:T(8,128)(2,1)S(1)}, bf16[1,2,256,128]{3,2,1,0:T(8,128)(2,1)}, u32[]{:S(2)}) copy-start(bf16[1,2,256,128]{3,2,1,0:T(8,128)(2,1)} %get-tuple-element.63.refs_0_) | copy-start | bytes 393220
  24.2 6.4 %copy-start.4 = (bf16[1,2,256,128]{3,2,1,0:T(8,128)(2,1)S(1)}, bf16[1,2,256,128]{3,2,1,0:T(8,128)(2,1)}, u32[]{:S(2)}) copy-start(bf16[1,2,256,128]{3,2,1,0:T(8,128)(2,1)} %get-tuple-element.58.refs_2_) | copy-start | bytes 393220
  28.0 4.3 %copy-start.6 = (f32[10]{0:T(128)S(1)}, f32[10]{0:T(128)}, u32[]{:S(2)}) copy-start(f32[10]{0:T(128)} %param.11) | copy-start | bytes 124
  28.0 11.2 %collective-permute-start.11 = (bf16[1,2,256,128]{3,2,1,0:T(8,128)(2,1)S(1)}, bf16[1,2,256,128]{3,2,1,0:T(8,128)(2,1)S(1)}, u32[]{:S(2)}, u32[]{:S(2)}) collective-permute-start(bf16[1,2,256,128]{3,2,1,0:T(8,128)(2,1)S(1)} %gate.3), channel_id=1, source_target_pairs={{5,0},{2,1},{7,2},{0,3},{1,4},{6,5},{3,6},{4,7},{13,8},{10,9},{15,... | collective-permute-start | bytes 393224 | tf_op jit(solution)/shard_map/ppermute | solution.py:694
  30.7 8.5 %collective-permute-start.10 = (bf16[1,2,256,128]{3,2,1,0:T(8,128)(2,1)S(1)}, bf16[1,2,256,128]{3,2,1,0:T(8,128)(2,1)S(1)}, u32[]{:S(2)}, u32[]{:S(2)}) collective-permute-start(bf16[1,2,256,128]{3,2,1,0:T(8,128)(2,1)S(1)} %get-tuple-element.62), channel_id=1, source_target_pairs={{4,0},{3,1},{6,2},{1,3},{0,4},{7,5},{2,6},{5,7},{12,8},{11,9},{14,... | collective-permute-start | bytes 393224 | tf_op jit(solution)/shard_map/ppermute | solution.py:694
  30.7 8.5 %collective-permute-start.8 = (bf16[1,2,256,128]{3,2,1,0:T(8,128)(2,1)}, bf16[1,2,256,128]{3,2,1,0:T(8,128)(2,1)S(1)}, u32[]{:S(2)}, u32[]{:S(2)}) collective-permute-start(bf16[1,2,256,128]{3,2,1,0:T(8,128)(2,1)} %get-tuple-element.59), channel_id=1, source_target_pairs={{2,0},{5,1},{0,2},{7,3},{6,4},{1,5},{4,6},{3,7},{10,8},{13,9},{8,1... | collective-permute-start | bytes 393224 | tf_op jit(solution)/shard_map/ppermute | solution.py:692
  31.2 8.0 %collective-permute-start.9 = (bf16[1,2,256,128]{3,2,1,0:T(8,128)(2,1)S(1)}, bf16[1,2,256,128]{3,2,1,0:T(8,128)(2,1)S(1)}, u32[]{:S(2)}, u32[]{:S(2)}) collective-permute-start(bf16[1,2,256,128]{3,2,1,0:T(8,128)(2,1)S(1)} %get-tuple-element.60), channel_id=1, source_target_pairs={{3,0},{4,1},{1,2},{6,3},{7,4},{0,5},{5,6},{2,7},{11,8},{12,9},{9,1... | collective-permute-start | bytes 393224 | tf_op jit(solution)/shard_map/ppermute | solution.py:692
  38.0 4.3 %collective-permute-start.7 = (f32[4,16,256]{2,1,0:T(8,128)S(1)}, f32[4,16,256]{2,1,0:T(8,128)S(1)}, u32[]{:S(2)}, u32[]{:S(2)}) collective-permute-start(f32[4,16,256]{2,1,0:T(8,128)S(1)} %row_stats.2.refs_1_.refs_10_.refs_18_), channel_id=1, source_target_pairs={{2,0},{5,1},{0,2},{7,3},{6,4},{1,5},{4,6},{3,7},{10,8},{13,9},{8,1... | collective-permute-start | bytes 196616 | tf_op jit(solution)/shard_map/ppermute | solution.py:705
  41.3 11.1 %collective-permute-start.12 = (f32[1,16,256]{2,1,0:T(8,128)S(1)}, f32[1,16,256]{2,1,0:T(8,128)S(1)}, u32[]{:S(2)}, u32[]{:S(2)}) collective-permute-start(f32[1,16,256]{2,1,0:T(8,128)S(1)} %row_stats.3.refs_3_.refs_20_), channel_id=1, source_target_pairs={{2,0},{5,1},{0,2},{7,3},{6,4},{1,5},{4,6},{3,7},{10,8},{13,9},{8,1... | collective-permute-start | bytes 49160 | tf_op jit(solution)/shard_map/ppermute | solution.py:705
  49.2 14.9 %collective-permute-start.16 = (bf16[1536,128]{1,0:T(8,128)(2,1)S(1)}, bf16[1536,128]{1,0:T(8,128)(2,1)S(1)}, u32[]{:S(2)}, u32[]{:S(2)}) collective-permute-start(bf16[1536,128]{1,0:T(8,128)(2,1)S(1)} %get-tuple-element.72), channel_id=1, source_target_pairs={{0,4},{1,3},{2,6},{3,1},{4,0},{5,7},{6,2},{7,5},{8,12},{9,11},{10,... | collective-permute-start | bytes 1179656 | tf_op jit(solution)/shard_map/ppermute | solution.py:737
  50.8 13.3 %collective-permute-start.17 = (bf16[1536,128]{1,0:T(8,128)(2,1)S(1)}, bf16[1536,128]{1,0:T(8,128)(2,1)S(1)}, u32[]{:S(2)}, u32[]{:S(2)}) collective-permute-start(bf16[1536,128]{1,0:T(8,128)(2,1)S(1)} %get-tuple-element.73), channel_id=1, source_target_pairs={{0,5},{1,2},{2,7},{3,0},{4,1},{5,6},{6,3},{7,4},{8,13},{9,10},{10,... | collective-permute-start | bytes 1179656 | tf_op jit(solution)/shard_map/ppermute | solution.py:737
  53.2 10.9 %collective-permute-start.13 = (f32[4,128]{1,0:T(4,128)S(1)}, f32[4,128]{1,0:T(4,128)S(1)}, u32[]{:S(2)}, u32[]{:S(2)}) collective-permute-start(f32[4,128]{1,0:T(4,128)S(1)} %sink_terms.1.refs_25_), channel_id=1, source_target_pairs={{0,8},{8,16},{16,24},{24,0},{1,9},{9,17},{17,25},{25,1},{2,10},{10... | collective-permute-start | bytes 6152 | tf_op jit(solution)/shard_map/ppermute | solution.py:645
  54.8 9.3 %collective-permute-start.14 = (f32[4,128]{1,0:T(4,128)S(1)}, f32[4,128]{1,0:T(4,128)S(1)}, u32[]{:S(2)}, u32[]{:S(2)}) collective-permute-start(f32[4,128]{1,0:T(4,128)S(1)} %sink_terms.1.refs_25_), channel_id=1, source_target_pairs={{0,16},{8,24},{16,0},{24,8},{1,17},{9,25},{17,1},{25,9},{2,18},{10... | collective-permute-start | bytes 6152 | tf_op jit(solution)/shard_map/ppermute | solution.py:645
  57.4 6.7 %collective-permute-start.15 = (f32[4,128]{1,0:T(4,128)S(1)}, f32[4,128]{1,0:T(4,128)S(1)}, u32[]{:S(2)}, u32[]{:S(2)}) collective-permute-start(f32[4,128]{1,0:T(4,128)S(1)} %sink_terms.1.refs_25_), channel_id=1, source_target_pairs={{0,24},{8,0},{16,8},{24,16},{1,25},{9,1},{17,9},{25,17},{2,26},{10... | collective-permute-start | bytes 6152 | tf_op jit(solution)/shard_map/ppermute | solution.py:645
  64.2 15.9 %collective-permute-start.18 = (bf16[3856,128]{1,0:T(8,128)(2,1)S(1)}, bf16[3856,128]{1,0:T(8,128)(2,1)S(1)}, u32[]{:S(2)}, u32[]{:S(2)}) collective-permute-start(bf16[3856,128]{1,0:T(8,128)(2,1)S(1)} %get-tuple-element.75), channel_id=1, source_target_pairs={{1,0},{0,1},{3,2},{2,3},{5,4},{4,5},{7,6},{6,7},{9,8},{8,9},{11,10... | collective-permute-start | bytes 2961416 | tf_op jit(solution)/shard_map/ppermute | solution.py:745
  64.3 10.6 %collective-permute-start.19 = (bf16[1280,128]{1,0:T(8,128)(2,1)S(1)}, bf16[1280,128]{1,0:T(8,128)(2,1)S(1)}, u32[]{:S(2)}, u32[]{:S(2)}) collective-permute-start(bf16[1280,128]{1,0:T(8,128)(2,1)S(1)} %get-tuple-element.76), channel_id=1, source_target_pairs={{0,2},{1,5},{2,0},{3,7},{4,6},{5,1},{6,4},{7,3},{8,10},{9,13},{10,... | collective-permute-start | bytes 983048 | tf_op jit(solution)/shard_map/ppermute | solution.py:742
  64.9 15.2 %collective-permute-start.20 = (bf16[1280,128]{1,0:T(8,128)(2,1)S(1)}, bf16[1280,128]{1,0:T(8,128)(2,1)S(1)}, u32[]{:S(2)}, u32[]{:S(2)}) collective-permute-start(bf16[1280,128]{1,0:T(8,128)(2,1)S(1)} %get-tuple-element.77), channel_id=1, source_target_pairs={{0,3},{1,4},{2,1},{3,6},{4,7},{5,0},{6,5},{7,2},{8,11},{9,12},{10,... | collective-permute-start | bytes 983048 | tf_op jit(solution)/shard_map/ppermute | solution.py:742
  65.0 15.1 %collective-permute-start.21 = (bf16[1040,128]{1,0:T(8,128)(2,1)S(1)}, bf16[1040,128]{1,0:T(8,128)(2,1)S(1)}, u32[]{:S(2)}, u32[]{:S(2)}) collective-permute-start(bf16[1040,128]{1,0:T(8,128)(2,1)S(1)} %get-tuple-element.82), channel_id=1, source_target_pairs={{0,4},{1,3},{2,6},{3,1},{4,0},{5,7},{6,2},{7,5},{8,12},{9,11},{10,... | collective-permute-start | bytes 798728 | tf_op jit(solution)/shard_map/ppermute | solution.py:737
  66.7 13.4 %collective-permute-start.22 = (bf16[1040,128]{1,0:T(8,128)(2,1)S(1)}, bf16[1040,128]{1,0:T(8,128)(2,1)S(1)}, u32[]{:S(2)}, u32[]{:S(2)}) collective-permute-start(bf16[1040,128]{1,0:T(8,128)(2,1)S(1)} %get-tuple-element.83), channel_id=1, source_target_pairs={{0,5},{1,2},{2,7},{3,0},{4,1},{5,6},{6,3},{7,4},{8,13},{9,10},{10,... | collective-permute-start | bytes 798728 | tf_op jit(solution)/shard_map/ppermute | solution.py:737

commit v5 on v4

--- a/solution.py
+++ b/solution.py
@@ -42,8 +42,7 @@
 
 
 def part_sizes(heads):
-    first = (heads + 1) // 2
-    return [size for size in (first, heads - first) if size]
+    return [heads - 1, 1] if heads > 1 else [1]
 
 
 def grid_side(groups):

time: 82.1 us -> 81.3 us (level)
  waiting for transfers between devices: 20.6 us -> 19.6 us
    ppermute x2, waiting for transfers between devices: 12.3 us -> 9.38 us  [body(): lax.ppermute(value, 'ctx', return_perm(groups, side, True, shift, cross))]
    ppermute x4, starting transfers between devices: 6.01 us -> 3.84 us  [body(): lax.ppermute(value, 'ctx', return_perm(groups, side, False, shift, cross))]
    ppermute x2, starting transfers between devices: 0.73 us -> 2.84 us  [body(): lax.ppermute(value, 'ctx', return_perm(groups, side, True, shift, cross))]
    ppermute x4, waiting for transfers between devices: 0.01 us -> 1.83 us  [body(): lax.ppermute(value, 'ctx', return_perm(groups, side, False, shift, cross))]
  transfers between devices with their start and end apart: 23 -> 23, of which waited for: 5 -> 6; matrix products, arithmetic and copies ran while one was open for 0% -> 0% of each run, Pallas kernels for 30% -> 30%
where the time goes in v5:
time: 81.3 us; the launch traced here: 80.8 us
  Pallas kernels  29.8 us (37%)
  starting transfers between devices  27.4 us (34%)
  waiting for transfers between devices  19.6 us (24%)
  local copies, waits for them, and re-layouts  3.1 us (4%)
  between operations  0.83 us (1%)
    pallas_call x2, Pallas kernels, grads(): pl.pallas_call(lambda *refs: grads_kernel(spans, slots, side, scaling, jo...  12.1 us
    ppermute x2, waiting for transfers between devices, body(): lax.ppermute(value, 'ctx', return_perm(groups, side, True, shift, cross))  9.38 us
    pallas_call x2, Pallas kernels, stats(): pl.pallas_call(lambda *refs: stats_kernel(first, heads, slots, scaling, *...  7.75 us
    ppermute x1, waiting for transfers between devices, body(): came = lax.ppermute(pair, 'ctx', gather_perm(groups, side, True, shift, 0))  7.4 us
    ppermute x4, starting transfers between devices, body(): kv.append(lax.ppermute(kv_oth if cross else kv_own, 'ctx', perm))  5.97 us
    ppermute x3, starting transfers between devices, sink_round(): return sum([lax.ppermute(held, axis, perm) for perm in perms], held)  5.57 us
    ppermute x4, starting transfers between devices, body(): qd.append(lax.ppermute(qd_oth if cross else qd_own, 'ctx', perm))  4.12 us
    ppermute x4, starting transfers between devices, body(): lax.ppermute(value, 'ctx', return_perm(groups, side, False, shift, cross))  3.84 us
  transfers between devices with their start and end apart: 23, of which 6 were waited for; matrix products, arithmetic and copies ran while one was open for 0% of the time, Pallas kernels for 30%

profile of v5, /device:TPU:0, one launch (start us, length us, event | category | flops | bytes accessed | tf_op | source)
XLA Modules:
  0.0 80.8 jit_solution(14342253769405945630)
XLA Ops:
  0.6 3.7 %pack.1 = (bf16[4,2,256,128]{3,2,1,0:T(8,128)(2,1)}, bf16[4,2,256,128]{3,2,1,0:T(8,128)(2,1)}, bf16[4,2,256,128]{3,2,1,0:T(8,128)(2,1)}, bf16[4,2,256,128]{3,2,1...) custom-call(bf16[1,256,1280]{2,1,0:T(8,128)(2,1)} %refs_0_.2, ...), custom_call_target="tpu_custom_call" | custom-call | flops 4000000000 | bytes 1 | tf_op jit(solution)/shard_map/pack/pallas_call | solution.py:118
  4.8 2.6 %collective-permute-start.3 = (bf16[4,2,256,128]{3,2,1,0:T(8,128)(2,1)}, bf16[4,2,256,128]{3,2,1,0:T(8,128)(2,1)S(1)}, u32[]{:S(2)}, u32[]{:S(2)}) collective-permute-start(bf16[4,2,256,128]{3,2,1,0:T(8,128)(2,1)} %get-tuple-element.46.refs_4_), channel_id=1, source_target_pairs={{2,0},{5,1},{0,2},{7,3},{6,4},{1,5},{4,6},{3,7},{10,8},{13,9},{8,1... | collective-permute-start | bytes 1572872 | tf_op jit(solution)/shard_map/ppermute | solution.py:691
  7.4 1.5 %collective-permute-start.5 = (bf16[4,2,256,128]{3,2,1,0:T(8,128)(2,1)}, bf16[4,2,256,128]{3,2,1,0:T(8,128)(2,1)S(1)}, u32[]{:S(2)}, u32[]{:S(2)}) collective-permute-start(bf16[4,2,256,128]{3,2,1,0:T(8,128)(2,1)} %get-tuple-element.47.refs_5_), channel_id=1, source_target_pairs={{4,0},{3,1},{6,2},{1,3},{0,4},{7,5},{2,6},{5,7},{12,8},{11,9},{14,... | collective-permute-start | bytes 1572872 | tf_op jit(solution)/shard_map/ppermute | solution.py:693
  9.0 0.6 collective-permute-start
  9.7 0.8 %collective-permute-done.refs_1_ = s32[10,1,6]{2,1,0:T(1,128)S(1)} collective-permute-done((s32[10,1,6]{2,1,0:T(1,128)S(1)}, s32[10,1,6]{2,1,0:T(1,128)S(1)}, u32[]{:S(2)}, u32[]{:S(2)}) %collective-permute-start) | collective-permute-done | bytes 272 | tf_op jit(solution)/shard_map/ppermute | solution.py:667
  10.5 1.6 %collective-permute-start.1 = (s32[10,2,6]{2,1,0:T(2,128)S(1)}, s32[10,2,6]{2,1,0:T(2,128)S(1)}, u32[]{:S(2)}, u32[]{:S(2)}) collective-permute-start(s32[10,2,6]{2,1,0:T(2,128)S(1)} %pad_add_fusion), channel_id=1, source_target_pairs={{2,0},{5,1},{0,2},{7,3},{6,4},{1,5},{4,6},{3,7},{10,8},{13,9},{8,1... | collective-permute-start | bytes 1448 | tf_op jit(solution)/shard_map/ppermute | solution.py:671
  12.1 7.4 %collective-permute-done.1 = s32[10,2,6]{2,1,0:T(2,128)S(1)} collective-permute-done((s32[10,2,6]{2,1,0:T(2,128)S(1)}, s32[10,2,6]{2,1,0:T(2,128)S(1)}, u32[]{:S(2)}, u32[]{:S(2)}) %collective-permute-start.1) | collective-permute-done | bytes 512 | tf_op jit(solution)/shard_map/ppermute | solution.py:671
  19.5 1.8 %collective-permute-start.6 = (bf16[4,2,256,128]{3,2,1,0:T(8,128)(2,1)}, bf16[4,2,256,128]{3,2,1,0:T(8,128)(2,1)S(1)}, u32[]{:S(2)}, u32[]{:S(2)}) collective-permute-start(bf16[4,2,256,128]{3,2,1,0:T(8,128)(2,1)} %get-tuple-element.55), channel_id=1, source_target_pairs={{5,0},{2,1},{7,2},{0,3},{1,4},{6,5},{3,6},{4,7},{13,8},{10,9},{15,... | collective-permute-start | bytes 1572872 | tf_op jit(solution)/shard_map/ppermute | solution.py:693
  21.3 1.0 %copy-done = bf16[4,2,256,128]{3,2,1,0:T(8,128)(2,1)S(1)} copy-done((bf16[4,2,256,128]{3,2,1,0:T(8,128)(2,1)S(1)}, bf16[4,2,256,128]{3,2,1,0:T(8,128)(2,1)}, u32[]{:S(2)}) %copy-start) | copy-done | bytes 524312
  22.3 1.0 %copy-done.1 = bf16[4,2,256,128]{3,2,1,0:T(8,128)(2,1)S(1)} copy-done((bf16[4,2,256,128]{3,2,1,0:T(8,128)(2,1)S(1)}, bf16[4,2,256,128]{3,2,1,0:T(8,128)(2,1)}, u32[]{:S(2)}) %copy-start.1) | copy-done | bytes 524312
  23.3 0.9 %copy-done.2 = bf16[1,2,256,128]{3,2,1,0:T(8,128)(2,1)S(1)} copy-done((bf16[1,2,256,128]{3,2,1,0:T(8,128)(2,1)S(1)}, bf16[1,2,256,128]{3,2,1,0:T(8,128)(2,1)}, u32[]{:S(2)}) %copy-start.2) | copy-done | bytes 131096
  24.2 3.7 %tile_lists.1 = (s32[64]{0:T(128)S(1)}, s32[22]{0:T(128)S(1)}, s32[64]{0:T(128)S(1)}, s32[22]{0:T(128)S(1)}, bf16[4,2,256,128]{3,2,1,0:T(8,128)(2,1)S(1)}, /*ind...) custom-call(s32[10,1,6]{2,1,0:T(1,128)S(1)} %copy.19.refs_0_, ...), custom_call_target="tpu_custom_call" | custom-call | flops 1 | bytes 1 | tf_op jit(solution)/shard_map/tile_lists/pallas_call | solution.py:540
  28.0 2.7 %collective-permute-start.11 = (bf16[1,2,256,128]{3,2,1,0:T(8,128)(2,1)S(1)}, bf16[1,2,256,128]{3,2,1,0:T(8,128)(2,1)S(1)}, u32[]{:S(2)}, u32[]{:S(2)}) collective-permute-start(bf16[1,2,256,128]{3,2,1,0:T(8,128)(2,1)S(1)} %gate.3), channel_id=1, source_target_pairs={{5,0},{2,1},{7,2},{0,3},{1,4},{6,5},{3,6},{4,7},{13,8},{10,9},{15,... | collective-permute-start | bytes 393224 | tf_op jit(solution)/shard_map/ppermute | solution.py:693
  31.2 1.0 %collective-permute-start.9 = (bf16[1,2,256,128]{3,2,1,0:T(8,128)(2,1)S(1)}, bf16[1,2,256,128]{3,2,1,0:T(8,128)(2,1)S(1)}, u32[]{:S(2)}, u32[]{:S(2)}) collective-permute-start(bf16[1,2,256,128]{3,2,1,0:T(8,128)(2,1)S(1)} %get-tuple-element.60), channel_id=1, source_target_pairs={{3,0},{4,1},{1,2},{6,3},{7,4},{0,5},{5,6},{2,7},{11,8},{12,9},{9,1... | collective-permute-start | bytes 393224 | tf_op jit(solution)/shard_map/ppermute | solution.py:691
  32.3 5.7 %row_stats.2.refs_1_.refs_10_ = f32[4,16,256]{2,1,0:T(8,128)S(1)} custom-call(s32[64]{0:T(128)S(1)} %get-tuple-element.50.refs_0_.refs_2_, f32[5]{0:T(128)S(1)} %broadcast_select_fusion.refs_1_.refs_0_, bf16[4,2,256,128]{3,2,1,0:T(8,128)(2,1)S(1)} %get-tuple-element.51.refs_2_, bf16[5,4,256,128]{3,2,1,0:T(8,128)(2,1)S(1)} %collective-permute-done.2.refs_3_.refs_7_.refs_1_, ...), custom_call_target="tpu_custom_call" | custom-call | flops 1 | bytes 1 | tf_op jit(solution)/shard_map/row_stats/pallas_call | solution.py:232
  38.0 1.2 %collective-permute-start.7 = (f32[4,16,256]{2,1,0:T(8,128)S(1)}, f32[4,16,256]{2,1,0:T(8,128)S(1)}, u32[]{:S(2)}, u32[]{:S(2)}) collective-permute-start(f32[4,16,256]{2,1,0:T(8,128)S(1)} %row_stats.2.refs_1_.refs_10_), channel_id=1, source_target_pairs={{2,0},{5,1},{0,2},{7,3},{6,4},{1,5},{4,6},{3,7},{10,8},{13,9},{8,1... | collective-permute-start | bytes 196616 | tf_op jit(solution)/shard_map/ppermute | solution.py:704
  39.2 2.1 %row_stats.3.refs_3_.refs_10_ = f32[1,16,256]{2,1,0:T(8,128)S(1)} custom-call(s32[22]{0:T(128)S(1)} %get-tuple-element.56.refs_3_.refs_0_, f32[5]{0:T(128)S(1)} %broadcast_select_fusion.refs_1_.refs_0_, bf16[1,2,256,128]{3,2,1,0:T(8,128)(2,1)S(1)} %get-tuple-element.57.refs_2_, bf16[5,4,256,128]{3,2,1,0:T(8,128)(2,1)S(1)} %collective-permute-done.2.refs_3_.refs_7_.refs_1_, ...), custom_call_target="tpu_custom_call" | custom-call | flops 1 | bytes 1 | tf_op jit(solution)/shard_map/row_stats/pallas_call | solution.py:232
  41.3 1.0 %collective-permute-start.12 = (f32[1,16,256]{2,1,0:T(8,128)S(1)}, f32[1,16,256]{2,1,0:T(8,128)S(1)}, u32[]{:S(2)}, u32[]{:S(2)}) collective-permute-start(f32[1,16,256]{2,1,0:T(8,128)S(1)} %row_stats.3.refs_3_.refs_10_), channel_id=1, source_target_pairs={{2,0},{5,1},{0,2},{7,3},{6,4},{1,5},{4,6},{3,7},{10,8},{13,9},{8,1... | collective-permute-start | bytes 49160 | tf_op jit(solution)/shard_map/ppermute | solution.py:704
  42.3 9.0 %gradients.2 = (f32[4,256,128]{2,1,0:T(8,128)S(1)}, f32[4,2,256,128]{3,2,1,0:T(8,128)S(1)}, bf16[3072,128]{1,0:T(8,128)(2,1)S(1)}, bf16[1024,128]{1,0:T(8,128)(2...) custom-call(s32[64]{0:T(128)S(1)} %get-tuple-element.64.refs_4_.refs_0_, ...), custom_call_target="tpu_custom_call" | custom-call | flops 16000000000 | bytes 1 | tf_op jit(solution)/shard_map/gradients/pallas_call | solution.py:390
  51.3 2.0 %collective-permute-start.16 = (bf16[2048,128]{1,0:T(8,128)(2,1)S(1)}, bf16[2048,128]{1,0:T(8,128)(2,1)S(1)}, u32[]{:S(2)}, u32[]{:S(2)}) collective-permute-start(bf16[2048,128]{1,0:T(8,128)(2,1)S(1)} %get-tuple-element.72), channel_id=1, source_target_pairs={{0,4},{1,3},{2,6},{3,1},{4,0},{5,7},{6,2},{7,5},{8,12},{9,11},{10,... | collective-permute-start | bytes 1572872 | tf_op jit(solution)/shard_map/ppermute | solution.py:736
  53.3 1.2 %collective-permute-start.17 = (bf16[2048,128]{1,0:T(8,128)(2,1)S(1)}, bf16[2048,128]{1,0:T(8,128)(2,1)S(1)}, u32[]{:S(2)}, u32[]{:S(2)}) collective-permute-start(bf16[2048,128]{1,0:T(8,128)(2,1)S(1)} %get-tuple-element.73), channel_id=1, source_target_pairs={{0,5},{1,2},{2,7},{3,0},{4,1},{5,6},{6,3},{7,4},{8,13},{9,10},{10,... | collective-permute-start | bytes 1572872 | tf_op jit(solution)/shard_map/ppermute | solution.py:736
  54.5 0.8 sink_terms.1.refs_15_
  55.3 1.6 %collective-permute-start.13 = (f32[4,128]{1,0:T(4,128)S(1)}, f32[4,128]{1,0:T(4,128)S(1)}, u32[]{:S(2)}, u32[]{:S(2)}) collective-permute-start(f32[4,128]{1,0:T(4,128)S(1)} %sink_terms.1.refs_15_), channel_id=1, source_target_pairs={{0,8},{8,16},{16,24},{24,0},{1,9},{9,17},{17,25},{25,1},{2,10},{10... | collective-permute-start | bytes 6152 | tf_op jit(solution)/shard_map/ppermute | solution.py:644
  56.9 2.6 %collective-permute-start.14 = (f32[4,128]{1,0:T(4,128)S(1)}, f32[4,128]{1,0:T(4,128)S(1)}, u32[]{:S(2)}, u32[]{:S(2)}) collective-permute-start(f32[4,128]{1,0:T(4,128)S(1)} %sink_terms.1.refs_15_), channel_id=1, source_target_pairs={{0,16},{8,24},{16,0},{24,8},{1,17},{9,25},{17,1},{25,9},{2,18},{10... | collective-permute-start | bytes 6152 | tf_op jit(solution)/shard_map/ppermute | solution.py:644
  59.5 1.4 %collective-permute-start.15 = (f32[4,128]{1,0:T(4,128)S(1)}, f32[4,128]{1,0:T(4,128)S(1)}, u32[]{:S(2)}, u32[]{:S(2)}) collective-permute-start(f32[4,128]{1,0:T(4,128)S(1)} %sink_terms.1.refs_15_), channel_id=1, source_target_pairs={{0,24},{8,0},{16,8},{24,16},{1,25},{9,1},{17,9},{25,17},{2,26},{10... | collective-permute-start | bytes 6152 | tf_op jit(solution)/shard_map/ppermute | solution.py:644
  60.9 3.1 %gradients.3 = (f32[1,256,128]{2,1,0:T(8,128)S(1)}, f32[1,2,256,128]{3,2,1,0:T(8,128)S(1)}, bf16[3856,128]{1,0:T(8,128)(2,1)S(1)}, bf16[1280,128]{1,0:T(8,128)(2...) custom-call(s32[22]{0:T(128)S(1)} %get-tuple-element.65.refs_5_.refs_0_, ...), custom_call_target="tpu_custom_call" | custom-call | flops 4000000000 | bytes 1 | tf_op jit(solution)/shard_map/gradients/pallas_call | solution.py:390
  64.0 1.8 %collective-permute-done.17.refs_4_.refs_7_ = bf16[2048,128]{1,0:T(8,128)(2,1)S(1)} collective-permute-done((bf16[2048,128]{1,0:T(8,128)(2,1)S(1)}, bf16[2048,128]{1,0:T(8,128)(2,1)S(1)}, u32[]{:S(2)}, u32[]{:S(2)}) %collective-permute-start.17) | collective-permute-done | bytes 524320 | tf_op jit(solution)/shard_map/ppermute | solution.py:736
  66.1 1.4 %collective-permute-start.19 = (bf16[1280,128]{1,0:T(8,128)(2,1)S(1)}, bf16[1280,128]{1,0:T(8,128)(2,1)S(1)}, u32[]{:S(2)}, u32[]{:S(2)}) collective-permute-start(bf16[1280,128]{1,0:T(8,128)(2,1)S(1)} %get-tuple-element.76), channel_id=1, source_target_pairs={{0,2},{1,5},{2,0},{3,7},{4,6},{5,1},{6,4},{7,3},{8,10},{9,13},{10,... | collective-permute-start | bytes 983048 | tf_op jit(solution)/shard_map/ppermute | solution.py:741
  67.5 1.4 %collective-permute-start.20 = (bf16[1280,128]{1,0:T(8,128)(2,1)S(1)}, bf16[1280,128]{1,0:T(8,128)(2,1)S(1)}, u32[]{:S(2)}, u32[]{:S(2)}) collective-permute-start(bf16[1280,128]{1,0:T(8,128)(2,1)S(1)} %get-tuple-element.77), channel_id=1, source_target_pairs={{0,3},{1,4},{2,1},{3,6},{4,7},{5,0},{6,5},{7,2},{8,11},{9,12},{10,... | collective-permute-start | bytes 983048 | tf_op jit(solution)/shard_map/ppermute | solution.py:741
  69.6 4.8 %collective-permute-done.19.refs_2_ = bf16[1280,128]{1,0:T(8,128)(2,1)S(1)} collective-permute-done((bf16[1280,128]{1,0:T(8,128)(2,1)S(1)}, bf16[1280,128]{1,0:T(8,128)(2,1)S(1)}, u32[]{:S(2)}, u32[]{:S(2)}) %collective-permute-start.19) | collective-permute-done | bytes 327712 | tf_op jit(solution)/shard_map/ppermute | solution.py:741
  74.3 4.6 %collective-permute-done.20.refs_3_ = bf16[1280,128]{1,0:T(8,128)(2,1)S(1)} collective-permute-done((bf16[1280,128]{1,0:T(8,128)(2,1)S(1)}, bf16[1280,128]{1,0:T(8,128)(2,1)S(1)}, u32[]{:S(2)}, u32[]{:S(2)}) %collective-permute-start.20) | collective-permute-done | bytes 327712 | tf_op jit(solution)/shard_map/ppermute | solution.py:741
  79.0 1.8 %closing_sums.1 = (bf16[1,256,1280]{2,1,0:T(8,128)(2,1)}, bf16[1,256,1280]{2,1,0:T(8,128)(2,1)}, bf16[1,256,1280]{2,1,0:T(8,128)(2,1)}, f32[1,10]{1,0:T(1,128)}) custom-call(f32[8,128]{1,0:T(8,128)S(1)} %get-tuple-element.74.refs_0_, bf16[3856,128]{1,0:T(8,128)(2,1)S(1)} %collective-permute-done.18.refs_1_, ...), custom_call_target="tpu_custom_call" | custom-call | flops 1 | bytes 1 | tf_op jit(solution)/shard_map/closing_sums/pallas_call | solution.py:462
  (44 shorter events, 2.3 us)
Async XLA Ops:
  0.6 8.3 %copy-start.5 = (s32[10,1,6]{0,1,2:T(1,128)S(1)}, s32[10,1,6]{0,1,2:T(1,128)}, u32[]{:S(2)}) copy-start(s32[10,1,6]{0,1,2:T(1,128)} %param.10) | copy-start | bytes 724
  4.3 23.6 %collective-permute-start.2 = (bf16[5,4,256,128]{3,2,1,0:T(8,128)(2,1)}, bf16[5,4,256,128]{3,2,1,0:T(8,128)(2,1)S(1)}, u32[]{:S(2)}, u32[]{:S(2)}) collective-permute-start(bf16[5,4,256,128]{3,2,1,0:T(8,128)(2,1)} %get-tuple-element.52), channel_id=1, source_target_pairs={{1,0},{0,1},{3,2},{2,3},{5,4},{4,5},{7,6},{6,7},{9,8},{8,9},{11,10... | collective-permute-start | bytes 3932168 | tf_op jit(solution)/shard_map/ppermute | solution.py:681
  4.8 25.8 %collective-permute-start.3 = (bf16[4,2,256,128]{3,2,1,0:T(8,128)(2,1)}, bf16[4,2,256,128]{3,2,1,0:T(8,128)(2,1)S(1)}, u32[]{:S(2)}, u32[]{:S(2)}) collective-permute-start(bf16[4,2,256,128]{3,2,1,0:T(8,128)(2,1)} %get-tuple-element.46.refs_4_), channel_id=1, source_target_pairs={{2,0},{5,1},{0,2},{7,3},{6,4},{1,5},{4,6},{3,7},{10,8},{13,9},{8,1... | collective-permute-start | bytes 1572872 | tf_op jit(solution)/shard_map/ppermute | solution.py:691
  7.4 23.3 %collective-permute-start.5 = (bf16[4,2,256,128]{3,2,1,0:T(8,128)(2,1)}, bf16[4,2,256,128]{3,2,1,0:T(8,128)(2,1)S(1)}, u32[]{:S(2)}, u32[]{:S(2)}) collective-permute-start(bf16[4,2,256,128]{3,2,1,0:T(8,128)(2,1)} %get-tuple-element.47.refs_5_), channel_id=1, source_target_pairs={{4,0},{3,1},{6,2},{1,3},{0,4},{7,5},{2,6},{5,7},{12,8},{11,9},{14,... | collective-permute-start | bytes 1572872 | tf_op jit(solution)/shard_map/ppermute | solution.py:693
  8.9 22.3 %collective-permute-start.4 = (bf16[4,2,256,128]{3,2,1,0:T(8,128)(2,1)}, bf16[4,2,256,128]{3,2,1,0:T(8,128)(2,1)S(1)}, u32[]{:S(2)}, u32[]{:S(2)}) collective-permute-start(bf16[4,2,256,128]{3,2,1,0:T(8,128)(2,1)} %get-tuple-element.53), channel_id=1, source_target_pairs={{3,0},{4,1},{1,2},{6,3},{7,4},{0,5},{5,6},{2,7},{11,8},{12,9},{9,1... | collective-permute-start | bytes 1572872 | tf_op jit(solution)/shard_map/ppermute | solution.py:691
  9.0 1.5 %collective-permute-start = (s32[10,1,6]{2,1,0:T(1,128)S(1)}, s32[10,1,6]{2,1,0:T(1,128)S(1)}, u32[]{:S(2)}, u32[]{:S(2)}) collective-permute-start(s32[10,1,6]{2,1,0:T(1,128)S(1)} %copy.19.refs_0_), channel_id=1, source_target_pairs={{1,0},{0,1},{3,2},{2,3},{5,4},{4,5},{7,6},{6,7},{9,8},{8,9},{11,10... | collective-permute-start | bytes 728 | tf_op jit(solution)/shard_map/ppermute | solution.py:667
  10.5 9.0 %collective-permute-start.1 = (s32[10,2,6]{2,1,0:T(2,128)S(1)}, s32[10,2,6]{2,1,0:T(2,128)S(1)}, u32[]{:S(2)}, u32[]{:S(2)}) collective-permute-start(s32[10,2,6]{2,1,0:T(2,128)S(1)} %pad_add_fusion), channel_id=1, source_target_pairs={{2,0},{5,1},{0,2},{7,3},{6,4},{1,5},{4,6},{3,7},{10,8},{13,9},{8,1... | collective-permute-start | bytes 1448 | tf_op jit(solution)/shard_map/ppermute | solution.py:671
  19.5 12.8 %collective-permute-start.6 = (bf16[4,2,256,128]{3,2,1,0:T(8,128)(2,1)}, bf16[4,2,256,128]{3,2,1,0:T(8,128)(2,1)S(1)}, u32[]{:S(2)}, u32[]{:S(2)}) collective-permute-start(bf16[4,2,256,128]{3,2,1,0:T(8,128)(2,1)} %get-tuple-element.55), channel_id=1, source_target_pairs={{5,0},{2,1},{7,2},{0,3},{1,4},{6,5},{3,6},{4,7},{13,8},{10,9},{15,... | collective-permute-start | bytes 1572872 | tf_op jit(solution)/shard_map/ppermute | solution.py:693
  21.2 1.0 %copy-start = (bf16[4,2,256,128]{3,2,1,0:T(8,128)(2,1)S(1)}, bf16[4,2,256,128]{3,2,1,0:T(8,128)(2,1)}, u32[]{:S(2)}) copy-start(bf16[4,2,256,128]{3,2,1,0:T(8,128)(2,1)} %get-tuple-element.47.refs_5_) | copy-start | bytes 1572868
  22.3 1.0 %copy-start.1 = (bf16[4,2,256,128]{3,2,1,0:T(8,128)(2,1)S(1)}, bf16[4,2,256,128]{3,2,1,0:T(8,128)(2,1)}, u32[]{:S(2)}) copy-start(bf16[4,2,256,128]{3,2,1,0:T(8,128)(2,1)} %get-tuple-element.46.refs_4_) | copy-start | bytes 1572868
  23.3 0.9 %copy-start.2 = (bf16[1,2,256,128]{3,2,1,0:T(8,128)(2,1)S(1)}, bf16[1,2,256,128]{3,2,1,0:T(8,128)(2,1)}, u32[]{:S(2)}) copy-start(bf16[1,2,256,128]{3,2,1,0:T(8,128)(2,1)} %get-tuple-element.49.refs_7_.refs_1_) | copy-start | bytes 393220
  24.2 3.7 %copy-start.3 = (bf16[1,2,256,128]{3,2,1,0:T(8,128)(2,1)S(1)}, bf16[1,2,256,128]{3,2,1,0:T(8,128)(2,1)}, u32[]{:S(2)}) copy-start(bf16[1,2,256,128]{3,2,1,0:T(8,128)(2,1)} %get-tuple-element.63.refs_0_) | copy-start | bytes 393220
  24.2 6.4 %copy-start.4 = (bf16[1,2,256,128]{3,2,1,0:T(8,128)(2,1)S(1)}, bf16[1,2,256,128]{3,2,1,0:T(8,128)(2,1)}, u32[]{:S(2)}) copy-start(bf16[1,2,256,128]{3,2,1,0:T(8,128)(2,1)} %get-tuple-element.58.refs_2_) | copy-start | bytes 393220
  27.9 4.3 %copy-start.6 = (f32[10]{0:T(128)S(1)}, f32[10]{0:T(128)}, u32[]{:S(2)}) copy-start(f32[10]{0:T(128)} %param.11) | copy-start | bytes 124
  28.0 11.2 %collective-permute-start.11 = (bf16[1,2,256,128]{3,2,1,0:T(8,128)(2,1)S(1)}, bf16[1,2,256,128]{3,2,1,0:T(8,128)(2,1)S(1)}, u32[]{:S(2)}, u32[]{:S(2)}) collective-permute-start(bf16[1,2,256,128]{3,2,1,0:T(8,128)(2,1)S(1)} %gate.3), channel_id=1, source_target_pairs={{5,0},{2,1},{7,2},{0,3},{1,4},{6,5},{3,6},{4,7},{13,8},{10,9},{15,... | collective-permute-start | bytes 393224 | tf_op jit(solution)/shard_map/ppermute | solution.py:693
  30.6 8.5 %collective-permute-start.10 = (bf16[1,2,256,128]{3,2,1,0:T(8,128)(2,1)S(1)}, bf16[1,2,256,128]{3,2,1,0:T(8,128)(2,1)S(1)}, u32[]{:S(2)}, u32[]{:S(2)}) collective-permute-start(bf16[1,2,256,128]{3,2,1,0:T(8,128)(2,1)S(1)} %get-tuple-element.62), channel_id=1, source_target_pairs={{4,0},{3,1},{6,2},{1,3},{0,4},{7,5},{2,6},{5,7},{12,8},{11,9},{14,... | collective-permute-start | bytes 393224 | tf_op jit(solution)/shard_map/ppermute | solution.py:693
  30.7 8.5 %collective-permute-start.8 = (bf16[1,2,256,128]{3,2,1,0:T(8,128)(2,1)}, bf16[1,2,256,128]{3,2,1,0:T(8,128)(2,1)S(1)}, u32[]{:S(2)}, u32[]{:S(2)}) collective-permute-start(bf16[1,2,256,128]{3,2,1,0:T(8,128)(2,1)} %get-tuple-element.59), channel_id=1, source_target_pairs={{2,0},{5,1},{0,2},{7,3},{6,4},{1,5},{4,6},{3,7},{10,8},{13,9},{8,1... | collective-permute-start | bytes 393224 | tf_op jit(solution)/shard_map/ppermute | solution.py:691
  31.2 8.0 %collective-permute-start.9 = (bf16[1,2,256,128]{3,2,1,0:T(8,128)(2,1)S(1)}, bf16[1,2,256,128]{3,2,1,0:T(8,128)(2,1)S(1)}, u32[]{:S(2)}, u32[]{:S(2)}) collective-permute-start(bf16[1,2,256,128]{3,2,1,0:T(8,128)(2,1)S(1)} %get-tuple-element.60), channel_id=1, source_target_pairs={{3,0},{4,1},{1,2},{6,3},{7,4},{0,5},{5,6},{2,7},{11,8},{12,9},{9,1... | collective-permute-start | bytes 393224 | tf_op jit(solution)/shard_map/ppermute | solution.py:691
  38.0 4.3 %collective-permute-start.7 = (f32[4,16,256]{2,1,0:T(8,128)S(1)}, f32[4,16,256]{2,1,0:T(8,128)S(1)}, u32[]{:S(2)}, u32[]{:S(2)}) collective-permute-start(f32[4,16,256]{2,1,0:T(8,128)S(1)} %row_stats.2.refs_1_.refs_10_), channel_id=1, source_target_pairs={{2,0},{5,1},{0,2},{7,3},{6,4},{1,5},{4,6},{3,7},{10,8},{13,9},{8,1... | collective-permute-start | bytes 196616 | tf_op jit(solution)/shard_map/ppermute | solution.py:704
  41.3 13.2 %collective-permute-start.12 = (f32[1,16,256]{2,1,0:T(8,128)S(1)}, f32[1,16,256]{2,1,0:T(8,128)S(1)}, u32[]{:S(2)}, u32[]{:S(2)}) collective-permute-start(f32[1,16,256]{2,1,0:T(8,128)S(1)} %row_stats.3.refs_3_.refs_10_), channel_id=1, source_target_pairs={{2,0},{5,1},{0,2},{7,3},{6,4},{1,5},{4,6},{3,7},{10,8},{13,9},{8,1... | collective-permute-start | bytes 49160 | tf_op jit(solution)/shard_map/ppermute | solution.py:704
  51.3 12.7 %collective-permute-start.16 = (bf16[2048,128]{1,0:T(8,128)(2,1)S(1)}, bf16[2048,128]{1,0:T(8,128)(2,1)S(1)}, u32[]{:S(2)}, u32[]{:S(2)}) collective-permute-start(bf16[2048,128]{1,0:T(8,128)(2,1)S(1)} %get-tuple-element.72), channel_id=1, source_target_pairs={{0,4},{1,3},{2,6},{3,1},{4,0},{5,7},{6,2},{7,5},{8,12},{9,11},{10,... | collective-permute-start | bytes 1572872 | tf_op jit(solution)/shard_map/ppermute | solution.py:736
  53.3 12.5 %collective-permute-start.17 = (bf16[2048,128]{1,0:T(8,128)(2,1)S(1)}, bf16[2048,128]{1,0:T(8,128)(2,1)S(1)}, u32[]{:S(2)}, u32[]{:S(2)}) collective-permute-start(bf16[2048,128]{1,0:T(8,128)(2,1)S(1)} %get-tuple-element.73), channel_id=1, source_target_pairs={{0,5},{1,2},{2,7},{3,0},{4,1},{5,6},{6,3},{7,4},{8,13},{9,10},{10,... | collective-permute-start | bytes 1572872 | tf_op jit(solution)/shard_map/ppermute | solution.py:736
  55.3 8.7 %collective-permute-start.13 = (f32[4,128]{1,0:T(4,128)S(1)}, f32[4,128]{1,0:T(4,128)S(1)}, u32[]{:S(2)}, u32[]{:S(2)}) collective-permute-start(f32[4,128]{1,0:T(4,128)S(1)} %sink_terms.1.refs_15_), channel_id=1, source_target_pairs={{0,8},{8,16},{16,24},{24,0},{1,9},{9,17},{17,25},{25,1},{2,10},{10... | collective-permute-start | bytes 6152 | tf_op jit(solution)/shard_map/ppermute | solution.py:644
  56.9 7.1 %collective-permute-start.14 = (f32[4,128]{1,0:T(4,128)S(1)}, f32[4,128]{1,0:T(4,128)S(1)}, u32[]{:S(2)}, u32[]{:S(2)}) collective-permute-start(f32[4,128]{1,0:T(4,128)S(1)} %sink_terms.1.refs_15_), channel_id=1, source_target_pairs={{0,16},{8,24},{16,0},{24,8},{1,17},{9,25},{17,1},{25,9},{2,18},{10... | collective-permute-start | bytes 6152 | tf_op jit(solution)/shard_map/ppermute | solution.py:644
  59.5 4.5 %collective-permute-start.15 = (f32[4,128]{1,0:T(4,128)S(1)}, f32[4,128]{1,0:T(4,128)S(1)}, u32[]{:S(2)}, u32[]{:S(2)}) collective-permute-start(f32[4,128]{1,0:T(4,128)S(1)} %sink_terms.1.refs_15_), channel_id=1, source_target_pairs={{0,24},{8,0},{16,8},{24,16},{1,25},{9,1},{17,9},{25,17},{2,26},{10... | collective-permute-start | bytes 6152 | tf_op jit(solution)/shard_map/ppermute | solution.py:644
  65.9 13.1 %collective-permute-start.18 = (bf16[3856,128]{1,0:T(8,128)(2,1)S(1)}, bf16[3856,128]{1,0:T(8,128)(2,1)S(1)}, u32[]{:S(2)}, u32[]{:S(2)}) collective-permute-start(bf16[3856,128]{1,0:T(8,128)(2,1)S(1)} %get-tuple-element.75), channel_id=1, source_target_pairs={{1,0},{0,1},{3,2},{2,3},{5,4},{4,5},{7,6},{6,7},{9,8},{8,9},{11,10... | collective-permute-start | bytes 2961416 | tf_op jit(solution)/shard_map/ppermute | solution.py:744
  66.1 8.2 %collective-permute-start.19 = (bf16[1280,128]{1,0:T(8,128)(2,1)S(1)}, bf16[1280,128]{1,0:T(8,128)(2,1)S(1)}, u32[]{:S(2)}, u32[]{:S(2)}) collective-permute-start(bf16[1280,128]{1,0:T(8,128)(2,1)S(1)} %get-tuple-element.76), channel_id=1, source_target_pairs={{0,2},{1,5},{2,0},{3,7},{4,6},{5,1},{6,4},{7,3},{8,10},{9,13},{10,... | collective-permute-start | bytes 983048 | tf_op jit(solution)/shard_map/ppermute | solution.py:741
  67.5 11.4 %collective-permute-start.20 = (bf16[1280,128]{1,0:T(8,128)(2,1)S(1)}, bf16[1280,128]{1,0:T(8,128)(2,1)S(1)}, u32[]{:S(2)}, u32[]{:S(2)}) collective-permute-start(bf16[1280,128]{1,0:T(8,128)(2,1)S(1)} %get-tuple-element.77), channel_id=1, source_target_pairs={{0,3},{1,4},{2,1},{3,6},{4,7},{5,0},{6,5},{7,2},{8,11},{9,12},{10,... | collective-permute-start | bytes 983048 | tf_op jit(solution)/shard_map/ppermute | solution.py:741
  68.9 10.0 %collective-permute-start.21 = (bf16[528,128]{1,0:T(8,128)(2,1)S(1)}, bf16[528,128]{1,0:T(8,128)(2,1)S(1)}, u32[]{:S(2)}, u32[]{:S(2)}) collective-permute-start(bf16[528,128]{1,0:T(8,128)(2,1)S(1)} %get-tuple-element.82), channel_id=1, source_target_pairs={{0,4},{1,3},{2,6},{3,1},{4,0},{5,7},{6,2},{7,5},{8,12},{9,11},{10,... | collective-permute-start | bytes 405512 | tf_op jit(solution)/shard_map/ppermute | solution.py:736
  69.3 9.7 %collective-permute-start.22 = (bf16[528,128]{1,0:T(8,128)(2,1)S(1)}, bf16[528,128]{1,0:T(8,128)(2,1)S(1)}, u32[]{:S(2)}, u32[]{:S(2)}) collective-permute-start(bf16[528,128]{1,0:T(8,128)(2,1)S(1)} %get-tuple-element.83), channel_id=1, source_target_pairs={{0,5},{1,2},{2,7},{3,0},{4,1},{5,6},{6,3},{7,4},{8,13},{9,10},{10,... | collective-permute-start | bytes 405512 | tf_op jit(solution)/shard_map/ppermute | solution.py:736

commit v6 on v5

--- a/solution.py
+++ b/solution.py
@@ -448,8 +448,8 @@
     half_heads = half // BLOCK
     _, at_query, at_key = coordinates(side)
     far = refs[per * len(sizes) - 2 * (side - 1) : per * len(sizes)]
-    mine = [sums_ref[0:1, :]] + [get_terms(ref) for ref in far[0::2]]
-    other = [get_terms(from_core)] + [get_terms(ref) for ref in far[1::2]]
+    mine = [sums_ref[0:1, :]] + [get_terms(ref) for ref in reversed(far[0::2])]
+    other = [get_terms(from_core)] + [get_terms(ref) for ref in reversed(far[1::2])]
     mine, other = sum(ordered(mine, at_key, side)), sum(ordered(other, at_query, side))
     low = jnp.where(core == 0, mine, other)
     high = pltpu.roll(jnp.where(core == 0, other, mine), half_heads, 1)

time: 81.3 us -> 81.1 us (level)
  no operation moved by 1% of the time
where the time goes in v6:
time: 81.1 us; the launch traced here: 80.8 us
  Pallas kernels  29.8 us (37%)
  starting transfers between devices  27.4 us (34%)
  waiting for transfers between devices  19.6 us (24%)
  local copies, waits for them, and re-layouts  3.1 us (4%)
  between operations  0.83 us (1%)
    pallas_call x2, Pallas kernels, grads(): pl.pallas_call(lambda *refs: grads_kernel(spans, slots, side, scaling, jo...  12.1 us
    ppermute x2, waiting for transfers between devices, body(): lax.ppermute(value, 'ctx', return_perm(groups, side, True, shift, cross))  9.39 us
    pallas_call x2, Pallas kernels, stats(): pl.pallas_call(lambda *refs: stats_kernel(first, heads, slots, scaling, *...  7.75 us
    ppermute x1, waiting for transfers between devices, body(): came = lax.ppermute(pair, 'ctx', gather_perm(groups, side, True, shift, 0))  7.4 us
    ppermute x4, starting transfers between devices, body(): kv.append(lax.ppermute(kv_oth if cross else kv_own, 'ctx', perm))  5.97 us
    ppermute x3, starting transfers between devices, sink_round(): return sum([lax.ppermute(held, axis, perm) for perm in perms], held)  5.57 us
    ppermute x4, starting transfers between devices, body(): qd.append(lax.ppermute(qd_oth if cross else qd_own, 'ctx', perm))  4.12 us
    ppermute x4, starting transfers between devices, body(): lax.ppermute(value, 'ctx', return_perm(groups, side, False, shift, cross))  3.84 us
  transfers between devices with their start and end apart: 23, of which 6 were waited for; matrix products, arithmetic and copies ran while one was open for 0% of the time, Pallas kernels for 30%

profile of v6, /device:TPU:0, one launch (start us, length us, event | category | flops | bytes accessed | tf_op | source)
XLA Modules:
  0.0 80.8 jit_solution(14342253769405945630)
XLA Ops:
  0.6 3.7 %pack.1 = (bf16[4,2,256,128]{3,2,1,0:T(8,128)(2,1)}, bf16[4,2,256,128]{3,2,1,0:T(8,128)(2,1)}, bf16[4,2,256,128]{3,2,1,0:T(8,128)(2,1)}, bf16[4,2,256,128]{3,2,1...) custom-call(bf16[1,256,1280]{2,1,0:T(8,128)(2,1)} %refs_0_.2, ...), custom_call_target="tpu_custom_call" | custom-call | flops 4000000000 | bytes 1 | tf_op jit(solution)/shard_map/pack/pallas_call | solution.py:118
  4.8 2.6 %collective-permute-start.3 = (bf16[4,2,256,128]{3,2,1,0:T(8,128)(2,1)}, bf16[4,2,256,128]{3,2,1,0:T(8,128)(2,1)S(1)}, u32[]{:S(2)}, u32[]{:S(2)}) collective-permute-start(bf16[4,2,256,128]{3,2,1,0:T(8,128)(2,1)} %get-tuple-element.46.refs_4_), channel_id=1, source_target_pairs={{2,0},{5,1},{0,2},{7,3},{6,4},{1,5},{4,6},{3,7},{10,8},{13,9},{8,1... | collective-permute-start | bytes 1572872 | tf_op jit(solution)/shard_map/ppermute | solution.py:691
  7.4 1.5 %collective-permute-start.5 = (bf16[4,2,256,128]{3,2,1,0:T(8,128)(2,1)}, bf16[4,2,256,128]{3,2,1,0:T(8,128)(2,1)S(1)}, u32[]{:S(2)}, u32[]{:S(2)}) collective-permute-start(bf16[4,2,256,128]{3,2,1,0:T(8,128)(2,1)} %get-tuple-element.47.refs_5_), channel_id=1, source_target_pairs={{4,0},{3,1},{6,2},{1,3},{0,4},{7,5},{2,6},{5,7},{12,8},{11,9},{14,... | collective-permute-start | bytes 1572872 | tf_op jit(solution)/shard_map/ppermute | solution.py:693
  9.0 0.6 collective-permute-start
  9.7 0.8 %collective-permute-done.refs_1_ = s32[10,1,6]{2,1,0:T(1,128)S(1)} collective-permute-done((s32[10,1,6]{2,1,0:T(1,128)S(1)}, s32[10,1,6]{2,1,0:T(1,128)S(1)}, u32[]{:S(2)}, u32[]{:S(2)}) %collective-permute-start) | collective-permute-done | bytes 272 | tf_op jit(solution)/shard_map/ppermute | solution.py:667
  10.5 1.6 %collective-permute-start.1 = (s32[10,2,6]{2,1,0:T(2,128)S(1)}, s32[10,2,6]{2,1,0:T(2,128)S(1)}, u32[]{:S(2)}, u32[]{:S(2)}) collective-permute-start(s32[10,2,6]{2,1,0:T(2,128)S(1)} %pad_add_fusion), channel_id=1, source_target_pairs={{2,0},{5,1},{0,2},{7,3},{6,4},{1,5},{4,6},{3,7},{10,8},{13,9},{8,1... | collective-permute-start | bytes 1448 | tf_op jit(solution)/shard_map/ppermute | solution.py:671
  12.1 7.4 %collective-permute-done.1 = s32[10,2,6]{2,1,0:T(2,128)S(1)} collective-permute-done((s32[10,2,6]{2,1,0:T(2,128)S(1)}, s32[10,2,6]{2,1,0:T(2,128)S(1)}, u32[]{:S(2)}, u32[]{:S(2)}) %collective-permute-start.1) | collective-permute-done | bytes 512 | tf_op jit(solution)/shard_map/ppermute | solution.py:671
  19.5 1.8 %collective-permute-start.6 = (bf16[4,2,256,128]{3,2,1,0:T(8,128)(2,1)}, bf16[4,2,256,128]{3,2,1,0:T(8,128)(2,1)S(1)}, u32[]{:S(2)}, u32[]{:S(2)}) collective-permute-start(bf16[4,2,256,128]{3,2,1,0:T(8,128)(2,1)} %get-tuple-element.55), channel_id=1, source_target_pairs={{5,0},{2,1},{7,2},{0,3},{1,4},{6,5},{3,6},{4,7},{13,8},{10,9},{15,... | collective-permute-start | bytes 1572872 | tf_op jit(solution)/shard_map/ppermute | solution.py:693
  21.3 1.0 %copy-done = bf16[4,2,256,128]{3,2,1,0:T(8,128)(2,1)S(1)} copy-done((bf16[4,2,256,128]{3,2,1,0:T(8,128)(2,1)S(1)}, bf16[4,2,256,128]{3,2,1,0:T(8,128)(2,1)}, u32[]{:S(2)}) %copy-start) | copy-done | bytes 524312
  22.3 1.0 %copy-done.1 = bf16[4,2,256,128]{3,2,1,0:T(8,128)(2,1)S(1)} copy-done((bf16[4,2,256,128]{3,2,1,0:T(8,128)(2,1)S(1)}, bf16[4,2,256,128]{3,2,1,0:T(8,128)(2,1)}, u32[]{:S(2)}) %copy-start.1) | copy-done | bytes 524312
  23.3 0.9 %copy-done.2 = bf16[1,2,256,128]{3,2,1,0:T(8,128)(2,1)S(1)} copy-done((bf16[1,2,256,128]{3,2,1,0:T(8,128)(2,1)S(1)}, bf16[1,2,256,128]{3,2,1,0:T(8,128)(2,1)}, u32[]{:S(2)}) %copy-start.2) | copy-done | bytes 131096
  24.2 3.7 %tile_lists.1 = (s32[64]{0:T(128)S(1)}, s32[22]{0:T(128)S(1)}, s32[64]{0:T(128)S(1)}, s32[22]{0:T(128)S(1)}, bf16[4,2,256,128]{3,2,1,0:T(8,128)(2,1)S(1)}, /*ind...) custom-call(s32[10,1,6]{2,1,0:T(1,128)S(1)} %copy.19.refs_0_, ...), custom_call_target="tpu_custom_call" | custom-call | flops 1 | bytes 1 | tf_op jit(solution)/shard_map/tile_lists/pallas_call | solution.py:540
  28.0 2.7 %collective-permute-start.11 = (bf16[1,2,256,128]{3,2,1,0:T(8,128)(2,1)S(1)}, bf16[1,2,256,128]{3,2,1,0:T(8,128)(2,1)S(1)}, u32[]{:S(2)}, u32[]{:S(2)}) collective-permute-start(bf16[1,2,256,128]{3,2,1,0:T(8,128)(2,1)S(1)} %gate.3), channel_id=1, source_target_pairs={{5,0},{2,1},{7,2},{0,3},{1,4},{6,5},{3,6},{4,7},{13,8},{10,9},{15,... | collective-permute-start | bytes 393224 | tf_op jit(solution)/shard_map/ppermute | solution.py:693
  30.7 0.5 collective-permute-start.8
  31.2 1.0 %collective-permute-start.9 = (bf16[1,2,256,128]{3,2,1,0:T(8,128)(2,1)S(1)}, bf16[1,2,256,128]{3,2,1,0:T(8,128)(2,1)S(1)}, u32[]{:S(2)}, u32[]{:S(2)}) collective-permute-start(bf16[1,2,256,128]{3,2,1,0:T(8,128)(2,1)S(1)} %get-tuple-element.60), channel_id=1, source_target_pairs={{3,0},{4,1},{1,2},{6,3},{7,4},{0,5},{5,6},{2,7},{11,8},{12,9},{9,1... | collective-permute-start | bytes 393224 | tf_op jit(solution)/shard_map/ppermute | solution.py:691
  32.3 5.7 %row_stats.2.refs_1_.refs_10_ = f32[4,16,256]{2,1,0:T(8,128)S(1)} custom-call(s32[64]{0:T(128)S(1)} %get-tuple-element.50.refs_0_.refs_2_, f32[5]{0:T(128)S(1)} %broadcast_select_fusion.refs_1_.refs_0_, bf16[4,2,256,128]{3,2,1,0:T(8,128)(2,1)S(1)} %get-tuple-element.51.refs_2_, bf16[5,4,256,128]{3,2,1,0:T(8,128)(2,1)S(1)} %collective-permute-done.2.refs_3_.refs_7_.refs_1_, ...), custom_call_target="tpu_custom_call" | custom-call | flops 1 | bytes 1 | tf_op jit(solution)/shard_map/row_stats/pallas_call | solution.py:232
  38.5 2.1 %row_stats.3.refs_3_.refs_10_ = f32[1,16,256]{2,1,0:T(8,128)S(1)} custom-call(s32[22]{0:T(128)S(1)} %get-tuple-element.56.refs_3_.refs_0_, f32[5]{0:T(128)S(1)} %broadcast_select_fusion.refs_1_.refs_0_, bf16[1,2,256,128]{3,2,1,0:T(8,128)(2,1)S(1)} %get-tuple-element.57.refs_2_, bf16[5,4,256,128]{3,2,1,0:T(8,128)(2,1)S(1)} %collective-permute-done.2.refs_3_.refs_7_.refs_1_, ...), custom_call_target="tpu_custom_call" | custom-call | flops 1 | bytes 1 | tf_op jit(solution)/shard_map/row_stats/pallas_call | solution.py:232
  40.6 1.7 %collective-permute-start.12 = (f32[1,16,256]{2,1,0:T(8,128)S(1)}, f32[1,16,256]{2,1,0:T(8,128)S(1)}, u32[]{:S(2)}, u32[]{:S(2)}) collective-permute-start(f32[1,16,256]{2,1,0:T(8,128)S(1)} %row_stats.3.refs_3_.refs_10_), channel_id=1, source_target_pairs={{2,0},{5,1},{0,2},{7,3},{6,4},{1,5},{4,6},{3,7},{10,8},{13,9},{8,1... | collective-permute-start | bytes 49160 | tf_op jit(solution)/shard_map/ppermute | solution.py:704
  42.3 9.0 %gradients.2 = (f32[4,256,128]{2,1,0:T(8,128)S(1)}, f32[4,2,256,128]{3,2,1,0:T(8,128)S(1)}, bf16[3072,128]{1,0:T(8,128)(2,1)S(1)}, bf16[1024,128]{1,0:T(8,128)(2...) custom-call(s32[64]{0:T(128)S(1)} %get-tuple-element.64.refs_4_.refs_0_, ...), custom_call_target="tpu_custom_call" | custom-call | flops 16000000000 | bytes 1 | tf_op jit(solution)/shard_map/gradients/pallas_call | solution.py:390
  51.3 2.0 %collective-permute-start.16 = (bf16[2048,128]{1,0:T(8,128)(2,1)S(1)}, bf16[2048,128]{1,0:T(8,128)(2,1)S(1)}, u32[]{:S(2)}, u32[]{:S(2)}) collective-permute-start(bf16[2048,128]{1,0:T(8,128)(2,1)S(1)} %get-tuple-element.72), channel_id=1, source_target_pairs={{0,4},{1,3},{2,6},{3,1},{4,0},{5,7},{6,2},{7,5},{8,12},{9,11},{10,... | collective-permute-start | bytes 1572872 | tf_op jit(solution)/shard_map/ppermute | solution.py:736
  53.3 1.2 %collective-permute-start.17 = (bf16[2048,128]{1,0:T(8,128)(2,1)S(1)}, bf16[2048,128]{1,0:T(8,128)(2,1)S(1)}, u32[]{:S(2)}, u32[]{:S(2)}) collective-permute-start(bf16[2048,128]{1,0:T(8,128)(2,1)S(1)} %get-tuple-element.73), channel_id=1, source_target_pairs={{0,5},{1,2},{2,7},{3,0},{4,1},{5,6},{6,3},{7,4},{8,13},{9,10},{10,... | collective-permute-start | bytes 1572872 | tf_op jit(solution)/shard_map/ppermute | solution.py:736
  54.5 0.8 sink_terms.1.refs_15_
  55.3 1.6 %collective-permute-start.13 = (f32[4,128]{1,0:T(4,128)S(1)}, f32[4,128]{1,0:T(4,128)S(1)}, u32[]{:S(2)}, u32[]{:S(2)}) collective-permute-start(f32[4,128]{1,0:T(4,128)S(1)} %sink_terms.1.refs_15_), channel_id=1, source_target_pairs={{0,8},{8,16},{16,24},{24,0},{1,9},{9,17},{17,25},{25,1},{2,10},{10... | collective-permute-start | bytes 6152 | tf_op jit(solution)/shard_map/ppermute | solution.py:644
  56.9 2.6 %collective-permute-start.14 = (f32[4,128]{1,0:T(4,128)S(1)}, f32[4,128]{1,0:T(4,128)S(1)}, u32[]{:S(2)}, u32[]{:S(2)}) collective-permute-start(f32[4,128]{1,0:T(4,128)S(1)} %sink_terms.1.refs_15_), channel_id=1, source_target_pairs={{0,16},{8,24},{16,0},{24,8},{1,17},{9,25},{17,1},{25,9},{2,18},{10... | collective-permute-start | bytes 6152 | tf_op jit(solution)/shard_map/ppermute | solution.py:644
  59.5 1.4 %collective-permute-start.15 = (f32[4,128]{1,0:T(4,128)S(1)}, f32[4,128]{1,0:T(4,128)S(1)}, u32[]{:S(2)}, u32[]{:S(2)}) collective-permute-start(f32[4,128]{1,0:T(4,128)S(1)} %sink_terms.1.refs_15_), channel_id=1, source_target_pairs={{0,24},{8,0},{16,8},{24,16},{1,25},{9,1},{17,9},{25,17},{2,26},{10... | collective-permute-start | bytes 6152 | tf_op jit(solution)/shard_map/ppermute | solution.py:644
  60.9 3.1 %gradients.3 = (f32[1,256,128]{2,1,0:T(8,128)S(1)}, f32[1,2,256,128]{3,2,1,0:T(8,128)S(1)}, bf16[3856,128]{1,0:T(8,128)(2,1)S(1)}, bf16[1280,128]{1,0:T(8,128)(2...) custom-call(s32[22]{0:T(128)S(1)} %get-tuple-element.65.refs_5_.refs_0_, ...), custom_call_target="tpu_custom_call" | custom-call | flops 4000000000 | bytes 1 | tf_op jit(solution)/shard_map/gradients/pallas_call | solution.py:390
  64.0 1.8 %collective-permute-done.17.refs_4_.refs_7_ = bf16[2048,128]{1,0:T(8,128)(2,1)S(1)} collective-permute-done((bf16[2048,128]{1,0:T(8,128)(2,1)S(1)}, bf16[2048,128]{1,0:T(8,128)(2,1)S(1)}, u32[]{:S(2)}, u32[]{:S(2)}) %collective-permute-start.17) | collective-permute-done | bytes 524320 | tf_op jit(solution)/shard_map/ppermute | solution.py:736
  66.1 1.4 %collective-permute-start.19 = (bf16[1280,128]{1,0:T(8,128)(2,1)S(1)}, bf16[1280,128]{1,0:T(8,128)(2,1)S(1)}, u32[]{:S(2)}, u32[]{:S(2)}) collective-permute-start(bf16[1280,128]{1,0:T(8,128)(2,1)S(1)} %get-tuple-element.76), channel_id=1, source_target_pairs={{0,2},{1,5},{2,0},{3,7},{4,6},{5,1},{6,4},{7,3},{8,10},{9,13},{10,... | collective-permute-start | bytes 983048 | tf_op jit(solution)/shard_map/ppermute | solution.py:741
  67.5 1.5 %collective-permute-start.20 = (bf16[1280,128]{1,0:T(8,128)(2,1)S(1)}, bf16[1280,128]{1,0:T(8,128)(2,1)S(1)}, u32[]{:S(2)}, u32[]{:S(2)}) collective-permute-start(bf16[1280,128]{1,0:T(8,128)(2,1)S(1)} %get-tuple-element.77), channel_id=1, source_target_pairs={{0,3},{1,4},{2,1},{3,6},{4,7},{5,0},{6,5},{7,2},{8,11},{9,12},{10,... | collective-permute-start | bytes 983048 | tf_op jit(solution)/shard_map/ppermute | solution.py:741
  69.6 4.8 %collective-permute-done.19.refs_2_ = bf16[1280,128]{1,0:T(8,128)(2,1)S(1)} collective-permute-done((bf16[1280,128]{1,0:T(8,128)(2,1)S(1)}, bf16[1280,128]{1,0:T(8,128)(2,1)S(1)}, u32[]{:S(2)}, u32[]{:S(2)}) %collective-permute-start.19) | collective-permute-done | bytes 327712 | tf_op jit(solution)/shard_map/ppermute | solution.py:741
  74.4 4.6 %collective-permute-done.20.refs_3_ = bf16[1280,128]{1,0:T(8,128)(2,1)S(1)} collective-permute-done((bf16[1280,128]{1,0:T(8,128)(2,1)S(1)}, bf16[1280,128]{1,0:T(8,128)(2,1)S(1)}, u32[]{:S(2)}, u32[]{:S(2)}) %collective-permute-start.20) | collective-permute-done | bytes 327712 | tf_op jit(solution)/shard_map/ppermute | solution.py:741
  79.0 1.8 %closing_sums.1 = (bf16[1,256,1280]{2,1,0:T(8,128)(2,1)}, bf16[1,256,1280]{2,1,0:T(8,128)(2,1)}, bf16[1,256,1280]{2,1,0:T(8,128)(2,1)}, f32[1,10]{1,0:T(1,128)}) custom-call(f32[8,128]{1,0:T(8,128)S(1)} %get-tuple-element.74.refs_0_, bf16[3856,128]{1,0:T(8,128)(2,1)S(1)} %collective-permute-done.18.refs_1_, ...), custom_call_target="tpu_custom_call" | custom-call | flops 1 | bytes 1 | tf_op jit(solution)/shard_map/closing_sums/pallas_call | solution.py:462
  (44 shorter events, 2.2 us)
Async XLA Ops:
  0.6 8.3 %copy-start.5 = (s32[10,1,6]{0,1,2:T(1,128)S(1)}, s32[10,1,6]{0,1,2:T(1,128)}, u32[]{:S(2)}) copy-start(s32[10,1,6]{0,1,2:T(1,128)} %param.10) | copy-start | bytes 724
  4.3 23.6 %collective-permute-start.2 = (bf16[5,4,256,128]{3,2,1,0:T(8,128)(2,1)}, bf16[5,4,256,128]{3,2,1,0:T(8,128)(2,1)S(1)}, u32[]{:S(2)}, u32[]{:S(2)}) collective-permute-start(bf16[5,4,256,128]{3,2,1,0:T(8,128)(2,1)} %get-tuple-element.52), channel_id=1, source_target_pairs={{1,0},{0,1},{3,2},{2,3},{5,4},{4,5},{7,6},{6,7},{9,8},{8,9},{11,10... | collective-permute-start | bytes 3932168 | tf_op jit(solution)/shard_map/ppermute | solution.py:681
  4.8 25.8 %collective-permute-start.3 = (bf16[4,2,256,128]{3,2,1,0:T(8,128)(2,1)}, bf16[4,2,256,128]{3,2,1,0:T(8,128)(2,1)S(1)}, u32[]{:S(2)}, u32[]{:S(2)}) collective-permute-start(bf16[4,2,256,128]{3,2,1,0:T(8,128)(2,1)} %get-tuple-element.46.refs_4_), channel_id=1, source_target_pairs={{2,0},{5,1},{0,2},{7,3},{6,4},{1,5},{4,6},{3,7},{10,8},{13,9},{8,1... | collective-permute-start | bytes 1572872 | tf_op jit(solution)/shard_map/ppermute | solution.py:691
  7.4 23.3 %collective-permute-start.5 = (bf16[4,2,256,128]{3,2,1,0:T(8,128)(2,1)}, bf16[4,2,256,128]{3,2,1,0:T(8,128)(2,1)S(1)}, u32[]{:S(2)}, u32[]{:S(2)}) collective-permute-start(bf16[4,2,256,128]{3,2,1,0:T(8,128)(2,1)} %get-tuple-element.47.refs_5_), channel_id=1, source_target_pairs={{4,0},{3,1},{6,2},{1,3},{0,4},{7,5},{2,6},{5,7},{12,8},{11,9},{14,... | collective-permute-start | bytes 1572872 | tf_op jit(solution)/shard_map/ppermute | solution.py:693
  8.9 22.3 %collective-permute-start.4 = (bf16[4,2,256,128]{3,2,1,0:T(8,128)(2,1)}, bf16[4,2,256,128]{3,2,1,0:T(8,128)(2,1)S(1)}, u32[]{:S(2)}, u32[]{:S(2)}) collective-permute-start(bf16[4,2,256,128]{3,2,1,0:T(8,128)(2,1)} %get-tuple-element.53), channel_id=1, source_target_pairs={{3,0},{4,1},{1,2},{6,3},{7,4},{0,5},{5,6},{2,7},{11,8},{12,9},{9,1... | collective-permute-start | bytes 1572872 | tf_op jit(solution)/shard_map/ppermute | solution.py:691
  9.0 1.5 %collective-permute-start = (s32[10,1,6]{2,1,0:T(1,128)S(1)}, s32[10,1,6]{2,1,0:T(1,128)S(1)}, u32[]{:S(2)}, u32[]{:S(2)}) collective-permute-start(s32[10,1,6]{2,1,0:T(1,128)S(1)} %copy.19.refs_0_), channel_id=1, source_target_pairs={{1,0},{0,1},{3,2},{2,3},{5,4},{4,5},{7,6},{6,7},{9,8},{8,9},{11,10... | collective-permute-start | bytes 728 | tf_op jit(solution)/shard_map/ppermute | solution.py:667
  10.5 9.0 %collective-permute-start.1 = (s32[10,2,6]{2,1,0:T(2,128)S(1)}, s32[10,2,6]{2,1,0:T(2,128)S(1)}, u32[]{:S(2)}, u32[]{:S(2)}) collective-permute-start(s32[10,2,6]{2,1,0:T(2,128)S(1)} %pad_add_fusion), channel_id=1, source_target_pairs={{2,0},{5,1},{0,2},{7,3},{6,4},{1,5},{4,6},{3,7},{10,8},{13,9},{8,1... | collective-permute-start | bytes 1448 | tf_op jit(solution)/shard_map/ppermute | solution.py:671
  19.5 12.8 %collective-permute-start.6 = (bf16[4,2,256,128]{3,2,1,0:T(8,128)(2,1)}, bf16[4,2,256,128]{3,2,1,0:T(8,128)(2,1)S(1)}, u32[]{:S(2)}, u32[]{:S(2)}) collective-permute-start(bf16[4,2,256,128]{3,2,1,0:T(8,128)(2,1)} %get-tuple-element.55), channel_id=1, source_target_pairs={{5,0},{2,1},{7,2},{0,3},{1,4},{6,5},{3,6},{4,7},{13,8},{10,9},{15,... | collective-permute-start | bytes 1572872 | tf_op jit(solution)/shard_map/ppermute | solution.py:693
  21.2 1.0 %copy-start = (bf16[4,2,256,128]{3,2,1,0:T(8,128)(2,1)S(1)}, bf16[4,2,256,128]{3,2,1,0:T(8,128)(2,1)}, u32[]{:S(2)}) copy-start(bf16[4,2,256,128]{3,2,1,0:T(8,128)(2,1)} %get-tuple-element.47.refs_5_) | copy-start | bytes 1572868
  22.3 1.0 %copy-start.1 = (bf16[4,2,256,128]{3,2,1,0:T(8,128)(2,1)S(1)}, bf16[4,2,256,128]{3,2,1,0:T(8,128)(2,1)}, u32[]{:S(2)}) copy-start(bf16[4,2,256,128]{3,2,1,0:T(8,128)(2,1)} %get-tuple-element.46.refs_4_) | copy-start | bytes 1572868
  23.3 0.9 %copy-start.2 = (bf16[1,2,256,128]{3,2,1,0:T(8,128)(2,1)S(1)}, bf16[1,2,256,128]{3,2,1,0:T(8,128)(2,1)}, u32[]{:S(2)}) copy-start(bf16[1,2,256,128]{3,2,1,0:T(8,128)(2,1)} %get-tuple-element.49.refs_7_.refs_1_) | copy-start | bytes 393220
  24.2 3.7 %copy-start.3 = (bf16[1,2,256,128]{3,2,1,0:T(8,128)(2,1)S(1)}, bf16[1,2,256,128]{3,2,1,0:T(8,128)(2,1)}, u32[]{:S(2)}) copy-start(bf16[1,2,256,128]{3,2,1,0:T(8,128)(2,1)} %get-tuple-element.63.refs_0_) | copy-start | bytes 393220
  24.2 6.4 %copy-start.4 = (bf16[1,2,256,128]{3,2,1,0:T(8,128)(2,1)S(1)}, bf16[1,2,256,128]{3,2,1,0:T(8,128)(2,1)}, u32[]{:S(2)}) copy-start(bf16[1,2,256,128]{3,2,1,0:T(8,128)(2,1)} %get-tuple-element.58.refs_2_) | copy-start | bytes 393220
  27.9 4.3 %copy-start.6 = (f32[10]{0:T(128)S(1)}, f32[10]{0:T(128)}, u32[]{:S(2)}) copy-start(f32[10]{0:T(128)} %param.11) | copy-start | bytes 124
  28.0 10.5 %collective-permute-start.11 = (bf16[1,2,256,128]{3,2,1,0:T(8,128)(2,1)S(1)}, bf16[1,2,256,128]{3,2,1,0:T(8,128)(2,1)S(1)}, u32[]{:S(2)}, u32[]{:S(2)}) collective-permute-start(bf16[1,2,256,128]{3,2,1,0:T(8,128)(2,1)S(1)} %gate.3), channel_id=1, source_target_pairs={{5,0},{2,1},{7,2},{0,3},{1,4},{6,5},{3,6},{4,7},{13,8},{10,9},{15,... | collective-permute-start | bytes 393224 | tf_op jit(solution)/shard_map/ppermute | solution.py:693
  30.6 7.8 %collective-permute-start.10 = (bf16[1,2,256,128]{3,2,1,0:T(8,128)(2,1)S(1)}, bf16[1,2,256,128]{3,2,1,0:T(8,128)(2,1)S(1)}, u32[]{:S(2)}, u32[]{:S(2)}) collective-permute-start(bf16[1,2,256,128]{3,2,1,0:T(8,128)(2,1)S(1)} %get-tuple-element.62), channel_id=1, source_target_pairs={{4,0},{3,1},{6,2},{1,3},{0,4},{7,5},{2,6},{5,7},{12,8},{11,9},{14,... | collective-permute-start | bytes 393224 | tf_op jit(solution)/shard_map/ppermute | solution.py:693
  30.7 7.8 %collective-permute-start.8 = (bf16[1,2,256,128]{3,2,1,0:T(8,128)(2,1)}, bf16[1,2,256,128]{3,2,1,0:T(8,128)(2,1)S(1)}, u32[]{:S(2)}, u32[]{:S(2)}) collective-permute-start(bf16[1,2,256,128]{3,2,1,0:T(8,128)(2,1)} %get-tuple-element.59), channel_id=1, source_target_pairs={{2,0},{5,1},{0,2},{7,3},{6,4},{1,5},{4,6},{3,7},{10,8},{13,9},{8,1... | collective-permute-start | bytes 393224 | tf_op jit(solution)/shard_map/ppermute | solution.py:691
  31.2 7.3 %collective-permute-start.9 = (bf16[1,2,256,128]{3,2,1,0:T(8,128)(2,1)S(1)}, bf16[1,2,256,128]{3,2,1,0:T(8,128)(2,1)S(1)}, u32[]{:S(2)}, u32[]{:S(2)}) collective-permute-start(bf16[1,2,256,128]{3,2,1,0:T(8,128)(2,1)S(1)} %get-tuple-element.60), channel_id=1, source_target_pairs={{3,0},{4,1},{1,2},{6,3},{7,4},{0,5},{5,6},{2,7},{11,8},{12,9},{9,1... | collective-permute-start | bytes 393224 | tf_op jit(solution)/shard_map/ppermute | solution.py:691
  38.0 4.3 %collective-permute-start.7 = (f32[4,16,256]{2,1,0:T(8,128)S(1)}, f32[4,16,256]{2,1,0:T(8,128)S(1)}, u32[]{:S(2)}, u32[]{:S(2)}) collective-permute-start(f32[4,16,256]{2,1,0:T(8,128)S(1)} %row_stats.2.refs_1_.refs_10_), channel_id=1, source_target_pairs={{2,0},{5,1},{0,2},{7,3},{6,4},{1,5},{4,6},{3,7},{10,8},{13,9},{8,1... | collective-permute-start | bytes 196616 | tf_op jit(solution)/shard_map/ppermute | solution.py:704
  40.6 14.0 %collective-permute-start.12 = (f32[1,16,256]{2,1,0:T(8,128)S(1)}, f32[1,16,256]{2,1,0:T(8,128)S(1)}, u32[]{:S(2)}, u32[]{:S(2)}) collective-permute-start(f32[1,16,256]{2,1,0:T(8,128)S(1)} %row_stats.3.refs_3_.refs_10_), channel_id=1, source_target_pairs={{2,0},{5,1},{0,2},{7,3},{6,4},{1,5},{4,6},{3,7},{10,8},{13,9},{8,1... | collective-permute-start | bytes 49160 | tf_op jit(solution)/shard_map/ppermute | solution.py:704
  51.3 12.7 %collective-permute-start.16 = (bf16[2048,128]{1,0:T(8,128)(2,1)S(1)}, bf16[2048,128]{1,0:T(8,128)(2,1)S(1)}, u32[]{:S(2)}, u32[]{:S(2)}) collective-permute-start(bf16[2048,128]{1,0:T(8,128)(2,1)S(1)} %get-tuple-element.72), channel_id=1, source_target_pairs={{0,4},{1,3},{2,6},{3,1},{4,0},{5,7},{6,2},{7,5},{8,12},{9,11},{10,... | collective-permute-start | bytes 1572872 | tf_op jit(solution)/shard_map/ppermute | solution.py:736
  53.3 12.5 %collective-permute-start.17 = (bf16[2048,128]{1,0:T(8,128)(2,1)S(1)}, bf16[2048,128]{1,0:T(8,128)(2,1)S(1)}, u32[]{:S(2)}, u32[]{:S(2)}) collective-permute-start(bf16[2048,128]{1,0:T(8,128)(2,1)S(1)} %get-tuple-element.73), channel_id=1, source_target_pairs={{0,5},{1,2},{2,7},{3,0},{4,1},{5,6},{6,3},{7,4},{8,13},{9,10},{10,... | collective-permute-start | bytes 1572872 | tf_op jit(solution)/shard_map/ppermute | solution.py:736
  55.3 8.7 %collective-permute-start.13 = (f32[4,128]{1,0:T(4,128)S(1)}, f32[4,128]{1,0:T(4,128)S(1)}, u32[]{:S(2)}, u32[]{:S(2)}) collective-permute-start(f32[4,128]{1,0:T(4,128)S(1)} %sink_terms.1.refs_15_), channel_id=1, source_target_pairs={{0,8},{8,16},{16,24},{24,0},{1,9},{9,17},{17,25},{25,1},{2,10},{10... | collective-permute-start | bytes 6152 | tf_op jit(solution)/shard_map/ppermute | solution.py:644
  56.9 7.1 %collective-permute-start.14 = (f32[4,128]{1,0:T(4,128)S(1)}, f32[4,128]{1,0:T(4,128)S(1)}, u32[]{:S(2)}, u32[]{:S(2)}) collective-permute-start(f32[4,128]{1,0:T(4,128)S(1)} %sink_terms.1.refs_15_), channel_id=1, source_target_pairs={{0,16},{8,24},{16,0},{24,8},{1,17},{9,25},{17,1},{25,9},{2,18},{10... | collective-permute-start | bytes 6152 | tf_op jit(solution)/shard_map/ppermute | solution.py:644
  59.5 4.5 %collective-permute-start.15 = (f32[4,128]{1,0:T(4,128)S(1)}, f32[4,128]{1,0:T(4,128)S(1)}, u32[]{:S(2)}, u32[]{:S(2)}) collective-permute-start(f32[4,128]{1,0:T(4,128)S(1)} %sink_terms.1.refs_15_), channel_id=1, source_target_pairs={{0,24},{8,0},{16,8},{24,16},{1,25},{9,1},{17,9},{25,17},{2,26},{10... | collective-permute-start | bytes 6152 | tf_op jit(solution)/shard_map/ppermute | solution.py:644
  65.9 13.1 %collective-permute-start.18 = (bf16[3856,128]{1,0:T(8,128)(2,1)S(1)}, bf16[3856,128]{1,0:T(8,128)(2,1)S(1)}, u32[]{:S(2)}, u32[]{:S(2)}) collective-permute-start(bf16[3856,128]{1,0:T(8,128)(2,1)S(1)} %get-tuple-element.75), channel_id=1, source_target_pairs={{1,0},{0,1},{3,2},{2,3},{5,4},{4,5},{7,6},{6,7},{9,8},{8,9},{11,10... | collective-permute-start | bytes 2961416 | tf_op jit(solution)/shard_map/ppermute | solution.py:744
  66.1 8.3 %collective-permute-start.19 = (bf16[1280,128]{1,0:T(8,128)(2,1)S(1)}, bf16[1280,128]{1,0:T(8,128)(2,1)S(1)}, u32[]{:S(2)}, u32[]{:S(2)}) collective-permute-start(bf16[1280,128]{1,0:T(8,128)(2,1)S(1)} %get-tuple-element.76), channel_id=1, source_target_pairs={{0,2},{1,5},{2,0},{3,7},{4,6},{5,1},{6,4},{7,3},{8,10},{9,13},{10,... | collective-permute-start | bytes 983048 | tf_op jit(solution)/shard_map/ppermute | solution.py:741
  67.5 11.5 %collective-permute-start.20 = (bf16[1280,128]{1,0:T(8,128)(2,1)S(1)}, bf16[1280,128]{1,0:T(8,128)(2,1)S(1)}, u32[]{:S(2)}, u32[]{:S(2)}) collective-permute-start(bf16[1280,128]{1,0:T(8,128)(2,1)S(1)} %get-tuple-element.77), channel_id=1, source_target_pairs={{0,3},{1,4},{2,1},{3,6},{4,7},{5,0},{6,5},{7,2},{8,11},{9,12},{10,... | collective-permute-start | bytes 983048 | tf_op jit(solution)/shard_map/ppermute | solution.py:741
  68.9 10.0 %collective-permute-start.21 = (bf16[528,128]{1,0:T(8,128)(2,1)S(1)}, bf16[528,128]{1,0:T(8,128)(2,1)S(1)}, u32[]{:S(2)}, u32[]{:S(2)}) collective-permute-start(bf16[528,128]{1,0:T(8,128)(2,1)S(1)} %get-tuple-element.82), channel_id=1, source_target_pairs={{0,4},{1,3},{2,6},{3,1},{4,0},{5,7},{6,2},{7,5},{8,12},{9,11},{10,... | collective-permute-start | bytes 405512 | tf_op jit(solution)/shard_map/ppermute | solution.py:736
  69.3 9.7 %collective-permute-start.22 = (bf16[528,128]{1,0:T(8,128)(2,1)S(1)}, bf16[528,128]{1,0:T(8,128)(2,1)S(1)}, u32[]{:S(2)}, u32[]{:S(2)}) collective-permute-start(bf16[528,128]{1,0:T(8,128)(2,1)S(1)} %get-tuple-element.83), channel_id=1, source_target_pairs={{0,5},{1,2},{2,7},{3,0},{4,1},{5,6},{6,3},{7,4},{8,13},{9,10},{10,... | collective-permute-start | bytes 405512 | tf_op jit(solution)/shard_map/ppermute | solution.py:736
